TPU v7x, 32 devices: a whole 2x2x4 slice. The times are simulated.
32 devices in a mesh: expert: 8 (over z, x), hidden: 4 (over y, core).
Axes of the slice: x: 2, y: 2, z: 4, core: 2. Of those that a mesh axis runs over, the one named last changes fastest.
Arguments:
- images: bfloat16 [224, 144, 512], P(('expert', 'hidden')), may hold values from -6 to 6
- lengths: int32 [224], P(('expert', 'hidden')), may hold values from 49 to 144, as said below
- priority: int32 [32, 1008], P(('expert', 'hidden')), may hold values from 0 to 1007, each once within a row
- top_experts: int32 [224, 144, 2], P(('expert', 'hidden')), may hold values from 0 to 7, all different within a row
- out_grad: bfloat16 [224, 144, 512], P(('expert', 'hidden')), may hold values from -6 to 6
- first_gain: float32 [512], replicated, may hold values from 0.5 to 1.5
- first_shift: float32 [512], replicated, may hold values from -1 to 1
- w_query: bfloat16 [512, 512], replicated, may hold values from -0.375 to 0.375
- w_key: bfloat16 [512, 512], replicated, may hold values from -0.25 to 0.25
- w_value: bfloat16 [512, 512], replicated, may hold values from -0.25 to 0.25
- w_output: bfloat16 [512, 512], replicated, may hold values from -0.75 to 0.75
- second_gain: float32 [512], replicated, may hold values from 0.5 to 1.5
- second_shift: float32 [512], replicated, may hold values from -0.5 to 0.5
- w_router: bfloat16 [512, 8], replicated, may hold values from -0.1875 to 0.1875
- w_expert_in: bfloat16 [8, 512, 2048], P('expert', None, 'hidden'), may hold values from -0.25 to 0.25
- w_expert_out: bfloat16 [8, 2048, 512], P('expert', 'hidden'), may hold values from -2 to 2
Outputs:
- block_out: bfloat16 [224, 144, 512], P(('expert', 'hidden'))
- grad_images: float32 [224, 144, 512], P(('expert', 'hidden'))
- grad_first_gain: float32 [512], replicated
- grad_first_shift: float32 [512], replicated
- grad_w_query: float32 [512, 512], replicated
- grad_w_key: float32 [512, 512], replicated
- grad_w_value: float32 [512, 512], replicated
- grad_w_output: float32 [512, 512], replicated
- grad_second_gain: float32 [512], replicated
- grad_second_shift: float32 [512], replicated
- grad_w_router: float32 [512, 8], replicated
- grad_w_expert_in: float32 [8, 512, 2048], P('expert', None, 'hidden')
- grad_w_expert_out: float32 [8, 2048, 512], P('expert', 'hidden')
Inputs may be any that keep to these rules, and one draw needn't show every extreme that they name: `lengths`: each image has either 49 or 144 valid patches, the first ones; the rest are padding. `priority`: each row is an ordering of the 1008 token slots of one routing group. `top_experts`: the two experts of a token differ; choices of padding tokens are ignored.
All inputs are finite; a program needn't handle non-finite values.
Results may differ from a plain program's by a relative error of at most 0.015.
Values may be sent and summed in bfloat16 or wider, within the bound.
No kernel may reach another device: no remote copies, remote signals or barrier semaphores. Data moves between devices by JAX's collectives and lax.ppermute only.
A program may use at most 192 MiB of HBM per device.

v0:
```python
from functools import partial

import jax
import jax.numpy as jnp
from jax import lax
from jax.sharding import PartitionSpec as P

HEADS = 8
TOPK = 2


EPSILON = 1e-06
NEGATIVE = -1e30


def layer_norm(values, scaling, offset):
    average = jnp.mean(values, axis=-1, keepdims=True)
    centred = values - average
    variance = jnp.mean(centred * centred, axis=-1, keepdims=True)
    return centred * lax.rsqrt(variance + EPSILON) * scaling + offset


def exact_gelu(values):
    return jax.nn.gelu(values, approximate=False)


def gate_lookup(logits, selected):
    return jnp.take_along_axis(jax.nn.softmax(logits, axis=-1), selected, axis=1)


def slot_targets(selected, present, ranking, expert_count, capacity):
    rows_count, top_count = selected.shape
    ranked = selected[ranking]
    ranked_present = present[ranking]
    flattened = ranked.T.reshape(-1)
    active = jnp.tile(ranked_present, top_count)
    labels = jnp.arange(expert_count, dtype=jnp.int32)
    onehot = ((flattened[:, None] == labels[None, :]) & active[:, None]).astype(jnp.int32)
    earlier = jnp.cumsum(onehot, axis=0, dtype=jnp.int32) - onehot
    position = jnp.sum(earlier * onehot, axis=1, dtype=jnp.int32)
    retained = active & (position < capacity)
    target = jnp.where(retained, flattened * capacity + position, expert_count * capacity)
    target = target.reshape(top_count, rows_count).T
    inverse = (
        jnp.zeros((rows_count,), jnp.int32).at[ranking].set(jnp.arange(rows_count, dtype=jnp.int32))
    )
    return target[inverse]


def fill_slots(row_list, target, slot_count):
    buffer = jnp.zeros((slot_count + 1, row_list[0].shape[1]), jnp.bfloat16)
    for column in range(len(row_list)):
        buffer = buffer.at[target[:, column]].set(row_list[column])
    return buffer[:slot_count]


def pick_rows(buffer, target):
    padded = jnp.concatenate([buffer, jnp.zeros((1, buffer.shape[1]), buffer.dtype)])
    return [padded[target[:, column]] for column in range(target.shape[1])]


def on_device(
    images,
    lengths,
    priority,
    top_experts,
    out_grad,
    first_gain,
    first_shift,
    w_query,
    w_key,
    w_value,
    w_output,
    second_gain,
    second_shift,
    w_router,
    w_expert_in,
    w_expert_out,
):
    image_count, patch_count, model_width = images.shape
    tok_rows = image_count * patch_count
    head_size = model_width // HEADS
    scaling = head_size ** (-0.5)
    expert_count = lax.axis_size("expert") * w_expert_in.shape[0]
    capacity = (21 * tok_rows * TOPK + 20 * expert_count - 1) // (20 * expert_count)
    slot_count = expert_count * capacity
    split_shape = (image_count, patch_count, HEADS, head_size)
    present = jnp.arange(patch_count, dtype=jnp.int32)[None, :] < lengths[:, None]
    selected = top_experts.reshape(tok_rows, TOPK)
    target = slot_targets(selected, present.reshape(tok_rows), priority[0], expert_count, capacity)
    tokens = images.astype(jnp.float32).reshape(tok_rows, model_width)
    normed_full, norm_one_back = jax.vjp(layer_norm, tokens, first_gain, first_shift)
    normed_low = normed_full.astype(jnp.bfloat16)

    def project(matrix):
        return (
            jnp.dot(normed_low, matrix, preferred_element_type=jnp.float32)
            .astype(jnp.bfloat16)
            .reshape(split_shape)
        )

    queries = project(w_query)
    key_rows = project(w_key)
    values = project(w_value)
    key_mask = present[:, None, None, :]

    def score_block():
        raw_scores = (
            jnp.einsum("iphd,iqhd->ihpq", queries, key_rows, preferred_element_type=jnp.float32)
            * scaling
        )
        return jnp.where(key_mask, raw_scores, NEGATIVE)

    scores = score_block()
    row_max = jnp.max(scores, axis=-1, keepdims=True)
    exponent = jnp.exp(scores - row_max)
    denominator = jnp.sum(exponent, axis=-1, keepdims=True)
    attn_probs = exponent / denominator
    log_total = row_max + jnp.log(denominator)
    probs_low = attn_probs.astype(jnp.bfloat16)
    mixed_heads = jnp.einsum(
        "ihpq,iqhd->iphd", probs_low, values, preferred_element_type=jnp.float32
    )
    mixed_heads = mixed_heads.astype(jnp.bfloat16).reshape(tok_rows, model_width)
    residual = tokens + jnp.dot(mixed_heads, w_output, preferred_element_type=jnp.float32)
    normed_two, norm_two_back = jax.vjp(layer_norm, residual, second_gain, second_shift)
    routed_low = normed_two.astype(jnp.bfloat16)
    logits = jnp.dot(routed_low, w_router, preferred_element_type=jnp.float32)
    gate_values, gate_back = jax.vjp(partial(gate_lookup, selected=selected), logits)
    send_rows = fill_slots([routed_low] * TOPK, target, slot_count).reshape(
        expert_count, capacity, model_width
    )
    received = lax.all_to_all(send_rows, "expert", split_axis=0, concat_axis=0, tiled=True)
    rows_in = received.reshape(-1, model_width)
    weight_in = w_expert_in[0]
    weight_out = w_expert_out[0]
    gathered = lax.all_gather(rows_in, "hidden", axis=0, tiled=True)
    row_block = gathered
    pre_block = jnp.dot(row_block, weight_in, preferred_element_type=jnp.float32)
    act_block = exact_gelu(pre_block).astype(jnp.bfloat16)
    expert_sum = lax.psum_scatter(
        jnp.dot(act_block, weight_out, preferred_element_type=jnp.float32),
        "hidden",
        scatter_dimension=0,
        tiled=True,
    )
    expert_res = expert_sum.astype(jnp.bfloat16).reshape(received.shape)
    returned = lax.all_to_all(
        expert_res, "expert", split_axis=0, concat_axis=0, tiled=True
    ).reshape(slot_count, model_width)
    picked = pick_rows(returned, target)
    out_full = residual
    for column in range(TOPK):
        out_full = out_full + gate_values[:, column : column + 1] * picked[column].astype(
            jnp.float32
        )
    block_out = out_full.astype(jnp.bfloat16).reshape(images.shape)
    cotangent = out_grad.astype(jnp.float32).reshape(tok_rows, model_width)
    grad_gate = jnp.stack(
        [jnp.sum(cotangent * picked[column].astype(jnp.float32), axis=1) for column in range(TOPK)],
        axis=1,
    )
    grad_list = [
        (gate_values[:, column : column + 1] * cotangent).astype(jnp.bfloat16)
        for column in range(TOPK)
    ]
    grad_slots = fill_slots(grad_list, target, slot_count).reshape(
        expert_count, capacity, model_width
    )
    grad_in = lax.all_to_all(grad_slots, "expert", split_axis=0, concat_axis=0, tiled=True).reshape(
        -1, model_width
    )
    grad_gathered = lax.all_gather(grad_in, "hidden", axis=0, tiled=True)
    block_count = lax.axis_size("expert") * lax.axis_size("hidden") // 16
    input_blocks = gathered.reshape(block_count, -1, model_width)
    grad_blocks = grad_gathered.reshape(block_count, -1, model_width)

    def expert_step(totals, block_pair):
        acc_in, acc_out = totals
        row_block, grad_block = block_pair
        pre_block = jnp.dot(row_block, weight_in, preferred_element_type=jnp.float32)
        act_block, block_back = jax.vjp(exact_gelu, pre_block)
        grad_act = jnp.einsum(
            "rd,fd->rf", grad_block, weight_out, preferred_element_type=jnp.float32
        )
        grad_block_pre = block_back(grad_act)[0].astype(jnp.bfloat16)
        acc_in = acc_in + jnp.einsum(
            "rd,rf->df", row_block, grad_block_pre, preferred_element_type=jnp.float32
        )
        acc_out = acc_out + jnp.einsum(
            "rf,rd->fd",
            act_block.astype(jnp.bfloat16),
            grad_block,
            preferred_element_type=jnp.float32,
        )
        return ((acc_in, acc_out), grad_block_pre)

    start_totals = (
        jnp.zeros(weight_in.shape, jnp.float32),
        jnp.zeros(weight_out.shape, jnp.float32),
    )
    (grad_first, grad_second), grad_pre_blocks = lax.scan(
        expert_step, start_totals, (input_blocks, grad_blocks)
    )
    grad_pre_all = grad_pre_blocks.reshape(-1, weight_in.shape[1])
    row_block = grad_pre_all
    slot_grad = lax.psum_scatter(
        jnp.einsum("rf,df->rd", row_block, weight_in, preferred_element_type=jnp.float32),
        "hidden",
        scatter_dimension=0,
        tiled=True,
    )
    back_slots = slot_grad.astype(jnp.bfloat16).reshape(received.shape)
    returned_grad = lax.all_to_all(
        back_slots, "expert", split_axis=0, concat_axis=0, tiled=True
    ).reshape(slot_count, model_width)
    grad_routed = jnp.zeros((tok_rows, model_width), jnp.float32)
    for picked_grad in pick_rows(returned_grad, target):
        grad_routed = grad_routed + picked_grad.astype(jnp.float32)
    grad_logits = gate_back(grad_gate)[0].astype(jnp.bfloat16)
    grad_router = jnp.einsum(
        "td,te->de", routed_low, grad_logits, preferred_element_type=jnp.float32
    )
    grad_routed = grad_routed + jnp.einsum(
        "te,de->td", grad_logits, w_router, preferred_element_type=jnp.float32
    )
    grad_residual, grad_second_gain, grad_second_shift = norm_two_back(grad_routed)
    grad_residual = grad_residual + cotangent
    grad_attn = grad_residual.astype(jnp.bfloat16)
    grad_output = jnp.einsum(
        "td,te->de", mixed_heads, grad_attn, preferred_element_type=jnp.float32
    )
    grad_mixed = jnp.einsum("te,de->td", grad_attn, w_output, preferred_element_type=jnp.float32)
    grad_mixed = grad_mixed.astype(jnp.bfloat16).reshape(split_shape)
    again_probs = jnp.exp(score_block() - log_total)
    grad_probs = jnp.einsum(
        "iphd,iqhd->ihpq", grad_mixed, values, preferred_element_type=jnp.float32
    )
    inner_sum = jnp.sum(grad_probs * again_probs, axis=-1, keepdims=True)
    grad_scores = (again_probs * (grad_probs - inner_sum)).astype(jnp.bfloat16)
    grad_values = jnp.einsum(
        "ihpq,iphd->iqhd",
        again_probs.astype(jnp.bfloat16),
        grad_mixed,
        preferred_element_type=jnp.float32,
    )
    grad_values = grad_values.astype(jnp.bfloat16).reshape(tok_rows, model_width)
    grad_queries = (
        jnp.einsum("ihpq,iqhd->iphd", grad_scores, key_rows, preferred_element_type=jnp.float32)
        * scaling
    )
    grad_queries = grad_queries.astype(jnp.bfloat16).reshape(tok_rows, model_width)
    grad_keys = (
        jnp.einsum("ihpq,iphd->iqhd", grad_scores, queries, preferred_element_type=jnp.float32)
        * scaling
    )
    grad_keys = grad_keys.astype(jnp.bfloat16).reshape(tok_rows, model_width)
    grad_query_w = jnp.einsum(
        "td,te->de", normed_low, grad_queries, preferred_element_type=jnp.float32
    )
    grad_key_w = jnp.einsum("td,te->de", normed_low, grad_keys, preferred_element_type=jnp.float32)
    grad_value_w = jnp.einsum(
        "td,te->de", normed_low, grad_values, preferred_element_type=jnp.float32
    )
    grad_normed = jnp.einsum("te,de->td", grad_queries, w_query, preferred_element_type=jnp.float32)
    grad_normed = grad_normed + jnp.einsum(
        "te,de->td", grad_keys, w_key, preferred_element_type=jnp.float32
    )
    grad_normed = grad_normed + jnp.einsum(
        "te,de->td", grad_values, w_value, preferred_element_type=jnp.float32
    )
    grad_tokens, grad_first_gain, grad_first_shift = norm_one_back(grad_normed)
    grad_images = (grad_residual + grad_tokens).reshape(images.shape)
    shared = lax.psum(
        (
            grad_query_w,
            grad_key_w,
            grad_value_w,
            grad_output,
            grad_router,
            grad_first_gain,
            grad_first_shift,
            grad_second_gain,
            grad_second_shift,
        ),
        ("expert", "hidden"),
    )
    return (
        block_out,
        grad_images,
        shared[5],
        shared[6],
        shared[0],
        shared[1],
        shared[2],
        shared[3],
        shared[7],
        shared[8],
        shared[4],
        grad_first[None],
        grad_second[None],
    )


def solution(mesh):
    return jax.shard_map(
        on_device,
        mesh=mesh,
        in_specs=(
            P(("expert", "hidden"), None, None),
            P(("expert", "hidden")),
            P(("expert", "hidden"), None),
            P(("expert", "hidden"), None, None),
            P(("expert", "hidden"), None, None),
            P(),
            P(),
            P(),
            P(),
            P(),
            P(),
            P(),
            P(),
            P(),
            P("expert", None, "hidden"),
            P("expert", "hidden", None),
        ),
        out_specs=(
            P(("expert", "hidden"), None, None),
            P(("expert", "hidden"), None, None),
            P(),
            P(),
            P(),
            P(),
            P(),
            P(),
            P(),
            P(),
            P(),
            P("expert", None, "hidden"),
            P("expert", "hidden", None),
        ),
        check_vma=False,
    )
```

profile of v0, /device:TPU:0, one launch (start us, length us, event | category | flops | bytes accessed | tf_op | source)
XLA Modules:
  0.0 1199.4 jit_solution(1025704041095804688)
XLA Ops:
  15.0 5.5 scatter_custom_fusion
  20.6 6.8 gather_fusion
  57.5 4.3 copy.97
  63.8 4.3 copy.95
  68.1 4.0 fusion.50
  89.0 7.9 scatter_custom_fusion.1
  96.9 9.5 scatter_custom_fusion.2
  113.2 58.8 %all_to_all.20 = bf16[8,265,512]{2,1,0:T(8,128)(2,1)} all-to-all(bf16[8,265,512]{2,1,0:T(8,128)(2,1)} %reshape.384), channel_id=1, replica_groups=mesh['expert'=8,'hidden'=4] {'expert'}, dimensions={0} | all-to-all | bytes 4341760 | tf_op jit(solution)/shard_map/all_to_all | solution.py:133
  175.7 58.7 %all-gather.3.cloned.1.call-done = bf16[8480,512]{1,0:T(8,128)(2,1)} async-done(((bf16[2120,512]{1,0:T(8,128)(2,1)}), bf16[8480,512]{1,0:T(8,128)(2,1)}) %all-gather.3.cloned.1.call-update) | async-done | bytes 8683536 | tf_op jit(solution)/shard_map/all_gather | solution.py:137
  234.4 48.5 %fusion.42 = f32[8480,512]{1,0:T(8,128)} fusion(bf16[1,512,512]{2,1,0:T(8,128)(2,1)} %param.33, bf16[8480,512]{1,0:T(8,128)(2,1)} %all-gather.3.cloned.1.call-done, bf16[1,512,512]{2,1,0:T(8,128)(2,1)S(1)} %copy-done.26), kind=kOutput, calls=%fused_computation.71 | convolution fusion | flops 9174138880 | bytes 27099136 | tf_op jit(solution)/shard_map/dot_general | solution.py:142
  283.1 129.7 %reduce-scatter.3.cloned.1.call-done = f32[2120,512]{1,0:T(8,128)} async-done(((f32[8480,512]{1,0:T(8,128)}), f32[2120,512]{1,0:T(8,128)}) %reduce-scatter.3.cloned.1.call-update) | async-done | bytes 4341776 | tf_op jit(solution)/shard_map/reduce_scatter | solution.py:141
  420.4 5.5 all-to-all-start.1
  429.2 47.9 %all-to-all-done.1 = bf16[8,265,512]{2,1,0:T(8,128)(2,1)} async-done(((bf16[8,265,512]{2,1,0:T(8,128)(2,1)}), bf16[8,265,512]{2,1,0:T(8,128)(2,1)}, u32[]{:S(2)}, u32[]{:S(2)}) %all-to-all-start.1) | async-done | bytes 2170912 | tf_op jit(solution)/shard_map/all_to_all | solution.py:148
  482.6 5.1 gather_fusion.4
  487.7 5.1 gather_fusion.3
  496.0 11.3 scatter_custom_fusion.5
  508.1 12.5 %gather_fusion.7 = f32[2016]{0:T(1024)S(1)} fusion(f32[1008,8]{0,1:T(8,128)S(1)} %get-tuple-element.134, s32[2016]{0:T(1024)S(1)} %reshape.465), kind=kCustom, calls=%fused_computation.7 | custom fusion | bytes 32256 | tf_op jit(solution)/shard_map/jvp(jit(take_along_axis))/gather | solution.py:28
  523.5 6.7 scatter_custom_fusion.3
  530.2 7.4 scatter_fusion
  541.4 55.1 %all_to_all.21 = bf16[8,265,512]{2,1,0:T(8,128)(2,1)} all-to-all(bf16[8,265,512]{2,1,0:T(8,128)(2,1)S(1)} %reshape.391), channel_id=1, replica_groups=mesh['expert'=8,'hidden'=4] {'expert'}, dimensions={0} | all-to-all | bytes 4341760 | tf_op jit(solution)/shard_map/all_to_all | solution.py:170
  600.5 57.6 %all-gather.5.cloned.1.call-done = bf16[8480,512]{1,0:T(8,128)(2,1)} async-done(((bf16[2120,512]{1,0:T(8,128)(2,1)}), bf16[8480,512]{1,0:T(8,128)(2,1)}) %all-gather.5.cloned.1.call-update) | async-done | bytes 8683536 | tf_op jit(solution)/shard_map/all_gather | solution.py:173
  658.1 90.0 %while.15 = (s32[]{:T(128)}, f32[512,512]{1,0:T(8,128)}, f32[512,512]{1,0:T(8,128)S(1)}, bf16[2,4240,512]{2,1,0:T(8,128)(2,1)}, bf16[2,4240,512]{2,1,0:T(8,128)(...) while((s32[]{:T(128)}, f32[512,512]{1,0:T(8,128)}, ...), condition=%wide.region_18.19_spmd.clone, body=%wide.region_17.18_spmd.clone.sunk | while | flops 9064472576 | bytes 98223320 | solution.py:202
  658.1 21.9 %fusion.200 = (f32[4240,512]{1,0:T(8,128)S(1)}, f32[4240,512]{1,0:T(8,128)}) fusion(bf16[512,512]{1,0:T(8,128)(2,1)S(1)} %get-tuple-element.233, bf16[2,4240,512]{2,1,0:T(8,128)(2,1)} %get-tuple-element.232, s32[]{:T(128)S(6)} %copy.140), kind=kOutput, calls=%fused_computation.15.clone.1 | convolution fusion | flops 2357575680 | bytes 22233092 | tf_op jit(solution)/shard_map/while/body/eval_jaxpr/dot_general | solution.py:181
  680.0 7.7 fusion.202
  687.7 9.6 bitcast_dynamic-update-slice_fusion.2
  697.3 4.8 fusion.201
  703.1 21.9 %fusion.200 = (f32[4240,512]{1,0:T(8,128)S(1)}, f32[4240,512]{1,0:T(8,128)}) fusion(bf16[512,512]{1,0:T(8,128)(2,1)S(1)} %get-tuple-element.233, bf16[2,4240,512]{2,1,0:T(8,128)(2,1)} %get-tuple-element.232, s32[]{:T(128)S(6)} %copy.140), kind=kOutput, calls=%fused_computation.15.clone.1 | convolution fusion | flops 2357575680 | bytes 22233092 | tf_op jit(solution)/shard_map/while/body/eval_jaxpr/dot_general | solution.py:181
  725.0 7.7 fusion.202
  732.7 9.6 bitcast_dynamic-update-slice_fusion.2
  742.3 4.8 fusion.201
  748.1 12.4 %fusion.81 = f32[8480,512]{1,0:T(8,128)} fusion(bf16[8480,512]{1,0:T(8,128)(2,1)} %bitcast.190, bf16[1,512,512]{2,1,0:T(8,128)(2,1)S(1)} %bitcast.200), kind=kOutput, calls=%fused_computation.184 | convolution fusion | flops 4445962240 | bytes 26574848 | tf_op jit(solution)/shard_map/rf,df->rd/dot_general | solution.py:208
  760.6 129.7 %reduce-scatter.5.cloned.1.call-done = f32[2120,512]{1,0:T(8,128)} async-done(((f32[8480,512]{1,0:T(8,128)}), f32[2120,512]{1,0:T(8,128)}) %reduce-scatter.5.cloned.1.call-update) | async-done | bytes 4341776 | tf_op jit(solution)/shard_map/reduce_scatter | solution.py:207
  897.8 5.6 all-to-all-start.3
  905.3 49.3 %all-to-all-done.3 = bf16[8,265,512]{2,1,0:T(8,128)(2,1)} async-done(((bf16[8,265,512]{2,1,0:T(8,128)(2,1)}), bf16[8,265,512]{2,1,0:T(8,128)(2,1)}, u32[]{:S(2)}, u32[]{:S(2)}) %all-to-all-start.3) | async-done | bytes 2170912 | tf_op jit(solution)/shard_map/all_to_all | solution.py:214
  960.0 5.1 gather_fusion.6
  965.1 5.1 gather_fusion.5
  973.7 3.9 fusion.124
  983.9 4.3 copy.112
  988.1 7.3 convert_bitcast_fusion
  995.5 5.9 multiply_reduce_fusion
  1009.8 4.2 copy.122
  1014.0 4.1 reshape.400
  1018.2 4.2 copy.116
  1022.4 4.0 reshape.398
  1026.4 4.2 copy.119
  1052.7 38.4 %all-reduce.3 = (f32[512]{0:T(512)}, f32[512]{0:T(512)}, f32[512]{0:T(512)}, f32[512]{0:T(512)}, f32[512,8]{0,1:T(8,128)}) all-reduce(f32[512]{0:T(512)S(1)} %get-tuple-element.89, f32[512]{0:T(512)S(1)} %get-tuple-element.92, f32[512]{0:T(512)S(1)} %get-tuple-element.87, ...), channel_id=1, replica_groups=mesh['expert'=8,'hidden'=4] {'expert','hidden'}, use_global_device_ids=true, to_apply=%region_30.31 | all-reduce | flops 6144 | bytes 49152 | tf_op jit(solution)/shard_map/psum | solution.py:274
  1091.1 3.9 add_add_fusion.2
  1095.0 88.7 %all-reduce.7.cloned.1.call-done = (f32[512,512]{1,0:T(8,128)}, f32[512,512]{1,0:T(8,128)}, f32[512,512]{1,0:T(8,128)}, f32[512,512]{1,0:T(8,128)}) async-done(((f32[512,512]{1,0:T(8,128)}, f32[512,512]{1,0:T(8,128)}, f32[512,512]{1,0:T(8,128)}, f32[512,512]{1,0:T(8,128)}), (f32[512,512]{1,0:T(8,128)}, f32[512,512]{1,0:T(8,128)}, f32[512,512]{1,0:T(8,128)}, ...) | async-done | bytes 4194320 | tf_op jit(solution)/shard_map/psum | solution.py:274
  (317 shorter events, 163.1 us)
Async XLA Ops:
  7.2 43.6 %copy-start = (bf16[512,512]{1,0:T(8,128)(2,1)S(1)}, bf16[512,512]{1,0:T(8,128)(2,1)}, u32[]{:S(2)}) copy-start(bf16[512,512]{1,0:T(8,128)(2,1)} %param.27) | copy-start | bytes 1572868
  7.2 227.2 %all-gather.3.cloned.1.call-start = ((), (), s32[]{:S(2)}) async-start(), calls=%async_computation.6 | async-start | bytes 10854400 | tf_op jit(solution)/shard_map/all_gather | solution.py:137
  9.4 30.0 %copy-start.46 = (f32[1008]{0:T(1024)}, f32[1008]{0:T(1024)S(1)}, u32[]{:S(2)}) copy-start(f32[1008]{0:T(1024)S(1)} %div.69) | copy-start | bytes 12100
  11.2 28.2 %copy-start.4 = (bf16[7,144,512]{2,1,0:T(8,128)(2,1)S(1)}, bf16[7,144,512]{2,1,0:T(8,128)(2,1)}, u32[]{:S(2)}) copy-start(bf16[7,144,512]{2,1,0:T(8,128)(2,1)} %param.18) | copy-start | bytes 3096580
  11.2 28.2 %copy-start.72 = (f32[512]{0:T(512)S(1)}, f32[512]{0:T(512)}, u32[]{:S(2)}) copy-start(f32[512]{0:T(512)} %param.23) | copy-start | bytes 6148
  11.2 28.2 %copy-start.78 = (f32[512]{0:T(512)S(1)}, f32[512]{0:T(512)}, u32[]{:S(2)}) copy-start(f32[512]{0:T(512)} %param.24) | copy-start | bytes 6148
  12.0 62.8 %copy-start.44 = (pred[7,144]{1,0:T(8,128)(4,1)}, pred[7,144]{1,0:T(8,128)(4,1)S(1)}, u32[]{:S(2)}) copy-start(pred[7,144]{1,0:T(8,128)(4,1)S(1)} %iota_compare_fusion.2) | copy-start | bytes 3028
  12.8 27.1 %copy-start.64 = (f32[1008]{0:T(1024)}, f32[1008]{0:T(1024)S(1)}, u32[]{:S(2)}) copy-start(f32[1008]{0:T(1024)S(1)} %add.174) | copy-start | bytes 12100
  12.9 27.1 %copy-start.48 = (f32[1008]{0:T(1024)}, f32[1008]{0:T(1024)S(1)}, u32[]{:S(2)}) copy-start(f32[1008]{0:T(1024)S(1)} %rsqrt.23) | copy-start | bytes 12100
  13.8 26.1 %copy-start.7 = (s32[7,144,2]{2,1,0:T(8,128)}, s32[7,144,2]{2,1,0:T(8,128)S(1)}, u32[]{:S(2)}) copy-start(s32[7,144,2]{2,1,0:T(8,128)S(1)} %copy.100) | copy-start | bytes 24196
  39.5 49.5 %copy-start.76 = (s32[1008]{0:T(1024)}, s32[1008]{0:T(1024)S(1)}, u32[]{:S(2)}) copy-start(s32[1008]{0:T(1024)S(1)} %get-tuple-element.96) | copy-start | bytes 12100
  39.5 57.4 %copy-start.66 = (s32[1008]{0:T(1024)}, s32[1008]{0:T(1024)S(1)}, u32[]{:S(2)}) copy-start(s32[1008]{0:T(1024)S(1)} %get-tuple-element.95) | copy-start | bytes 12100
  48.1 20.0 %copy-start.10 = (bf16[7,144,8,64]{1,3,2,0:T(8,128)(2,1)}, bf16[7,144,8,64]{1,3,2,0:T(8,128)(2,1)S(1)}, u32[]{:S(2)}) copy-start(bf16[7,144,8,64]{1,3,2,0:T(8,128)(2,1)S(1)} %copy.96) | copy-start | bytes 3096580
  88.5 24.7 %copy-start.2 = (f32[1008,512]{1,0:T(8,128)}, f32[1008,512]{1,0:T(8,128)S(1)}, u32[]{:S(2)}) copy-start(f32[1008,512]{1,0:T(8,128)S(1)} %get-tuple-element.142) | copy-start | bytes 6193156
  88.5 17.9 %copy-start.35 = (f32[1008]{0:T(1024)}, f32[1008]{0:T(1024)S(1)}, u32[]{:S(2)}) copy-start(f32[1008]{0:T(1024)S(1)} %broadcast_multiply_fusion.1) | copy-start | bytes 12100
  89.0 17.5 %copy-start.62 = (f32[1008]{0:T(1024)}, f32[1008]{0:T(1024)S(1)}, u32[]{:S(2)}) copy-start(f32[1008]{0:T(1024)S(1)} %multiply_reduce_fusion.5) | copy-start | bytes 12100
  89.0 17.4 %copy-start.39 = (f32[1008]{0:T(1024)}, f32[1008]{0:T(1024)S(1)}, u32[]{:S(2)}) copy-start(f32[1008]{0:T(1024)S(1)} %fusion.77) | copy-start | bytes 12100
  109.5 124.9 %copy-start.26 = (bf16[1,512,512]{2,1,0:T(8,128)(2,1)S(1)}, bf16[1,512,512]{2,1,0:T(8,128)(2,1)}, u32[]{:S(2)}) copy-start(bf16[1,512,512]{2,1,0:T(8,128)(2,1)} %param.32) | copy-start | bytes 1572868
  175.6 237.2 %reduce-scatter.3.cloned.1.call-start = ((), (), s32[]{:S(2)}) async-start(), calls=%async_computation.7 | async-start | bytes 21708800 | tf_op jit(solution)/shard_map/reduce_scatter | solution.py:141
  283.0 143.0 %copy-start.50 = (s32[7,144,2]{1,2,0:T(2,128)S(1)}, s32[7,144,2]{1,2,0:T(2,128)}, u32[]{:S(2)}) copy-start(s32[7,144,2]{1,2,0:T(2,128)} %param.21) | copy-start | bytes 24196
  283.0 143.1 %copy-start.80 = (s32[2]{0:T(128)S(1)}, s32[2]{0:T(128)}, u32[]{:S(2)}) copy-start(s32[2]{0:T(128)} %constant.208) | copy-start | bytes 28
  283.0 143.2 %copy-start.81 = (s32[2]{0:T(128)S(1)}, s32[2]{0:T(128)}, u32[]{:S(2)}) copy-start(s32[2]{0:T(128)} %constant.211) | copy-start | bytes 28
  283.0 144.3 %copy-start.67 = (s32[1008]{0:T(1024)S(1)}, s32[1008]{0:T(1024)}, u32[]{:S(2)}) copy-start(s32[1008]{0:T(1024)} %copy-done.66) | copy-start | bytes 12100
  283.0 144.3 %copy-start.77 = (s32[1008]{0:T(1024)S(1)}, s32[1008]{0:T(1024)}, u32[]{:S(2)}) copy-start(s32[1008]{0:T(1024)} %copy-done.76) | copy-start | bytes 12100
  283.0 144.3 %copy-start.3 = (f32[1008,512]{1,0:T(8,128)S(1)}, f32[1008,512]{1,0:T(8,128)}, u32[]{:S(2)}) copy-start(f32[1008,512]{1,0:T(8,128)} %copy-done.2) | copy-start | bytes 6193156
  283.0 144.3 %copy-start.36 = (f32[1008]{0:T(1024)S(1)}, f32[1008]{0:T(1024)}, u32[]{:S(2)}) copy-start(f32[1008]{0:T(1024)} %copy-done.35) | copy-start | bytes 12100
  283.1 144.3 %copy-start.40 = (f32[1008]{0:T(1024)S(1)}, f32[1008]{0:T(1024)}, u32[]{:S(2)}) copy-start(f32[1008]{0:T(1024)} %copy-done.39) | copy-start | bytes 12100
  283.1 144.3 %copy-start.52 = (f32[512]{0:T(512)S(1)}, f32[512]{0:T(512)}, u32[]{:S(2)}) copy-start(f32[512]{0:T(512)} %param.29) | copy-start | bytes 6148
  283.1 144.3 %copy-start.75 = (f32[512]{0:T(512)S(1)}, f32[512]{0:T(512)}, u32[]{:S(2)}) copy-start(f32[512]{0:T(512)} %param.30) | copy-start | bytes 6148
  420.4 56.7 %all-to-all-start.1 = ((bf16[8,265,512]{2,1,0:T(8,128)(2,1)}), bf16[8,265,512]{2,1,0:T(8,128)(2,1)}, u32[]{:S(2)}, u32[]{:S(2)}) async-start(bf16[8,265,512]{2,1,0:T(8,128)(2,1)} %reshape.386), calls=%async_computation.2 | async-start | bytes 4456448 | tf_op jit(solution)/shard_map/all_to_all | solution.py:148
  425.9 232.1 %all-gather.5.cloned.1.call-start = ((), (), s32[]{:S(2)}) async-start(), calls=%async_computation.8 | async-start | bytes 10854400 | tf_op jit(solution)/shard_map/all_gather | solution.py:173
  427.4 60.3 %copy-start.60 = (s32[1024]{0:T(1024)}, s32[1024]{0:T(1024)S(1)}, u32[]{:S(2)}) copy-start(s32[1024]{0:T(1024)S(1)} %get-tuple-element.149) | copy-start | bytes 12292
  427.4 60.3 %copy-start.58 = (s32[1024]{0:T(1024)}, s32[1024]{0:T(1024)S(1)}, u32[]{:S(2)}) copy-start(s32[1024]{0:T(1024)S(1)} %get-tuple-element.150) | copy-start | bytes 12292
  539.1 119.0 %copy-start.27 = (bf16[1,512,512]{2,1,0:T(8,128)(2,1)S(1)}, bf16[1,512,512]{2,1,0:T(8,128)(2,1)}, u32[]{:S(2)}) copy-start(bf16[1,512,512]{2,1,0:T(8,128)(2,1)} %param.32) | copy-start | bytes 1572868
  600.2 290.2 %reduce-scatter.5.cloned.1.call-start = ((), (), s32[]{:S(2)}) async-start(), calls=%async_computation.9 | async-start | bytes 21708800 | tf_op jit(solution)/shard_map/reduce_scatter | solution.py:207
  760.5 143.0 %copy-start.32 = (f32[7,8,144]{2,1,0:T(8,128)S(1)}, f32[7,8,144]{2,1,0:T(8,128)}, u32[]{:S(2)}) copy-start(f32[7,8,144]{2,1,0:T(8,128)} %copy-done.31) | copy-start | bytes 96772
  760.5 143.0 %copy-start.34 = (f32[7,8,144]{2,1,0:T(8,128)S(1)}, f32[7,8,144]{2,1,0:T(8,128)}, u32[]{:S(2)}) copy-start(f32[7,8,144]{2,1,0:T(8,128)} %copy-done.33) | copy-start | bytes 96772
  760.5 143.0 %copy-start.5 = (bf16[7,144,512]{2,1,0:T(8,128)(2,1)S(1)}, bf16[7,144,512]{2,1,0:T(8,128)(2,1)}, u32[]{:S(2)}) copy-start(bf16[7,144,512]{2,1,0:T(8,128)(2,1)} %param.18) | copy-start | bytes 3096580
  760.6 143.0 %copy-start.43 = (f32[7,144]{1,0:T(8,128)S(1)}, f32[7,144]{1,0:T(8,128)}, u32[]{:S(2)}) copy-start(f32[7,144]{1,0:T(8,128)} %copy-done.42) | copy-start | bytes 12100
  760.6 143.0 %copy-start.71 = (f32[7,144]{1,0:T(8,128)S(1)}, f32[7,144]{1,0:T(8,128)}, u32[]{:S(2)}) copy-start(f32[7,144]{1,0:T(8,128)} %get-tuple-element.135) | copy-start | bytes 12100
  760.6 143.0 %copy-start.73 = (f32[512]{0:T(512)S(1)}, f32[512]{0:T(512)}, u32[]{:S(2)}) copy-start(f32[512]{0:T(512)} %param.23) | copy-start | bytes 6148
  760.6 143.0 %copy-start.79 = (f32[512]{0:T(512)S(1)}, f32[512]{0:T(512)}, u32[]{:S(2)}) copy-start(f32[512]{0:T(512)} %param.24) | copy-start | bytes 6148
  760.6 144.5 %copy-start.17 = (bf16[1008,512]{1,0:T(8,128)(2,1)S(1)}, bf16[1008,512]{1,0:T(8,128)(2,1)}, u32[]{:S(2)}) copy-start(bf16[1008,512]{1,0:T(8,128)(2,1)} %copy-done.16) | copy-start | bytes 3096580
  760.6 144.5 %copy-start.38 = (bf16[1008,8]{0,1:T(8,128)(2,1)S(1)}, bf16[1008,8]{0,1:T(8,128)(2,1)}, u32[]{:S(2)}) copy-start(bf16[1008,8]{0,1:T(8,128)(2,1)} %get-tuple-element.133) | copy-start | bytes 48388
  897.8 62.2 %copy-start.61 = (s32[1024]{0:T(1024)S(1)}, s32[1024]{0:T(1024)}, u32[]{:S(2)}) copy-start(s32[1024]{0:T(1024)} %copy-done.60) | copy-start | bytes 12292
  897.8 56.8 %all-to-all-start.3 = ((bf16[8,265,512]{2,1,0:T(8,128)(2,1)}), bf16[8,265,512]{2,1,0:T(8,128)(2,1)}, u32[]{:S(2)}, u32[]{:S(2)}) async-start(bf16[8,265,512]{2,1,0:T(8,128)(2,1)} %reshape.395), calls=%async_computation.5 | async-start | bytes 4456448 | tf_op jit(solution)/shard_map/all_to_all | solution.py:214
  903.5 280.2 %all-reduce.7.cloned.1.call-start = ((), (), s32[]{:S(2)}) async-start(), calls=%async_computation.10 | async-start | bytes 8388608 | tf_op jit(solution)/shard_map/psum | solution.py:274
  905.3 59.8 %copy-start.59 = (s32[1024]{0:T(1024)S(1)}, s32[1024]{0:T(1024)}, u32[]{:S(2)}) copy-start(s32[1024]{0:T(1024)} %copy-done.58) | copy-start | bytes 12292
  (49 other events, 331.5 us)
Sparse Core Ops, SparseCore 0:
  175.8 58.6 all-gather.2
  283.1 129.6 reduce-scatter.2
  600.3 57.7 all-gather.4
  760.6 129.6 reduce-scatter.4
  1042.3 141.3 all-reduce.6
where the time goes:
time: 1200 us
  waiting for transfers between devices  562 us (47%)
  matrix products  206 us (17%)
  local copies, waits for them, and re-layouts  181 us (15%)
  blocking collectives  152 us (13%)
  other arithmetic  72.1 us (6%)
  between operations  15.5 us (1%)
    reduce_scatter x1, waiting for transfers between devices, on_device(): lax.psum_scatter(jnp.dot(act_block, weight_out, preferred_element_type=jn...  130 us
    reduce_scatter x1, waiting for transfers between devices, on_device(): lax.psum_scatter(jnp.einsum('rf,df->rd', row_block, weight_in, preferred_...  130 us
    psum x1, waiting for transfers between devices, on_device(): lax.psum((grad_query_w, grad_key_w, grad_value_w, grad_output, grad_route...  88.7 us
    all_to_all x1, blocking collectives, on_device(): lax.all_to_all(send_rows, 'expert', split_axis=0, concat_axis=0, tiled=True)  58.8 us
    all_gather x1, waiting for transfers between devices, on_device(): gathered = lax.all_gather(rows_in, 'hidden', axis=0, tiled=True)  58.7 us
    all_gather x1, waiting for transfers between devices, on_device(): grad_gathered = lax.all_gather(grad_in, 'hidden', axis=0, tiled=True)  57.6 us
    all_to_all x1, blocking collectives, on_device(): lax.all_to_all(grad_slots, 'expert', split_axis=0, concat_axis=0, tiled=T...  55.1 us
    all_to_all x1, waiting for transfers between devices, on_device(): lax.all_to_all(back_slots, 'expert', split_axis=0, concat_axis=0, tiled=T...  49.3 us
  transfers between devices with their start and end apart: 7, of which 7 were waited for; matrix products, arithmetic and copies ran while one was open for 2% of the time, Pallas kernels for 0%

commit v1 on v0

v1 whole, which is shorter than its diff:
```python
import jax
import jax.numpy as jnp
from jax import lax
from jax.sharding import PartitionSpec as P

HEADS = 8
TOPK = 2
EPSILON = 1e-06
NEGATIVE = -1e30
BF = jnp.bfloat16
F32 = jnp.float32


def swap(value, axes, size, flip):
    return lax.ppermute(value, axes, [(i, i ^ flip) for i in range(size)])


def bits_of(size):
    count = size.bit_length() - 1
    assert size == 1 << count
    return range(count)


def reduce_scatter(parts, axes, size):
    index = lax.axis_index(axes)
    for bit in bits_of(size):
        pairs = parts.reshape((parts.shape[0] // 2, 2) + parts.shape[1:])
        odd = ((index >> bit) & 1) == 1
        mine = jnp.where(odd, pairs[:, 1], pairs[:, 0])
        other = jnp.where(odd, pairs[:, 0], pairs[:, 1]).astype(BF)
        parts = mine + swap(other, axes, size, 1 << bit).astype(F32)
    return parts[0]


def all_gather(part, axes, size):
    index = lax.axis_index(axes)
    parts = part[None]
    for bit in reversed(bits_of(size)):
        odd = ((index >> bit) & 1) == 1
        came = swap(parts, axes, size, 1 << bit)
        pairs = jnp.where(odd, jnp.stack([came, parts], 1), jnp.stack([parts, came], 1))
        parts = pairs.reshape((-1,) + part.shape)
    return parts


def all_sum(value, axes, size):
    for bit in bits_of(size):
        value = value + swap(value, axes, size, 1 << bit)
    return value


def exchange(blocks, axes, size):
    index = lax.axis_index(axes)
    taken = []
    for flip in range(size):
        block = lax.dynamic_index_in_dim(blocks, index ^ flip, 0, keepdims=False)
        taken.append(block if flip == 0 else swap(block, axes, size, flip))
    return taken


def exchange_back(block_list, axes, size):
    index = lax.axis_index(axes)
    came = jnp.stack(
        [b if s == 0 else swap(b, axes, size, s) for s, b in enumerate(block_list)]
    )
    order = index ^ jnp.arange(size, dtype=jnp.int32)
    return came[order]


def layer_norm(values, scaling, offset):
    average = jnp.mean(values, axis=-1, keepdims=True)
    centred = values - average
    variance = jnp.mean(centred * centred, axis=-1, keepdims=True)
    return centred * lax.rsqrt(variance + EPSILON) * scaling + offset


def exact_gelu(values):
    return jax.nn.gelu(values, approximate=False)


def gate_lookup(logits, selected):
    chosen = selected[:, :, None] == jnp.arange(logits.shape[1], dtype=jnp.int32)
    router = jax.nn.softmax(logits, axis=-1)
    return jnp.sum(jnp.where(chosen, router[:, None, :], 0.0), axis=-1)


def slot_targets(selected, present, ranking, expert_count, capacity, stride):
    rows_count, top_count = selected.shape
    ranked = selected[ranking]
    ranked_present = present[ranking]
    flattened = ranked.T.reshape(-1)
    active = jnp.tile(ranked_present, top_count)
    labels = jnp.arange(expert_count, dtype=jnp.int32)
    onehot = ((flattened[:, None] == labels[None, :]) & active[:, None]).astype(jnp.int32)
    earlier = jnp.cumsum(onehot, axis=0, dtype=jnp.int32) - onehot
    position = jnp.sum(earlier * onehot, axis=1, dtype=jnp.int32)
    retained = active & (position < capacity)
    target = jnp.where(retained, flattened * stride + position, expert_count * stride)
    target = target.reshape(top_count, rows_count).T
    inverse = (
        jnp.zeros((rows_count,), jnp.int32).at[ranking].set(jnp.arange(rows_count, dtype=jnp.int32))
    )
    return target[inverse]


def mm(spec, left, right):
    return jnp.einsum(spec, left, right, preferred_element_type=F32)


def make_on_device(experts, hidden):
    def on_device(
        images,
        lengths,
        priority,
        top_experts,
        out_grad,
        first_gain,
        first_shift,
        w_query,
        w_key,
        w_value,
        w_output,
        second_gain,
        second_shift,
        w_router,
        w_expert_in,
        w_expert_out,
    ):
        world = ("expert", "hidden")
        image_count, patch_count, width = images.shape
        rows = image_count * patch_count
        head_size = width // HEADS
        scaling = head_size ** (-0.5)
        capacity = (21 * rows * TOPK + 20 * experts - 1) // (20 * experts)
        stride = (capacity + 15) // 16 * 16
        slots = experts * stride
        split_shape = (image_count, patch_count, HEADS, head_size)

        units = w_expert_in.shape[2]
        own = jnp.concatenate([w_expert_in[0].reshape(units, width), w_expert_out[0]])
        whole = all_gather(own, "hidden", hidden)
        weight_in = whole[:, :units].reshape(hidden, width, units)
        weight_out = whole[:, units:]

        present = jnp.arange(patch_count, dtype=jnp.int32)[None, :] < lengths[:, None]
        selected = top_experts.reshape(rows, TOPK)
        target = slot_targets(selected, present.reshape(rows), priority[0], experts, capacity, stride)
        slot_at = jnp.arange(slots, dtype=jnp.int32)
        chosen = [target[:, j : j + 1] == slot_at[None, :] for j in range(TOPK)]
        low_chosen = [c.astype(BF) for c in chosen]
        either = low_chosen[0] + low_chosen[1]

        cot_low = out_grad.reshape(rows, width)
        cot_slots = mm("ts,td->sd", either, cot_low).astype(BF).reshape(experts, stride, width)
        cot_in = exchange(cot_slots, "expert", experts)

        tokens = images.astype(F32).reshape(rows, width)
        normed_full, norm_one_back = jax.vjp(layer_norm, tokens, first_gain, first_shift)
        normed_low = normed_full.astype(BF)

        def project(matrix):
            return mm("td,de->te", normed_low, matrix).astype(BF).reshape(split_shape)

        queries = project(w_query)
        key_rows = project(w_key)
        values = project(w_value)
        key_mask = present[:, None, None, :]

        def score_block():
            raw_scores = mm("iphd,iqhd->ihpq", queries, key_rows) * scaling
            return jnp.where(key_mask, raw_scores, NEGATIVE)

        scores = score_block()
        row_max = jnp.max(scores, axis=-1, keepdims=True)
        exponent = jnp.exp(scores - row_max)
        denominator = jnp.sum(exponent, axis=-1, keepdims=True)
        attn_probs = exponent / denominator
        log_total = row_max + jnp.log(denominator)
        probs_low = attn_probs.astype(BF)
        mixed_heads = mm("ihpq,iqhd->iphd", probs_low, values).astype(BF).reshape(rows, width)
        residual = tokens + mm("td,de->te", mixed_heads, w_output)
        normed_two, norm_two_back = jax.vjp(layer_norm, residual, second_gain, second_shift)
        routed_low = normed_two.astype(BF)
        logits = mm("td,de->te", routed_low, w_router)
        gate_values, gate_back = jax.vjp(lambda v: gate_lookup(v, selected), logits)

        send_rows = mm("ts,td->sd", either, routed_low).astype(BF).reshape(experts, stride, width)
        gate_slots = sum(
            jnp.sum(jnp.where(chosen[j], gate_values[:, j : j + 1], 0.0), axis=0)
            for j in range(TOPK)
        ).reshape(experts, stride)
        rows_in = exchange(send_rows, "expert", experts)
        gates_in = exchange(gate_slots, "expert", experts)

        row_block = jnp.concatenate(rows_in)
        cot_block = jnp.concatenate(cot_in)
        gate_block = jnp.concatenate(gates_in)
        grad_block = (gate_block[:, None] * cot_block.astype(F32)).astype(BF)
        pre = mm("rd,hdf->hrf", row_block, weight_in)
        act, gelu_back = jax.vjp(exact_gelu, pre)
        act_low = act.astype(BF)
        expert_res = mm("hrf,hfd->rd", act_low, weight_out).astype(BF)
        grad_act = mm("rd,hfd->hrf", grad_block, weight_out)
        grad_pre = gelu_back(grad_act)[0].astype(BF)
        slot_grad = mm("hrf,hdf->rd", grad_pre, weight_in).astype(BF)
        gate_grad = jnp.sum(cot_block.astype(F32) * expert_res.astype(F32), axis=1)

        def by_sender(array):
            return list(array.reshape((experts, stride) + array.shape[1:]))

        back_grad = exchange_back(by_sender(slot_grad), "expert", experts).reshape(slots, width)
        back_gate = exchange_back(by_sender(gate_grad), "expert", experts).reshape(slots)
        back_res = exchange_back(by_sender(expert_res), "expert", experts).reshape(slots, width)

        grad_in_parts = mm("rd,hrf->hdf", row_block, grad_pre)
        grad_out_parts = mm("hrf,rd->hfd", act_low, grad_block)
        expert_sums = reduce_scatter(
            jnp.concatenate([grad_in_parts.reshape(hidden, units, width), grad_out_parts], axis=1),
            "hidden",
            hidden,
        )

        out_full = residual
        for j in range(TOPK):
            out_full = out_full + gate_values[:, j : j + 1] * mm("ts,sd->td", low_chosen[j], back_res)
        block_out = out_full.astype(BF).reshape(images.shape)

        cotangent = cot_low.astype(F32)
        grad_gate = jnp.stack(
            [jnp.sum(jnp.where(chosen[j], back_gate[None, :], 0.0), axis=1) for j in range(TOPK)],
            axis=1,
        )
        grad_routed = mm("ts,sd->td", either, back_grad)
        grad_logits = gate_back(grad_gate)[0].astype(BF)
        grad_router = mm("td,te->de", routed_low, grad_logits)
        grad_routed = grad_routed + mm("te,de->td", grad_logits, w_router)
        grad_residual, grad_second_gain, grad_second_shift = norm_two_back(grad_routed)
        grad_residual = grad_residual + cotangent
        grad_attn = grad_residual.astype(BF)
        grad_output = mm("td,te->de", mixed_heads, grad_attn)
        grad_mixed = mm("te,de->td", grad_attn, w_output).astype(BF).reshape(split_shape)
        again_probs = jnp.exp(score_block() - log_total)
        grad_probs = mm("iphd,iqhd->ihpq", grad_mixed, values)
        inner_sum = jnp.sum(grad_probs * again_probs, axis=-1, keepdims=True)
        grad_scores = (again_probs * (grad_probs - inner_sum)).astype(BF)
        grad_values = mm("ihpq,iphd->iqhd", again_probs.astype(BF), grad_mixed)
        grad_values = grad_values.astype(BF).reshape(rows, width)
        grad_queries = mm("ihpq,iqhd->iphd", grad_scores, key_rows) * scaling
        grad_queries = grad_queries.astype(BF).reshape(rows, width)
        grad_keys = mm("ihpq,iphd->iqhd", grad_scores, queries) * scaling
        grad_keys = grad_keys.astype(BF).reshape(rows, width)
        grad_query_w = mm("td,te->de", normed_low, grad_queries)
        grad_key_w = mm("td,te->de", normed_low, grad_keys)
        grad_value_w = mm("td,te->de", normed_low, grad_values)
        grad_normed = mm("te,de->td", grad_queries, w_query)
        grad_normed = grad_normed + mm("te,de->td", grad_keys, w_key)
        grad_normed = grad_normed + mm("te,de->td", grad_values, w_value)
        grad_tokens, grad_first_gain, grad_first_shift = norm_one_back(grad_normed)
        grad_images = (grad_residual + grad_tokens).reshape(images.shape)

        devices = experts * hidden

        def all_reduce(matrices):
            stacked = jnp.concatenate(matrices)
            parts = stacked.reshape(devices, -1, width)
            total = reduce_scatter(parts, world, devices).astype(BF)
            total = all_gather(total, world, devices).reshape(stacked.shape)
            return [t.astype(F32) for t in jnp.split(total, len(matrices))]

        (sum_output,) = all_reduce([grad_output])
        sum_query, sum_key, sum_value = all_reduce([grad_query_w, grad_key_w, grad_value_w])
        small_two = jnp.concatenate(
            [grad_router.T, grad_second_gain[None], grad_second_shift[None]]
        )
        small_two = all_sum(small_two, world, devices)
        small_one = all_sum(jnp.stack([grad_first_gain, grad_first_shift]), world, devices)
        return (
            block_out,
            grad_images,
            small_one[0],
            small_one[1],
            sum_query,
            sum_key,
            sum_value,
            sum_output,
            small_two[experts],
            small_two[experts + 1],
            small_two[:experts].T,
            expert_sums[:units].reshape(w_expert_in.shape),
            expert_sums[None, units:],
        )

    return on_device


def solution(mesh):
    both = ("expert", "hidden")
    return jax.shard_map(
        make_on_device(mesh.shape["expert"], mesh.shape["hidden"]),
        mesh=mesh,
        in_specs=(
            P(both, None, None),
            P(both),
            P(both, None),
            P(both, None, None),
            P(both, None, None),
            P(),
            P(),
            P(),
            P(),
            P(),
            P(),
            P(),
            P(),
            P(),
            P("expert", None, "hidden"),
            P("expert", "hidden", None),
        ),
        out_specs=(
            P(both, None, None),
            P(both, None, None),
            P(),
            P(),
            P(),
            P(),
            P(),
            P(),
            P(),
            P(),
            P(),
            P("expert", None, "hidden"),
            P("expert", "hidden", None),
        ),
        check_vma=False,
    )
```

time: 1200 us -> 645 us (0.54)
  waiting for transfers between devices: 562 us -> 128 us
  blocking collectives: 152 us -> 0 us
  starting transfers between devices: 11.5 us -> 137 us
  local copies, waits for them, and re-layouts: 181 us -> 134 us
  matrix products: 206 us -> 167 us
  between operations: 15.5 us -> 2.88 us
    reduce_scatter x2 -> x0, waiting for transfers between devices: 259 us -> none  [the longest x1 130 us: on_device(): lax.psum_scatter(jnp.dot(act_block, weight_out, preferred_element_type=jn...]
    ppermute x0 -> x76, starting transfers between devices: none -> 137 us  [swap(): return lax.ppermute(value, axes, [(i, i ^ flip) for i in range(size)])]
    ppermute x0 -> x76, waiting for transfers between devices: none -> 128 us  [swap(): return lax.ppermute(value, axes, [(i, i ^ flip) for i in range(size)])]
    all_gather x2 -> x0, waiting for transfers between devices: 116 us -> none  [the longest x1 58.7 us: on_device(): gathered = lax.all_gather(rows_in, 'hidden', axis=0, tiled=True)]
    all_to_all x2 -> x0, blocking collectives: 114 us -> none  [the longest x1 58.8 us: on_device(): lax.all_to_all(send_rows, 'expert', split_axis=0, concat_axis=0, tiled=True)]
    all_to_all x2 -> x0, waiting for transfers between devices: 97.2 us -> none  [the longest x1 49.3 us: on_device(): lax.all_to_all(back_slots, 'expert', split_axis=0, concat_axis=0, tiled=T...]
    psum x1 -> x0, waiting for transfers between devices: 88.7 us -> none  [on_device(): lax.psum((grad_query_w, grad_key_w, grad_value_w, grad_output, grad_route...]
    dot_general x31 -> x32, matrix products: 206 us -> 167 us  [mm(): return jnp.einsum(spec, left, right, preferred_element_type=F32)]
  transfers between devices with their start and end apart: 7 -> 76, of which waited for: 7 -> 19; matrix products, arithmetic and copies ran while one was open for 2% -> 32% of each run, Pallas kernels for 0% -> 0%
where the time goes in v1:
time: 645 us; the launch traced here: 633 us
  matrix products  167 us (26%)
  starting transfers between devices  137 us (21%)
  local copies, waits for them, and re-layouts  134 us (21%)
  waiting for transfers between devices  128 us (20%)
  other arithmetic  64.2 us (10%)
    dot_general x32, matrix products, mm(): return jnp.einsum(spec, left, right, preferred_element_type=F32)  167 us
    ppermute x76, starting transfers between devices, swap(): return lax.ppermute(value, axes, [(i, i ^ flip) for i in range(size)])  137 us
    ppermute x76, waiting for transfers between devices, swap(): return lax.ppermute(value, axes, [(i, i ^ flip) for i in range(size)])  128 us
    unnamed x233, local copies, waits for them, and re-layouts  34.6 us
    reshape x6, local copies, waits for them, and re-layouts, project(): return mm('td,de->te', normed_low, matrix).astype(BF).reshape(split_shape)  19.9 us
  transfers between devices with their start and end apart: 76, of which 19 were waited for; matrix products, arithmetic and copies ran while one was open for 32% of the time, Pallas kernels for 0%

profile of v1, /device:TPU:0, one launch (start us, length us, event | category | flops | bytes accessed | tf_op | source)
XLA Modules:
  0.0 633.0 jit_solution(18291784099121946018)
XLA Ops:
  9.9 4.3 copy.223
  21.6 3.5 convolution_convert_fusion.5
  25.1 3.8 reshape.1011
  28.9 4.3 copy.225
  33.3 3.9 fusion.50
  51.7 5.3 scatter_custom_fusion
  57.0 7.0 %gather_fusion = pred[1008]{0:T(1024)(128)(4,1)S(1)} fusion(pred[1008]{0:T(1024)(128)(4,1)S(1)} %lt.100, s32[1024]{0:T(1024)S(1)} %get-tuple-element.102), kind=kCustom, calls=%fused_computation | custom fusion | bytes 6048 | tf_op jit(solution)/shard_map/gather | solution.py:90
  78.4 3.5 convolution_convert_fusion.1
  95.4 4.7 convolution_convert_fusion
  105.2 11.0 %collective-permute-done = bf16[1,1024,512]{2,1,0:T(8,128)(2,1)} collective-permute-done((bf16[1,1024,512]{2,1,0:T(8,128)(2,1)}, bf16[1,1024,512]{2,1,0:T(8,128)(2,1)}, u32[]{:S(2)}, u32[]{:S(2)}) %collective-permute-start) | collective-permute-done | bytes 1048608 | tf_op jit(solution)/shard_map/ppermute | solution.py:15
  116.3 3.9 maximum_select_fusion.1
  125.0 3.6 collective-permute-start.7
  135.3 16.1 %collective-permute-done.6 = bf16[272,512]{1,0:T(8,128)(2,1)S(1)} collective-permute-done((bf16[272,512]{1,0:T(8,128)(2,1)}, bf16[272,512]{1,0:T(8,128)(2,1)S(1)}, u32[]{:S(2)}, u32[]{:S(2)}) %collective-permute-start.6) | collective-permute-done | bytes 278560 | tf_op jit(solution)/shard_map/ppermute | solution.py:15
  152.1 5.8 collective-permute-start.25
  158.6 6.9 %collective-permute-start.26 = (bf16[272,512]{1,0:T(8,128)(2,1)S(1)}, bf16[272,512]{1,0:T(8,128)(2,1)S(1)}, u32[]{:S(2)}, u32[]{:S(2)}) collective-permute-start(bf16[272,512]{1,0:T(8,128)(2,1)S(1)} %copy-done.51), channel_id=1, source_target_pairs={{0,16},{4,20},{8,24},{12,28},{16,0},{20,4},{24,8},{28,12},{1,17},{... | collective-permute-start | bytes 835592 | tf_op jit(solution)/shard_map/ppermute | solution.py:15
  172.3 24.6 %collective-permute-done.26 = bf16[272,512]{1,0:T(8,128)(2,1)S(1)} collective-permute-done((bf16[272,512]{1,0:T(8,128)(2,1)S(1)}, bf16[272,512]{1,0:T(8,128)(2,1)S(1)}, u32[]{:S(2)}, u32[]{:S(2)}) %collective-permute-start.26) | collective-permute-done | bytes 278560 | tf_op jit(solution)/shard_map/ppermute | solution.py:15
  197.0 7.9 %collective-permute-done.27 = bf16[272,512]{1,0:T(8,128)(2,1)S(1)} collective-permute-done((bf16[272,512]{1,0:T(8,128)(2,1)S(1)}, bf16[272,512]{1,0:T(8,128)(2,1)S(1)}, u32[]{:S(2)}, u32[]{:S(2)}) %collective-permute-start.27) | collective-permute-done | bytes 278560 | tf_op jit(solution)/shard_map/ppermute | solution.py:15
  208.2 4.5 maximum_select_fusion
  212.7 6.3 copy.234
  219.1 44.8 %fusion.9 = (bf16[4,2176,512]{1,2,0:T(8,128)(2,1)S(1)}, f32[4,2176,512]{1,2,0:T(8,128)}, f32[4,512,2176]{2,1,0:T(8,128)}) fusion(bf16[2176,512]{1,0:T(8,128)(2,1)} %constant_dynamic-update-slice_fusion, bf16[4,1024,512]{1,2,0:T(8,128)(2,1)} %bitcast.575), kind=kOutput, calls=%fused_computation.24 | convolution fusion | flops 4853071872 | bytes 48889856 | tf_op jit(solution)/shard_map/rd,hdf->hrf/dot_general | solution.py:107
  263.9 5.9 fusion.31
  269.9 11.5 %collective-permute-start.38 = (f32[272]{0:T(512)S(1)}, f32[272]{0:T(512)S(1)}, u32[]{:S(2)}, u32[]{:S(2)}) collective-permute-start(f32[272]{0:T(512)S(1)} %get-tuple-element.79), channel_id=1, source_target_pairs={{0,8},{4,12},{8,0},{12,4},{16,24},{20,28},{24,16},{28,20},{1,9},{5... | collective-permute-start | bytes 3272 | tf_op jit(solution)/shard_map/ppermute | solution.py:15
  305.9 3.7 collective-permute-start.20
  323.0 8.5 %fusion.73 = f32[4,512,512]{2,1,0:T(8,128)S(1)} fusion(bf16[4,2176,512]{1,2,0:T(8,128)(2,1)} %copy-done.96, bf16[2176,512]{1,0:T(8,128)(2,1)} %copy-done.77, f32[2176]{0:T(1024)S(1)} %concatenate.83), kind=kOutput, calls=%fused_computation.136 | convolution fusion | flops 4566745088 | bytes 15344128 | tf_op jit(solution)/shard_map/hrf,rd->hfd/dot_general | solution.py:107
  331.5 19.3 %fusion.6 = bf16[4,2176,512]{1,2,0:T(8,128)(2,1)} fusion(f32[4,2176,512]{1,2,0:T(8,128)} %get-tuple-element.36, f32[4,512,2176]{2,1,0:T(8,128)} %get-tuple-element.92, bf16[4,1024,512]{1,2,0:T(8,128)(2,1)S(1)} %bitcast.577, bf16[2176,512]{1,0:T(8,128)(2,1)} %copy-done.77, f32[2176]{0:T(1024)S(1)} %concatenate.83), kind=kOutput, calls=%fused_computation.16 | convolution fusion | flops 4629135360 | bytes 48902144 | tf_op jit(solution)/shard_map/rd,hfd->hrf/dot_general | solution.py:107
  350.8 11.3 %fusion.56 = f32[4,512,512]{2,1,0:T(8,128)} fusion(bf16[4,2176,512]{1,2,0:T(8,128)(2,1)} %fusion.6, bf16[2176,512]{1,0:T(8,128)(2,1)} %constant_dynamic-update-slice_fusion), kind=kOutput, calls=%fused_computation.97 | convolution fusion | flops 4563402752 | bytes 15335424 | tf_op jit(solution)/shard_map/rd,hrf->hdf/dot_general | solution.py:107
  362.1 9.8 %fusion.29 = bf16[2176,512]{1,0:T(8,128)(2,1)} fusion(bf16[4,2176,512]{1,2,0:T(8,128)(2,1)} %fusion.6, bf16[4,1024,512]{1,2,0:T(8,128)(2,1)S(1)} %bitcast.578), kind=kOutput, calls=%fused_computation.62 | convolution fusion | flops 4564516864 | bytes 13238272 | tf_op jit(solution)/shard_map/hrf,hdf->rd/dot_general | solution.py:107
  389.0 7.9 %collective-permute-start.32 = (bf16[272,512]{1,0:T(8,128)(2,1)}, bf16[272,512]{1,0:T(8,128)(2,1)S(1)}, u32[]{:S(2)}, u32[]{:S(2)}) collective-permute-start(bf16[272,512]{1,0:T(8,128)(2,1)} %get-tuple-element.41), channel_id=1, source_target_pairs={{0,12},{4,8},{8,4},{12,0},{16,28},{20,24},{24,20},{28,16},{1,13},{... | collective-permute-start | bytes 835592 | tf_op jit(solution)/shard_map/ppermute | solution.py:15
  397.0 6.0 collective-permute-start.33
  405.0 4.4 fusion.24
  409.5 3.9 add_convert_fusion.1
  421.4 11.1 %collective-permute-done.33 = bf16[272,512]{1,0:T(8,128)(2,1)} collective-permute-done((bf16[272,512]{1,0:T(8,128)(2,1)}, bf16[272,512]{1,0:T(8,128)(2,1)}, u32[]{:S(2)}, u32[]{:S(2)}) %collective-permute-start.33) | collective-permute-done | bytes 278560 | tf_op jit(solution)/shard_map/ppermute | solution.py:15
  434.2 5.3 collective-permute-done.34
  441.6 3.7 gather_fusion.4
  445.3 5.9 multiply_reduce_fusion.1
  459.2 3.9 copy.240
  463.1 7.7 %multiply_reduce_fusion = (f32[7,8,144]{2,1,0:T(8,128)S(1)}, f32[7,8,144,144]{2,3,1,0:T(8,128)S(1)}) fusion(f32[7,8,144]{2,1,0:T(8,128)S(1)} %copy-done.47, f32[7,8,144,144]{2,3,1,0:T(8,128)} %copy-done.1, pred[7,144]{1,0:T(8,128)(4,1)S(1)} %copy-done.61, bf16[7,144,8,64]{1,3,2,0:T(8,128)(2,1)} %copy.240, bf16[7,144,8,64]{1,3,2,0:T(8,128)(2,1)} %copy.225), kind=kOutput, calls=%fused_computation.50 | convolution fusion | flops 154433664 | bytes 11419632 | tf_op jit(solution)/shard_map/iphd,iqhd->ihpq/dot_general | solution.py:107
  470.8 5.5 multiply_convert_fusion
  485.2 4.2 copy.247
  510.7 4.2 copy.250
  514.9 4.0 reshape.1026
  535.4 10.0 %collective-permute-start.47 = (f32[2,512]{1,0:T(2,128)S(1)}, f32[2,512]{1,0:T(2,128)S(1)}, u32[]{:S(2)}, u32[]{:S(2)}) collective-permute-start(f32[2,512]{1,0:T(2,128)S(1)} %add.267), channel_id=1, source_target_pairs={{0,8},{1,9},{2,10},{3,11},{4,12},{5,13},{6,14},{7,15},{8,0},{9,1},... | collective-permute-start | bytes 12296 | tf_op jit(solution)/shard_map/ppermute | solution.py:15
  551.6 3.5 add_add_fusion.2
  563.8 4.0 collective-permute-done.50
  570.5 3.6 collective-permute-done.51
  586.1 3.5 collective-permute-done.54
  590.8 3.5 collective-permute-done.55
  602.9 24.5 %collective-permute-done.57 = bf16[8,48,512]{2,1,0:T(8,128)(2,1)S(1)} collective-permute-done((bf16[8,48,512]{2,1,0:T(8,128)(2,1)S(1)}, bf16[8,48,512]{2,1,0:T(8,128)(2,1)S(1)}, u32[]{:S(2)}, u32[]{:S(2)}) %collective-permute-start.57) | collective-permute-done | bytes 393248 | tf_op jit(solution)/shard_map/ppermute | solution.py:15
  (540 shorter events, 254.1 us)
Async XLA Ops:
  83.2 38.7 %collective-permute-start.2 = (bf16[272,512]{1,0:T(8,128)(2,1)}, bf16[272,512]{1,0:T(8,128)(2,1)}, u32[]{:S(2)}, u32[]{:S(2)}) collective-permute-start(bf16[272,512]{1,0:T(8,128)(2,1)} %get-tuple-element.64), channel_id=1, source_target_pairs={{0,4},{4,0},{8,12},{12,8},{16,20},{20,16},{24,28},{28,24},{1,5},{5... | collective-permute-start | bytes 835592 | tf_op jit(solution)/shard_map/ppermute | solution.py:15
  86.1 38.8 %collective-permute-start.3 = (bf16[272,512]{1,0:T(8,128)(2,1)}, bf16[272,512]{1,0:T(8,128)(2,1)}, u32[]{:S(2)}, u32[]{:S(2)}) collective-permute-start(bf16[272,512]{1,0:T(8,128)(2,1)} %get-tuple-element.63), channel_id=1, source_target_pairs={{0,8},{4,12},{8,0},{12,4},{16,24},{20,28},{24,16},{28,20},{1,9},{5... | collective-permute-start | bytes 835592 | tf_op jit(solution)/shard_map/ppermute | solution.py:15
  87.7 42.6 %collective-permute-start.4 = (bf16[272,512]{1,0:T(8,128)(2,1)}, bf16[272,512]{1,0:T(8,128)(2,1)}, u32[]{:S(2)}, u32[]{:S(2)}) collective-permute-start(bf16[272,512]{1,0:T(8,128)(2,1)} %get-tuple-element.62), channel_id=1, source_target_pairs={{0,12},{4,8},{8,4},{12,0},{16,28},{20,24},{24,20},{28,16},{1,13},{... | collective-permute-start | bytes 835592 | tf_op jit(solution)/shard_map/ppermute | solution.py:15
  87.7 44.6 %collective-permute-start.5 = (bf16[272,512]{1,0:T(8,128)(2,1)}, bf16[272,512]{1,0:T(8,128)(2,1)}, u32[]{:S(2)}, u32[]{:S(2)}) collective-permute-start(bf16[272,512]{1,0:T(8,128)(2,1)} %get-tuple-element.61), channel_id=1, source_target_pairs={{0,16},{4,20},{8,24},{12,28},{16,0},{20,4},{24,8},{28,12},{1,17},{... | collective-permute-start | bytes 835592 | tf_op jit(solution)/shard_map/ppermute | solution.py:15
  92.2 24.1 %collective-permute-start = (bf16[1,1024,512]{2,1,0:T(8,128)(2,1)}, bf16[1,1024,512]{2,1,0:T(8,128)(2,1)}, u32[]{:S(2)}, u32[]{:S(2)}) collective-permute-start(bf16[1,1024,512]{2,1,0:T(8,128)(2,1)} %get-tuple-element.70), channel_id=1, source_target_pairs={{0,2},{1,3},{2,0},{3,1},{4,6},{5,7},{6,4},{7,5},{8,10},{9,11},{10,... | collective-permute-start | bytes 3145736 | tf_op jit(solution)/shard_map/ppermute | solution.py:15
  120.1 88.1 %collective-permute-start.1 = (bf16[2,1024,512]{2,1,0:T(8,128)(2,1)}, bf16[2,1024,512]{2,1,0:T(8,128)(2,1)}, u32[]{:S(2)}, u32[]{:S(2)}) collective-permute-start(bf16[2,1024,512]{2,1,0:T(8,128)(2,1)} %maximum_select_fusion.1), channel_id=1, source_target_pairs={{0,1},{1,0},{2,3},{3,2},{4,5},{5,4},{6,7},{7,6},{8,9},{9,8},{10,11... | collective-permute-start | bytes 6291464 | tf_op jit(solution)/shard_map/ppermute | solution.py:15
  121.9 29.4 %collective-permute-start.6 = (bf16[272,512]{1,0:T(8,128)(2,1)}, bf16[272,512]{1,0:T(8,128)(2,1)S(1)}, u32[]{:S(2)}, u32[]{:S(2)}) collective-permute-start(bf16[272,512]{1,0:T(8,128)(2,1)} %get-tuple-element.60), channel_id=1, source_target_pairs={{0,20},{4,16},{8,28},{12,24},{16,4},{20,0},{24,12},{28,8},{1,21},{... | collective-permute-start | bytes 835592 | tf_op jit(solution)/shard_map/ppermute | solution.py:15
  125.0 27.2 %collective-permute-start.7 = (bf16[272,512]{1,0:T(8,128)(2,1)}, bf16[272,512]{1,0:T(8,128)(2,1)S(1)}, u32[]{:S(2)}, u32[]{:S(2)}) collective-permute-start(bf16[272,512]{1,0:T(8,128)(2,1)} %get-tuple-element.59), channel_id=1, source_target_pairs={{0,24},{4,28},{8,16},{12,20},{16,8},{20,12},{24,0},{28,4},{1,25},{... | collective-permute-start | bytes 835592 | tf_op jit(solution)/shard_map/ppermute | solution.py:15
  130.2 28.4 %collective-permute-start.8 = (bf16[272,512]{1,0:T(8,128)(2,1)S(1)}, bf16[272,512]{1,0:T(8,128)(2,1)S(1)}, u32[]{:S(2)}, u32[]{:S(2)}) collective-permute-start(bf16[272,512]{1,0:T(8,128)(2,1)S(1)} %copy-done.52), channel_id=1, source_target_pairs={{0,28},{4,24},{8,20},{12,16},{16,12},{20,8},{24,4},{28,0},{1,29},{... | collective-permute-start | bytes 835592 | tf_op jit(solution)/shard_map/ppermute | solution.py:15
  132.3 34.0 %collective-permute-start.23 = (bf16[272,512]{1,0:T(8,128)(2,1)}, bf16[272,512]{1,0:T(8,128)(2,1)S(1)}, u32[]{:S(2)}, u32[]{:S(2)}) collective-permute-start(bf16[272,512]{1,0:T(8,128)(2,1)} %get-tuple-element.50), channel_id=1, source_target_pairs={{0,4},{4,0},{8,12},{12,8},{16,20},{20,16},{24,28},{28,24},{1,5},{5... | collective-permute-start | bytes 835592 | tf_op jit(solution)/shard_map/ppermute | solution.py:15
  151.4 16.9 %collective-permute-start.24 = (bf16[272,512]{1,0:T(8,128)(2,1)S(1)}, bf16[272,512]{1,0:T(8,128)(2,1)S(1)}, u32[]{:S(2)}, u32[]{:S(2)}) collective-permute-start(bf16[272,512]{1,0:T(8,128)(2,1)S(1)} %copy-done.54), channel_id=1, source_target_pairs={{0,8},{4,12},{8,0},{12,4},{16,24},{20,28},{24,16},{28,20},{1,9},{5... | collective-permute-start | bytes 835592 | tf_op jit(solution)/shard_map/ppermute | solution.py:15
  152.1 19.2 %collective-permute-start.25 = (bf16[272,512]{1,0:T(8,128)(2,1)S(1)}, bf16[272,512]{1,0:T(8,128)(2,1)S(1)}, u32[]{:S(2)}, u32[]{:S(2)}) collective-permute-start(bf16[272,512]{1,0:T(8,128)(2,1)S(1)} %copy-done.53), channel_id=1, source_target_pairs={{0,12},{4,8},{8,4},{12,0},{16,28},{20,24},{24,20},{28,16},{1,13},{... | collective-permute-start | bytes 835592 | tf_op jit(solution)/shard_map/ppermute | solution.py:15
  158.6 38.3 %collective-permute-start.26 = (bf16[272,512]{1,0:T(8,128)(2,1)S(1)}, bf16[272,512]{1,0:T(8,128)(2,1)S(1)}, u32[]{:S(2)}, u32[]{:S(2)}) collective-permute-start(bf16[272,512]{1,0:T(8,128)(2,1)S(1)} %copy-done.51), channel_id=1, source_target_pairs={{0,16},{4,20},{8,24},{12,28},{16,0},{20,4},{24,8},{28,12},{1,17},{... | collective-permute-start | bytes 835592 | tf_op jit(solution)/shard_map/ppermute | solution.py:15
  166.3 38.6 %collective-permute-start.27 = (bf16[272,512]{1,0:T(8,128)(2,1)S(1)}, bf16[272,512]{1,0:T(8,128)(2,1)S(1)}, u32[]{:S(2)}, u32[]{:S(2)}) collective-permute-start(bf16[272,512]{1,0:T(8,128)(2,1)S(1)} %copy-done.50), channel_id=1, source_target_pairs={{0,20},{4,16},{8,28},{12,24},{16,4},{20,0},{24,12},{28,8},{1,21},{... | collective-permute-start | bytes 835592 | tf_op jit(solution)/shard_map/ppermute | solution.py:15
  168.3 36.6 %collective-permute-start.28 = (bf16[272,512]{1,0:T(8,128)(2,1)S(1)}, bf16[272,512]{1,0:T(8,128)(2,1)S(1)}, u32[]{:S(2)}, u32[]{:S(2)}) collective-permute-start(bf16[272,512]{1,0:T(8,128)(2,1)S(1)} %copy-done.49), channel_id=1, source_target_pairs={{0,24},{4,28},{8,16},{12,20},{16,8},{20,12},{24,0},{28,4},{1,25},{... | collective-permute-start | bytes 835592 | tf_op jit(solution)/shard_map/ppermute | solution.py:15
  171.3 33.6 %collective-permute-start.29 = (bf16[272,512]{1,0:T(8,128)(2,1)S(1)}, bf16[272,512]{1,0:T(8,128)(2,1)S(1)}, u32[]{:S(2)}, u32[]{:S(2)}) collective-permute-start(bf16[272,512]{1,0:T(8,128)(2,1)S(1)} %copy-done.48), channel_id=1, source_target_pairs={{0,28},{4,24},{8,20},{12,16},{16,12},{20,8},{24,4},{28,0},{1,29},{... | collective-permute-start | bytes 835592 | tf_op jit(solution)/shard_map/ppermute | solution.py:15
  269.8 17.2 %collective-permute-start.37 = (f32[272]{0:T(512)S(1)}, f32[272]{0:T(512)S(1)}, u32[]{:S(2)}, u32[]{:S(2)}) collective-permute-start(f32[272]{0:T(512)S(1)} %get-tuple-element.80), channel_id=1, source_target_pairs={{0,4},{4,0},{8,12},{12,8},{16,20},{20,16},{24,28},{28,24},{1,5},{5... | collective-permute-start | bytes 3272 | tf_op jit(solution)/shard_map/ppermute | solution.py:15
  269.9 19.4 %collective-permute-start.38 = (f32[272]{0:T(512)S(1)}, f32[272]{0:T(512)S(1)}, u32[]{:S(2)}, u32[]{:S(2)}) collective-permute-start(f32[272]{0:T(512)S(1)} %get-tuple-element.79), channel_id=1, source_target_pairs={{0,8},{4,12},{8,0},{12,4},{16,24},{20,28},{24,16},{28,20},{1,9},{5... | collective-permute-start | bytes 3272 | tf_op jit(solution)/shard_map/ppermute | solution.py:15
  281.4 11.1 %collective-permute-start.39 = (f32[272]{0:T(512)S(1)}, f32[272]{0:T(512)S(1)}, u32[]{:S(2)}, u32[]{:S(2)}) collective-permute-start(f32[272]{0:T(512)S(1)} %get-tuple-element.78), channel_id=1, source_target_pairs={{0,12},{4,8},{8,4},{12,0},{16,28},{20,24},{24,20},{28,16},{1,13},{... | collective-permute-start | bytes 3272 | tf_op jit(solution)/shard_map/ppermute | solution.py:15
  282.8 9.7 %collective-permute-start.40 = (f32[272]{0:T(512)S(1)}, f32[272]{0:T(512)S(1)}, u32[]{:S(2)}, u32[]{:S(2)}) collective-permute-start(f32[272]{0:T(512)S(1)} %get-tuple-element.77), channel_id=1, source_target_pairs={{0,16},{4,20},{8,24},{12,28},{16,0},{20,4},{24,8},{28,12},{1,17},{... | collective-permute-start | bytes 3272 | tf_op jit(solution)/shard_map/ppermute | solution.py:15
  302.2 9.3 %collective-permute-start.16 = (f32[272]{0:T(512)S(1)}, f32[272]{0:T(512)S(1)}, u32[]{:S(2)}, u32[]{:S(2)}) collective-permute-start(f32[272]{0:T(512)S(1)} %get-tuple-element.27), channel_id=1, source_target_pairs={{0,4},{4,0},{8,12},{12,8},{16,20},{20,16},{24,28},{28,24},{1,5},{5... | collective-permute-start | bytes 3272 | tf_op jit(solution)/shard_map/ppermute | solution.py:15
  303.7 9.4 %collective-permute-start.17 = (f32[272]{0:T(512)S(1)}, f32[272]{0:T(512)S(1)}, u32[]{:S(2)}, u32[]{:S(2)}) collective-permute-start(f32[272]{0:T(512)S(1)} %get-tuple-element.26), channel_id=1, source_target_pairs={{0,8},{4,12},{8,0},{12,4},{16,24},{20,28},{24,16},{28,20},{1,9},{5... | collective-permute-start | bytes 3272 | tf_op jit(solution)/shard_map/ppermute | solution.py:15
  303.7 11.8 %collective-permute-start.18 = (f32[272]{0:T(512)S(1)}, f32[272]{0:T(512)S(1)}, u32[]{:S(2)}, u32[]{:S(2)}) collective-permute-start(f32[272]{0:T(512)S(1)} %get-tuple-element.25), channel_id=1, source_target_pairs={{0,12},{4,8},{8,4},{12,0},{16,28},{20,24},{24,20},{28,16},{1,13},{... | collective-permute-start | bytes 3272 | tf_op jit(solution)/shard_map/ppermute | solution.py:15
  305.8 11.3 %collective-permute-start.19 = (f32[272]{0:T(512)S(1)}, f32[272]{0:T(512)S(1)}, u32[]{:S(2)}, u32[]{:S(2)}) collective-permute-start(f32[272]{0:T(512)S(1)} %get-tuple-element.24), channel_id=1, source_target_pairs={{0,16},{4,20},{8,24},{12,28},{16,0},{20,4},{24,8},{28,12},{1,17},{... | collective-permute-start | bytes 3272 | tf_op jit(solution)/shard_map/ppermute | solution.py:15
  305.9 11.1 %collective-permute-start.20 = (f32[272]{0:T(512)S(1)}, f32[272]{0:T(512)S(1)}, u32[]{:S(2)}, u32[]{:S(2)}) collective-permute-start(f32[272]{0:T(512)S(1)} %get-tuple-element.23), channel_id=1, source_target_pairs={{0,20},{4,16},{8,28},{12,24},{16,4},{20,0},{24,12},{28,8},{1,21},{... | collective-permute-start | bytes 3272 | tf_op jit(solution)/shard_map/ppermute | solution.py:15
  315.5 64.8 %collective-permute-start.9 = (bf16[272,512]{1,0:T(8,128)(2,1)}, bf16[272,512]{1,0:T(8,128)(2,1)}, u32[]{:S(2)}, u32[]{:S(2)}) collective-permute-start(bf16[272,512]{1,0:T(8,128)(2,1)} %get-tuple-element.57), channel_id=1, source_target_pairs={{0,4},{4,0},{8,12},{12,8},{16,20},{20,16},{24,28},{28,24},{1,5},{5... | collective-permute-start | bytes 835592 | tf_op jit(solution)/shard_map/ppermute | solution.py:15
  317.0 65.9 %collective-permute-start.10 = (bf16[272,512]{1,0:T(8,128)(2,1)}, bf16[272,512]{1,0:T(8,128)(2,1)}, u32[]{:S(2)}, u32[]{:S(2)}) collective-permute-start(bf16[272,512]{1,0:T(8,128)(2,1)} %get-tuple-element.56), channel_id=1, source_target_pairs={{0,8},{4,12},{8,0},{12,4},{16,24},{20,28},{24,16},{28,20},{1,9},{5... | collective-permute-start | bytes 835592 | tf_op jit(solution)/shard_map/ppermute | solution.py:15
  317.0 69.2 %collective-permute-start.11 = (bf16[272,512]{1,0:T(8,128)(2,1)}, bf16[272,512]{1,0:T(8,128)(2,1)}, u32[]{:S(2)}, u32[]{:S(2)}) collective-permute-start(bf16[272,512]{1,0:T(8,128)(2,1)} %get-tuple-element.55), channel_id=1, source_target_pairs={{0,12},{4,8},{8,4},{12,0},{16,28},{20,24},{24,20},{28,16},{1,13},{... | collective-permute-start | bytes 835592 | tf_op jit(solution)/shard_map/ppermute | solution.py:15
  319.1 68.2 %collective-permute-start.12 = (bf16[272,512]{1,0:T(8,128)(2,1)}, bf16[272,512]{1,0:T(8,128)(2,1)S(1)}, u32[]{:S(2)}, u32[]{:S(2)}) collective-permute-start(bf16[272,512]{1,0:T(8,128)(2,1)} %get-tuple-element.54), channel_id=1, source_target_pairs={{0,16},{4,20},{8,24},{12,28},{16,0},{20,4},{24,8},{28,12},{1,17},{... | collective-permute-start | bytes 835592 | tf_op jit(solution)/shard_map/ppermute | solution.py:15
  319.5 69.3 %collective-permute-start.13 = (bf16[272,512]{1,0:T(8,128)(2,1)}, bf16[272,512]{1,0:T(8,128)(2,1)S(1)}, u32[]{:S(2)}, u32[]{:S(2)}) collective-permute-start(bf16[272,512]{1,0:T(8,128)(2,1)} %get-tuple-element.53), channel_id=1, source_target_pairs={{0,20},{4,16},{8,28},{12,24},{16,4},{20,0},{24,12},{28,8},{1,21},{... | collective-permute-start | bytes 835592 | tf_op jit(solution)/shard_map/ppermute | solution.py:15
  383.0 14.0 %collective-permute-start.15 = (bf16[272,512]{1,0:T(8,128)(2,1)S(1)}, bf16[272,512]{1,0:T(8,128)(2,1)S(1)}, u32[]{:S(2)}, u32[]{:S(2)}) collective-permute-start(bf16[272,512]{1,0:T(8,128)(2,1)S(1)} %copy-done.55), channel_id=1, source_target_pairs={{0,28},{4,24},{8,20},{12,16},{16,12},{20,8},{24,4},{28,0},{1,29},{... | collective-permute-start | bytes 835592 | tf_op jit(solution)/shard_map/ppermute | solution.py:15
  386.2 208.5 %collective-permute-start.74 = (bf16[2,1024,512]{2,1,0:T(8,128)(2,1)}, bf16[2,1024,512]{2,1,0:T(8,128)(2,1)}, u32[]{:S(2)}, u32[]{:S(2)}) collective-permute-start(bf16[2,1024,512]{2,1,0:T(8,128)(2,1)} %fusion.59), channel_id=1, source_target_pairs={{0,1},{1,0},{2,3},{3,2},{4,5},{5,4},{6,7},{7,6},{8,9},{9,8},{10,11... | collective-permute-start | bytes 6291464 | tf_op jit(solution)/shard_map/ppermute | solution.py:15
  387.3 26.1 %collective-permute-start.30 = (bf16[272,512]{1,0:T(8,128)(2,1)}, bf16[272,512]{1,0:T(8,128)(2,1)}, u32[]{:S(2)}, u32[]{:S(2)}) collective-permute-start(bf16[272,512]{1,0:T(8,128)(2,1)} %get-tuple-element.43), channel_id=1, source_target_pairs={{0,4},{4,0},{8,12},{12,8},{16,20},{20,16},{24,28},{28,24},{1,5},{5... | collective-permute-start | bytes 835592 | tf_op jit(solution)/shard_map/ppermute | solution.py:15
  388.9 27.2 %collective-permute-start.31 = (bf16[272,512]{1,0:T(8,128)(2,1)}, bf16[272,512]{1,0:T(8,128)(2,1)S(1)}, u32[]{:S(2)}, u32[]{:S(2)}) collective-permute-start(bf16[272,512]{1,0:T(8,128)(2,1)} %get-tuple-element.42), channel_id=1, source_target_pairs={{0,8},{4,12},{8,0},{12,4},{16,24},{20,28},{24,16},{28,20},{1,9},{5... | collective-permute-start | bytes 835592 | tf_op jit(solution)/shard_map/ppermute | solution.py:15
  389.0 29.0 %collective-permute-start.32 = (bf16[272,512]{1,0:T(8,128)(2,1)}, bf16[272,512]{1,0:T(8,128)(2,1)S(1)}, u32[]{:S(2)}, u32[]{:S(2)}) collective-permute-start(bf16[272,512]{1,0:T(8,128)(2,1)} %get-tuple-element.41), channel_id=1, source_target_pairs={{0,12},{4,8},{8,4},{12,0},{16,28},{20,24},{24,20},{28,16},{1,13},{... | collective-permute-start | bytes 835592 | tf_op jit(solution)/shard_map/ppermute | solution.py:15
  397.0 35.5 %collective-permute-start.33 = (bf16[272,512]{1,0:T(8,128)(2,1)}, bf16[272,512]{1,0:T(8,128)(2,1)}, u32[]{:S(2)}, u32[]{:S(2)}) collective-permute-start(bf16[272,512]{1,0:T(8,128)(2,1)} %get-tuple-element.40), channel_id=1, source_target_pairs={{0,16},{4,20},{8,24},{12,28},{16,0},{20,4},{24,8},{28,12},{1,17},{... | collective-permute-start | bytes 835592 | tf_op jit(solution)/shard_map/ppermute | solution.py:15
  413.4 26.0 %collective-permute-start.34 = (bf16[272,512]{1,0:T(8,128)(2,1)S(1)}, bf16[272,512]{1,0:T(8,128)(2,1)S(1)}, u32[]{:S(2)}, u32[]{:S(2)}) collective-permute-start(bf16[272,512]{1,0:T(8,128)(2,1)S(1)} %copy-done.59), channel_id=1, source_target_pairs={{0,20},{4,16},{8,28},{12,24},{16,4},{20,0},{24,12},{28,8},{1,21},{... | collective-permute-start | bytes 835592 | tf_op jit(solution)/shard_map/ppermute | solution.py:15
  416.1 24.1 %collective-permute-start.35 = (bf16[272,512]{1,0:T(8,128)(2,1)S(1)}, bf16[272,512]{1,0:T(8,128)(2,1)S(1)}, u32[]{:S(2)}, u32[]{:S(2)}) collective-permute-start(bf16[272,512]{1,0:T(8,128)(2,1)S(1)} %copy-done.58), channel_id=1, source_target_pairs={{0,24},{4,28},{8,16},{12,20},{16,8},{20,12},{24,0},{28,4},{1,25},{... | collective-permute-start | bytes 835592 | tf_op jit(solution)/shard_map/ppermute | solution.py:15
  418.0 22.9 %collective-permute-start.36 = (bf16[272,512]{1,0:T(8,128)(2,1)S(1)}, bf16[272,512]{1,0:T(8,128)(2,1)S(1)}, u32[]{:S(2)}, u32[]{:S(2)}) collective-permute-start(bf16[272,512]{1,0:T(8,128)(2,1)S(1)} %copy-done.57), channel_id=1, source_target_pairs={{0,28},{4,24},{8,20},{12,16},{16,12},{20,8},{24,4},{28,0},{1,29},{... | collective-permute-start | bytes 835592 | tf_op jit(solution)/shard_map/ppermute | solution.py:15
  508.3 20.9 %collective-permute-start.69 = (f32[10,512]{1,0:T(8,128)S(1)}, f32[10,512]{1,0:T(8,128)S(1)}, u32[]{:S(2)}, u32[]{:S(2)}) collective-permute-start(f32[10,512]{1,0:T(8,128)S(1)} %pad_maximum_fusion.3), channel_id=1, source_target_pairs={{0,1},{1,0},{2,3},{3,2},{4,5},{5,4},{6,7},{7,6},{8,9},{9,8},{10,11... | collective-permute-start | bytes 61448 | tf_op jit(solution)/shard_map/ppermute | solution.py:15
  510.2 20.6 %collective-permute-start.59 = (bf16[16,16,512]{2,1,0:T(8,128)(2,1)S(1)}, bf16[16,16,512]{2,1,0:T(8,128)(2,1)S(1)}, u32[]{:S(2)}, u32[]{:S(2)}) collective-permute-start(bf16[16,16,512]{2,1,0:T(8,128)(2,1)S(1)} %fusion.92), channel_id=1, source_target_pairs={{0,1},{1,0},{2,3},{3,2},{4,5},{5,4},{6,7},{7,6},{8,9},{9,8},{10,11... | collective-permute-start | bytes 786440 | tf_op jit(solution)/shard_map/ppermute | solution.py:15
  524.6 33.6 %collective-permute-start.49 = (bf16[16,48,512]{2,1,0:T(8,128)(2,1)}, bf16[16,48,512]{2,1,0:T(8,128)(2,1)}, u32[]{:S(2)}, u32[]{:S(2)}) collective-permute-start(bf16[16,48,512]{2,1,0:T(8,128)(2,1)} %fusion.80), channel_id=1, source_target_pairs={{0,1},{1,0},{2,3},{3,2},{4,5},{5,4},{6,7},{7,6},{8,9},{9,8},{10,11... | collective-permute-start | bytes 2359304 | tf_op jit(solution)/shard_map/ppermute | solution.py:15
  529.3 16.2 %collective-permute-start.70 = (f32[10,512]{1,0:T(8,128)S(1)}, f32[10,512]{1,0:T(8,128)S(1)}, u32[]{:S(2)}, u32[]{:S(2)}) collective-permute-start(f32[10,512]{1,0:T(8,128)S(1)} %fusion.136), channel_id=1, source_target_pairs={{0,2},{1,3},{2,0},{3,1},{4,6},{5,7},{6,4},{7,5},{8,10},{9,11},{10,... | collective-permute-start | bytes 61448 | tf_op jit(solution)/shard_map/ppermute | solution.py:15
  531.0 15.7 %collective-permute-start.60 = (bf16[8,16,512]{2,1,0:T(8,128)(2,1)S(1)}, bf16[8,16,512]{2,1,0:T(8,128)(2,1)S(1)}, u32[]{:S(2)}, u32[]{:S(2)}) collective-permute-start(bf16[8,16,512]{2,1,0:T(8,128)(2,1)S(1)} %fusion.99), channel_id=1, source_target_pairs={{0,2},{1,3},{2,0},{3,1},{4,6},{5,7},{6,4},{7,5},{8,10},{9,11},{10,... | collective-permute-start | bytes 393224 | tf_op jit(solution)/shard_map/ppermute | solution.py:15
  535.4 12.2 %collective-permute-start.47 = (f32[2,512]{1,0:T(2,128)S(1)}, f32[2,512]{1,0:T(2,128)S(1)}, u32[]{:S(2)}, u32[]{:S(2)}) collective-permute-start(f32[2,512]{1,0:T(2,128)S(1)} %add.267), channel_id=1, source_target_pairs={{0,8},{1,9},{2,10},{3,11},{4,12},{5,13},{6,14},{7,15},{8,0},{9,1},... | collective-permute-start | bytes 12296 | tf_op jit(solution)/shard_map/ppermute | solution.py:15
  586.0 16.8 %collective-permute-start.68 = (bf16[16,16,512]{2,1,0:T(8,128)(2,1)S(1)}, bf16[16,16,512]{2,1,0:T(8,128)(2,1)S(1)}, u32[]{:S(2)}, u32[]{:S(2)}) collective-permute-start(bf16[16,16,512]{2,1,0:T(8,128)(2,1)S(1)} %bitcast.599), channel_id=1, source_target_pairs={{0,1},{1,0},{2,3},{3,2},{4,5},{5,4},{6,7},{7,6},{8,9},{9,8},{10,11... | collective-permute-start | bytes 786440 | tf_op jit(solution)/shard_map/ppermute | solution.py:15
  597.7 31.0 %collective-permute-start.75 = (bf16[1,1024,512]{2,1,0:T(8,128)(2,1)S(1)}, bf16[1,1024,512]{2,1,0:T(8,128)(2,1)S(1)}, u32[]{:S(2)}, u32[]{:S(2)}) collective-permute-start(bf16[1,1024,512]{2,1,0:T(8,128)(2,1)S(1)} %fusion.77), channel_id=1, source_target_pairs={{0,2},{1,3},{2,0},{3,1},{4,6},{5,7},{6,4},{7,5},{8,10},{9,11},{10,... | collective-permute-start | bytes 3145736 | tf_op jit(solution)/shard_map/ppermute | solution.py:15
  600.1 27.3 %collective-permute-start.57 = (bf16[8,48,512]{2,1,0:T(8,128)(2,1)S(1)}, bf16[8,48,512]{2,1,0:T(8,128)(2,1)S(1)}, u32[]{:S(2)}, u32[]{:S(2)}) collective-permute-start(bf16[8,48,512]{2,1,0:T(8,128)(2,1)S(1)} %bitcast.596), channel_id=1, source_target_pairs={{0,2},{1,3},{2,0},{3,1},{4,6},{5,7},{6,4},{7,5},{8,10},{9,11},{10,... | collective-permute-start | bytes 1179656 | tf_op jit(solution)/shard_map/ppermute | solution.py:15
  (129 other events, 1256.5 us)

commit v2 on v1

v2 whole, which is shorter than its diff:
```python
import functools

import jax
import jax.numpy as jnp
from jax import lax
from jax.experimental import pallas as pl
from jax.experimental.pallas import tpu as pltpu
from jax.sharding import PartitionSpec as P

HEADS = 8
TOPK = 2
GROUP = 4
EPSILON = 1e-06
NEGATIVE = -1e30
BF = jnp.bfloat16
F32 = jnp.float32
I32 = jnp.int32


def swap(value, axis, size, flip):
    return lax.ppermute(value, axis, [(i, i ^ flip) for i in range(size)])


def to_all(blocks, axes):
    return lax.all_to_all(blocks, axes, split_axis=0, concat_axis=0, tiled=True)


def together(*values):
    return lax.optimization_barrier(values)


def dot(left, right):
    return jnp.dot(left, right, preferred_element_type=F32)


def dot_nt(left, right):
    return lax.dot_general(left, right, (((1,), (1,)), ((), ())), preferred_element_type=F32)


def dot_tn(left, right):
    return lax.dot_general(left, right, (((0,), (0,)), ((), ())), preferred_element_type=F32)


def row_block(rows):
    return next(size for size in (336, 144, 48, 16) if rows % size == 0)


def iota(shape, dim):
    return lax.broadcasted_iota(jnp.int32, shape, dim)


def high_low(value):
    high = value.astype(BF)
    return high, (value - high.astype(F32)).astype(BF)


def normalise(values):
    average = jnp.mean(values, axis=-1, keepdims=True)
    centred = values - average
    variance = jnp.mean(centred * centred, axis=-1, keepdims=True)
    rstd = lax.rsqrt(variance + EPSILON)
    return centred * rstd, rstd


def norm_back(grad, xhat, rstd, gain):
    scaled = grad * gain
    average = jnp.mean(scaled, axis=-1, keepdims=True)
    along = jnp.mean(scaled * xhat, axis=-1, keepdims=True)
    return rstd * (scaled - average - xhat * along)


def cumulative(value):
    size = jnp.abs(value)
    base = 1.0 + 0.23164188 * size
    guess = pl.reciprocal(base, approx=True)
    t = guess * (2.0 - base * guess)
    bell = jnp.exp(-0.5 * value * value)
    poly = t * (0.127414796 + t * (-0.142248368 + t * (0.7107068705 + t * (-0.7265760135 + t * 0.5307027145))))
    tail = poly * bell
    return jnp.where(value >= 0.0, 1.0 - tail, tail), bell * 0.3989422804014327


def dispatch(targets, data, start, count):
    rows = targets.shape[1]
    slot = iota((count, rows), 0) + start
    hit = (targets[0:1, :] == slot) | (targets[1:2, :] == slot)
    return dot(jnp.where(hit, 1.0, 0.0).astype(BF), data)


def to_columns(row):
    count = row.shape[1]
    gap = -count % 128
    if gap:
        row = jnp.concatenate([row, jnp.zeros((1, gap), F32)], axis=1)
    return jnp.transpose(jnp.broadcast_to(row, (128, count + gap)))[:count]


def route_kernel(
    len_ref, pri_ref, top_ref, cot_ref, col_ref, row_ref, send_ref, column_ref, early_ref,
    *, experts, capacity, first, stride, patches,
):
    rows = pri_ref.shape[1]
    step = row_block(rows)
    token = iota((1, rows), 1)
    present = token < 0
    for i in range(rows // patches):
        present = present | ((token >= i * patches) & (token < i * patches + len_ref[i]))

    column_ref[...] = to_columns(pri_ref[...].astype(F32))
    lane = iota((step, rows), 1).astype(F32)
    place = iota((step, rows), 0).astype(F32)

    def ranks(block, total):
        base = pl.multiple_of(block * step, 16)
        hit = column_ref[pl.ds(base, step), 0:1] == lane
        here = place + (block * step).astype(F32)
        return total + jnp.sum(jnp.where(hit, here, 0.0), axis=0, keepdims=True)

    rank = lax.fori_loop(0, rows // step, ranks, jnp.zeros((1, rows), F32))
    column_ref[...] = to_columns(rank)

    def compare(block, carry):
        here = pl.ds(pl.multiple_of(block * step, 16), step)
        early_ref[here, :] = jnp.where(column_ref[here, 0:1] < rank, 1.0, 0.0).astype(BF)
        return carry

    lax.fori_loop(0, rows // step, compare, 0)
    label = iota((2 * experts, rows), 0)
    tops = [top_ref[0:1, :], top_ref[1:2, :]]
    hot = ((label == tops[0]) | (label == tops[1] + experts)) & present
    hot = jnp.where(hot, 1.0, 0.0)
    counts = dot(hot.astype(BF), early_ref[...])
    before = jnp.sum(hot[:experts], axis=1, keepdims=True)
    counts = [counts[:experts] * hot[:experts], (counts[experts:] + before) * hot[experts:]]
    found = []
    for j in range(TOPK):
        position = jnp.sum(counts[j], axis=0, keepdims=True)
        slot = (tops[j] * stride).astype(F32) + position + jnp.where(position >= first, 2.0, 0.0)
        found.append(jnp.where(present & (position < capacity), slot, -1.0))
    columns = [to_columns(f) for f in found]
    which = iota(columns[0].shape, 1)
    both = jnp.where(which == 0, columns[0], jnp.where(which == 1, columns[1], -1.0))
    col_ref[...] = both.astype(jnp.int32)
    which = iota((8, rows), 0)
    targets = jnp.where(which == 0, found[0], jnp.where(which == 1, found[1], -1.0))
    targets = targets.astype(jnp.int32)
    row_ref[...] = targets
    for e in range(experts):
        send_ref[e] = dispatch(targets, cot_ref[...], e * stride, stride).astype(BF)


def put_rows(ref, e, block, column):
    count, width = block.shape
    eye = iota((count, width), 0) == iota((count, width), 1)
    high, low = high_low(jnp.sum(jnp.where(eye, column, 0.0), axis=0, keepdims=True))
    ref[e, 0 : count - 16, :] = block[0 : count - 16].astype(BF)
    tail = iota((16, width), 0)
    last = block[count - 16 :]
    last = jnp.where(tail == 14, high.astype(F32), jnp.where(tail == 15, low.astype(F32), last))
    ref[e, count - 16 :, :] = last.astype(BF)


def get_column(ref, e):
    count, width = ref.shape[1:]
    last = jnp.where(iota((16, width), 0) >= 14, ref[e, count - 16 :, :].astype(F32), 0.0)
    eye = iota((count, width), 0) == iota((count, width), 1)
    return jnp.sum(jnp.where(eye, jnp.sum(last, axis=0, keepdims=True), 0.0), axis=1, keepdims=True)


def stack_heads(block, heads, size):
    head = iota(block.shape, 1) // size
    zero = jnp.zeros(block.shape, block.dtype)
    return jnp.concatenate([jnp.where(head == h, block, zero) for h in range(heads)])


def take_heads(stacked, heads, size):
    rows = stacked.shape[0] // heads
    head = iota((rows, stacked.shape[1]), 1) // size
    taken = stacked[:rows]
    for h in range(1, heads):
        taken = jnp.where(head == h, stacked[h * rows : (h + 1) * rows], taken)
    return taken


def forward_kernel(
    len_ref, image_ref, gain_one, shift_one, wq_ref, wk_ref, wv_ref, wo_ref, gain_two, shift_two,
    router_ref, row_ref, normed_ref, q_ref, k_ref, v_ref, prob_ref, mixed_ref, residual_ref, two_ref,
    soft_ref, send_a, send_b, side_ref, *, experts, stride, patches, group,
):
    rows, width = image_ref.shape
    size = width // HEADS
    lanes = group * size
    step = row_block(rows)

    def project(block, carry):
        here = pl.ds(pl.multiple_of(block * step, 16), step)
        xhat, _ = normalise(image_ref[here, :].astype(F32))
        normed = (xhat * gain_one[...] + shift_one[...]).astype(BF)
        normed_ref[here, :] = normed
        q_ref[here, :] = (dot(normed, wq_ref[...]) * size**-0.5).astype(BF)
        k_ref[here, :] = dot(normed, wk_ref[...]).astype(BF)
        v_ref[here, :] = dot(normed, wv_ref[...]).astype(BF)
        return carry

    lax.fori_loop(0, rows // step, project, 0)

    def attend(image, carry):
        here = pl.ds(pl.multiple_of(image * patches, 16), patches)
        length = len_ref[image]
        for g in range(HEADS // group):
            cols = pl.ds(g * lanes, lanes)
            queries = stack_heads(q_ref[here, cols], group, size)
            scores = dot_nt(k_ref[here, cols], queries)
            scores = jnp.where(iota(scores.shape, 0) < length, scores, NEGATIVE)
            top = jnp.max(scores, axis=0, keepdims=True)
            exponent = jnp.exp(scores - top)
            total = jnp.sum(exponent, axis=0, keepdims=True)
            probs = (exponent * (1.0 / total)).astype(BF)
            prob_ref[image, g] = probs
            mixed = take_heads(dot_tn(probs, v_ref[here, cols]), group, size)
            mixed_ref[here, cols] = mixed.astype(BF)
        return carry

    lax.fori_loop(0, rows // patches, attend, 0)

    def finish(block, carry):
        here = pl.ds(pl.multiple_of(block * step, 16), step)
        residual = image_ref[here, :].astype(F32) + dot(mixed_ref[here, :], wo_ref[...])
        residual_ref[here, :] = residual
        xhat, _ = normalise(residual)
        two = (xhat * gain_two[...] + shift_two[...]).astype(BF)
        two_ref[here, :] = two
        logits = dot(two, router_ref[...])
        valid = iota(logits.shape, 1) < experts
        logits = jnp.where(valid, logits, NEGATIVE)
        exponent = jnp.exp(logits - jnp.max(logits, axis=1, keepdims=True))
        soft = exponent / jnp.sum(exponent, axis=1, keepdims=True)
        soft_ref[here, :] = soft
        high, low = high_low(soft)
        side_ref[here, 0:128] = high
        side_ref[here, 128:256] = low
        return carry

    lax.fori_loop(0, rows // step, finish, 0)

    targets = row_ref[...]
    begin = 0
    for send_ref in (send_a, send_b):
        count = send_ref.shape[1]
        for e in range(experts):
            slot = iota((count, rows), 0) + (e * stride + begin)
            hit = (targets[0:1, :] == slot) | (targets[1:2, :] == slot)
            hot = jnp.where(hit, 1.0, 0.0).astype(BF)
            side = dot(hot, side_ref[...])
            side = side[:, 0:128] + side[:, 128:256]
            gate = jnp.sum(jnp.where(iota(side.shape, 1) == e, side, 0.0), axis=1, keepdims=True)
            put_rows(send_ref, e, dot(hot, two_ref[...]), gate)
        begin += count


def expert_kernel(x_ref, cot_ref, *refs, begin):
    weights, (res_ref, back_ref, act_ref, pre_ref, grad_ref) = refs[:-5], refs[-5:]
    pieces = len(weights) // 2
    chunks, count, width = x_ref.shape
    units = weights[0].shape[1]
    gates = [get_column(x_ref, c) for c in range(chunks)]
    gate = jnp.concatenate(gates)
    x = x_ref[...].reshape(chunks * count, width)
    cot = cot_ref[:, begin : begin + count, :].reshape(chunks * count, width).astype(F32)
    grad = (gate * cot).astype(BF)
    grad_ref[...] = grad.reshape(chunks, count, width)
    result = jnp.zeros((chunks * count, width), F32)
    back = jnp.zeros((chunks * count, width), F32)
    for s in range(pieces):
        cols = pl.ds(s * units, units)
        first, second = weights[s], weights[pieces + s]
        hidden = dot(x, first[...])
        below, bell = cumulative(hidden)
        act = (hidden * below).astype(BF)
        act_ref[:, :, cols] = act.reshape(chunks, count, units)
        result = result + dot(act, second[...])
        pre = (dot_nt(grad, second[...]) * (below + hidden * bell)).astype(BF)
        pre_ref[:, :, cols] = pre.reshape(chunks, count, units)
        back = back + dot_nt(pre, first[...])
    res_ref[...] = (gate * result).astype(BF).reshape(chunks, count, width)
    along = jnp.sum(cot * result, axis=1, keepdims=True)
    for c in range(chunks):
        here = slice(c * count, (c + 1) * count)
        put_rows(back_ref, c, back[here], along[here])


def expert_grad_kernel(
    x_a, x_b, pre_a, pre_b, act_a, act_b, grad_a, grad_b, in_near, in_far, out_near, out_far
):
    near = pl.program_id(0) < pl.num_programs(0) // 2
    grad_in = (dot_tn(x_a[...], pre_a[...]) + dot_tn(x_b[...], pre_b[...])).astype(BF)
    grad_out = (dot_tn(act_a[...], grad_a[...]) + dot_tn(act_b[...], grad_b[...])).astype(BF)

    @pl.when(near)
    def _():
        in_near[0] = grad_in
        out_near[0] = grad_out

    @pl.when(jnp.logical_not(near))
    def _():
        in_far[0] = grad_in
        out_far[0] = grad_out


def hot_of(col_ref, here, slots):
    columns = col_ref[here, :]
    slot = iota((columns.shape[0], slots), 1)
    hit = (columns[:, 0:1] == slot) | (columns[:, 1:2] == slot)
    return jnp.where(hit, 1.0, 0.0).astype(BF)


def backward_kernel(*refs, experts, stride, patches, group):
    (back_a, back_b, col_ref, soft_ref, residual_ref, cot_ref, two_ref, mixed_ref, normed_ref, q_ref, k_ref, v_ref, prob_ref,
     gain_two, router_ref, wo_ref,
     resid_ref, gq_ref, gk_ref, gv_ref, wg_out_ref, wg_q_ref, wg_k_ref, wg_v_ref, wg_router_ref, small_ref,
     slots_ref, attn_ref, gm_ref, logit_ref) = refs
    rows, width = cot_ref.shape
    size = width // HEADS
    lanes = group * size
    step = 144
    slots = experts * stride
    for e in range(experts):
        base = e * stride
        for back_ref in (back_a, back_b):
            here = slice(base, base + back_ref.shape[1])
            base += back_ref.shape[1]
            slots_ref[here, 0:width] = back_ref[e]
            along = get_column(back_ref, e)
            label = iota((along.shape[0], 128), 1)
            high, low = high_low(jnp.where(label == e, along, 0.0))
            slots_ref[here, width : width + 128] = high
            slots_ref[here, width + 128 : width + 256] = low

    def combine(block, carry):
        gain_sum, shift_sum = carry
        here = pl.ds(pl.multiple_of(block * step, 16), step)
        both = dot(hot_of(col_ref, here, slots), slots_ref[...])
        grad_two = both[:, 0:width]
        grad_gate = both[:, width : width + 128] + both[:, width + 128 : width + 256]
        soft = soft_ref[here, :]
        inner = jnp.sum(soft * grad_gate, axis=1, keepdims=True)
        logits = (soft * (grad_gate - inner)).astype(BF)
        logit_ref[here, :] = logits
        grad_two = grad_two + dot_nt(logits, router_ref[...])
        xhat, rstd = normalise(residual_ref[here, :])
        grad = cot_ref[here, :].astype(F32) + norm_back(grad_two, xhat, rstd, gain_two[...])
        resid_ref[here, :] = grad
        low = grad.astype(BF)
        attn_ref[here, :] = low
        gm_ref[here, :] = dot_nt(low, wo_ref[...]).astype(BF)
        gain_sum = gain_sum + jnp.sum(grad_two * xhat, axis=0, keepdims=True)
        shift_sum = shift_sum + jnp.sum(grad_two, axis=0, keepdims=True)
        return gain_sum, shift_sum

    zero = jnp.zeros((1, width), F32)
    gain_sum, shift_sum = lax.fori_loop(0, rows // step, combine, (zero, zero))
    which = iota((8, width), 0)
    small_ref[...] = jnp.where(which == 0, gain_sum, jnp.where(which == 1, shift_sum, 0.0))
    wg_router_ref[...] = dot_tn(logit_ref[...], two_ref[...])
    wg_out_ref[...] = dot_tn(mixed_ref[...], attn_ref[...]).astype(BF)

    def attend(image, carry):
        here = pl.ds(pl.multiple_of(image * patches, 16), patches)
        for g in range(HEADS // group):
            cols = pl.ds(g * lanes, lanes)
            probs = prob_ref[image, g]
            wide = probs.astype(F32)
            mixed = stack_heads(gm_ref[here, cols], group, size)
            keys = k_ref[here, cols]
            grad_probs = dot_nt(v_ref[here, cols], mixed)
            inner = jnp.sum(grad_probs * wide, axis=0, keepdims=True)
            scores = (wide * (grad_probs - inner)).astype(BF)
            gv_ref[here, cols] = dot(probs, mixed).astype(BF)
            gk_ref[here, cols] = dot(scores, stack_heads(q_ref[here, cols], group, size)).astype(BF)
            queries = take_heads(dot_tn(scores, keys), group, size)
            gq_ref[here, cols] = (queries * size**-0.5).astype(BF)
        return carry

    lax.fori_loop(0, rows // patches, attend, 0)
    wg_q_ref[...] = dot_tn(normed_ref[...], gq_ref[...]).astype(BF)
    wg_k_ref[...] = dot_tn(normed_ref[...], gk_ref[...]).astype(BF)
    wg_v_ref[...] = dot_tn(normed_ref[...], gv_ref[...]).astype(BF)


def output_kernel(col_ref, residual_ref, res_a, res_b, out_ref, slots_ref):
    step = 144
    base = 0
    for e in range(res_a.shape[0]):
        for res_ref in (res_a, res_b):
            slots_ref[base : base + res_ref.shape[1], :] = res_ref[e]
            base += res_ref.shape[1]

    def combine(block, carry):
        here = pl.ds(pl.multiple_of(block * step, 16), step)
        moe = dot(hot_of(col_ref, here, slots_ref.shape[0]), slots_ref[...])
        out_ref[here, :] = (residual_ref[here, :] + moe).astype(BF)
        return carry

    lax.fori_loop(0, residual_ref.shape[0] // step, combine, 0)


def image_kernel(gq_ref, gk_ref, gv_ref, wq_ref, wk_ref, wv_ref, image_ref, resid_ref, gain_one, out_ref, small_ref):
    rows, width = image_ref.shape
    step = row_block(rows)

    def finish(block, carry):
        gain_sum, shift_sum = carry
        here = pl.ds(pl.multiple_of(block * step, 16), step)
        grad = dot_nt(gq_ref[here, :], wq_ref[...])
        grad = grad + dot_nt(gk_ref[here, :], wk_ref[...])
        grad = grad + dot_nt(gv_ref[here, :], wv_ref[...])
        xhat, rstd = normalise(image_ref[here, :].astype(F32))
        out_ref[here, :] = resid_ref[here, :] + norm_back(grad, xhat, rstd, gain_one[...])
        gain_sum = gain_sum + jnp.sum(grad * xhat, axis=0, keepdims=True)
        shift_sum = shift_sum + jnp.sum(grad, axis=0, keepdims=True)
        return gain_sum, shift_sum

    zero = jnp.zeros((1, width), F32)
    gain_sum, shift_sum = lax.fori_loop(0, rows // step, finish, (zero, zero))
    which = iota((8, width), 0)
    small_ref[...] = jnp.where(which == 0, gain_sum, jnp.where(which == 1, shift_sum, 0.0))


COST = pl.CostEstimate(flops=0, bytes_accessed=0, transcendentals=0)
SCALAR = pl.BlockSpec(memory_space=pltpu.SMEM)
VECTOR = pl.BlockSpec(memory_space=pltpu.VMEM)


def call(kernel, outs, args, scalars=0, scratch=(), **names):
    return pl.pallas_call(
        functools.partial(kernel, **names) if names else kernel,
        out_shape=[jax.ShapeDtypeStruct(shape, kind) for shape, kind in outs],
        in_specs=[SCALAR] * scalars + [VECTOR] * (len(args) - scalars),
        out_specs=[VECTOR] * len(outs),
        scratch_shapes=scratch,
        compiler_params=pltpu.CompilerParams(vmem_limit_bytes=56 << 20),
        cost_estimate=COST,
    )(*args)


def make_on_device(experts, hidden):
    group = ("hh", "el")
    half_e, half_h = experts // 2, hidden // 2

    def over_eh(value):
        return swap(value, "eh", 2, 1)

    def moves(own):
        axes = ("eh", "hh")
        paths = ([(0, 2), (3, 1)], [(1, 0), (2, 3)], [(1, 2), (2, 1)])
        return [lax.ppermute(own, axes, pairs) for pairs in paths]

    def over_hh(value):
        return swap(value, "hh", 2, 1)

    def fold_hl(parts):
        for bit in reversed(range(half_h.bit_length() - 2)):
            count = parts.shape[0] // 2
            far = swap(parts[count:], "hl", half_h, 1 << bit)
            parts = (parts[:count].astype(F32) + far.astype(F32)).astype(BF)
        return parts

    def gather_hl(parts):
        index = lax.axis_index("hl")
        for bit in range(half_h.bit_length() - 1):
            far = swap(parts, "hl", half_h, 1 << bit)
            odd = ((index >> bit) & 1) == 1
            parts = jnp.where(odd, jnp.concatenate([far, parts]), jnp.concatenate([parts, far]))
        return parts

    def scatter_hl(parts):
        index = lax.axis_index("hl")
        for bit in reversed(range(half_h.bit_length() - 1)):
            pairs = parts.reshape((2, -1) + parts.shape[1:])
            odd = (index >> bit) & 1
            keep = lax.dynamic_index_in_dim(pairs, odd, 0, keepdims=False)
            give = lax.dynamic_index_in_dim(pairs, 1 - odd, 0, keepdims=False)
            far = swap(give, "hl", half_h, 1 << bit)
            parts = (keep.astype(F32) + far.astype(F32)).astype(BF)
        return parts[0]

    def on_device(
        images,
        lengths,
        priority,
        top_experts,
        out_grad,
        first_gain,
        first_shift,
        w_query,
        w_key,
        w_value,
        w_output,
        second_gain,
        second_shift,
        w_router,
        w_expert_in,
        w_expert_out,
    ):
        devices = experts * hidden
        image_count, patches, width = images.shape
        rows = image_count * patches
        units = w_expert_in.shape[2]
        hidden_all = units * hidden
        capacity = (21 * rows * TOPK + 20 * experts - 1) // (20 * experts)
        stride = (capacity + 4 + 15) // 16 * 16
        count_a = (stride // 2 + 15) // 16 * 16
        slots = experts * stride
        hh = lax.axis_index("hh")
        same = lax.axis_index("eh") == hh

        block = ((experts, stride, width), BF)
        block_a = ((experts, count_a, width), BF)
        block_b = ((experts, stride - count_a, width), BF)
        token_low = ((rows, width), BF)
        token_wide = ((rows, width), F32)

        own_in, own_out = w_expert_in[0], w_expert_out[0]
        moved_in, moved_out = moves(own_in), moves(own_out)

        cot = out_grad.reshape(rows, width)
        column, row, cot_send = call(
            route_kernel,
            [((rows, 128), I32), ((8, rows), I32), block],
            [lengths, priority, top_experts.reshape(rows, TOPK).T, cot],
            scalars=1,
            scratch=[pltpu.VMEM((rows, 128), F32), pltpu.VMEM((rows, rows), BF)],
            experts=experts,
            capacity=capacity,
            first=count_a - 2,
            stride=stride,
            patches=patches,
        )
        cot_in = to_all(cot_send, group)

        gain_one, shift_one, gain_two, shift_two = (
            v.reshape(1, width) for v in (first_gain, first_shift, second_gain, second_shift)
        )
        router = jnp.pad(w_router, ((0, 0), (0, 128 - experts)))
        tokens = images.reshape(rows, width)
        normed, queries, keys, values, probs, mixed, residual, two, soft, send_a, send_b = call(
            forward_kernel,
            [token_low] * 4
            + [((image_count, HEADS // GROUP, patches, GROUP * patches), BF), token_low, token_wide]
            + [token_low, ((rows, 128), F32), block_a, block_b],
            [lengths, tokens, gain_one, shift_one, w_query, w_key, w_value, w_output]
            + [gain_two, shift_two, router, row],
            scalars=1,
            scratch=[pltpu.VMEM((rows, 256), BF)],
            experts=experts,
            stride=stride,
            patches=patches,
            group=GROUP,
        )

        send_a, cot_in = together(send_a, cot_in)
        x_a = to_all(send_a, group)
        send_b, moved_in, moved_out = together(send_b, moved_in, moved_out)
        x_b = to_all(send_b, group)

        def pieces_of(own, moved):
            by_eh, by_hh, by_both = moved
            pieces = [jnp.where(same, own, by_eh), jnp.where(same, by_hh, by_both)]
            for bit in range(half_h.bit_length() - 1):
                pieces = pieces + [swap(p, "hl", half_h, 1 << bit) for p in pieces]
            return pieces

        weights = pieces_of(own_in, moved_in) + pieces_of(own_out, moved_out)

        def serve(x, begin):
            count = x.shape[1]

            def spec(rows_here, lanes):
                return pl.BlockSpec((2, rows_here, lanes), lambda i: (i, 0, 0))

            lanes_out = (width, width, hidden_all, hidden_all, width)
            return pl.pallas_call(
                functools.partial(expert_kernel, begin=begin),
                grid=(experts // 2,),
                out_shape=[jax.ShapeDtypeStruct((experts, count, n), BF) for n in lanes_out],
                in_specs=[spec(count, width), spec(stride, width)]
                + [pl.BlockSpec(w.shape, lambda i: (0, 0)) for w in weights],
                out_specs=[spec(count, n) for n in lanes_out],
                compiler_params=pltpu.CompilerParams(vmem_limit_bytes=56 << 20),
                cost_estimate=COST,
            )(x, cot_in, *weights)

        result_a, back_a, act_a, pre_a, grad_a = serve(x_a, 0)
        back_a = to_all(back_a, group)
        result_b, back_b, act_b, pre_b, grad_b = serve(x_b, count_a)
        back_b = to_all(back_b, group)

        half = hidden // 2

        def near(f):
            return (jnp.minimum(f, half - 1), 0, 0)

        def far(f):
            return (jnp.maximum(f - half, 0), 0, 0)

        def rows_of(array):
            return array.reshape(-1, array.shape[2])

        pairs = [x_a, x_b, pre_a, pre_b, act_a, act_b, grad_a, grad_b]
        pairs = [rows_of(p) for p in pairs]
        full = [pl.BlockSpec(p.shape, lambda f: (0, 0)) for p in pairs[:2]]
        part = [pl.BlockSpec((p.shape[0], units), lambda f: (0, f)) for p in pairs[:2]]
        in_near, in_far, out_near, out_far = pl.pallas_call(
            expert_grad_kernel,
            grid=(hidden,),
            out_shape=[jax.ShapeDtypeStruct((half, width, units), BF)] * 2
            + [jax.ShapeDtypeStruct((half, units, width), BF)] * 2,
            in_specs=full + part + part + full,
            out_specs=[pl.BlockSpec((1, width, units), near), pl.BlockSpec((1, width, units), far)]
            + [pl.BlockSpec((1, units, width), near), pl.BlockSpec((1, units, width), far)],
            compiler_params=pltpu.CompilerParams(vmem_limit_bytes=56 << 20),
            cost_estimate=COST,
        )(*pairs)

        def fold_far(near_parts, far_parts):
            came = swap(far_parts, "hl", half_h, half_h // 2)
            return fold_hl((near_parts.astype(F32) + came.astype(F32)).astype(BF))

        parts_in, parts_out = fold_far(in_near, in_far), fold_far(out_near, out_far)
        result_a, result_b, back_a, back_b, parts_in, parts_out = together(
            result_a, result_b, back_a, back_b, parts_in, parts_out
        )
        result_a, result_b = to_all(result_a, group), to_all(result_b, group)
        came_in, came_out = over_hh(parts_in[1]), over_hh(parts_out[1])

        resid, gq, gk, gv, wg_out, wg_q, wg_k, wg_v, wg_router, small_two = call(
            backward_kernel,
            [token_wide] + [token_low] * 3 + [((width, width), BF)] * 4
            + [((128, width), F32), ((8, width), F32)],
            [back_a, back_b, column, soft, residual, cot, two, mixed, normed, queries, keys, values, probs]
            + [gain_two, router, w_output],
            scratch=[
                pltpu.VMEM((slots, width + 256), BF),
                pltpu.VMEM((rows, width), BF),
                pltpu.VMEM((rows, width), BF),
                pltpu.VMEM((rows, 128), BF),
            ],
            experts=experts,
            stride=stride,
            patches=patches,
            group=GROUP,
        )

        wg_out, wg_q, wg_k, wg_v, gq, came_in, came_out = together(
            wg_out, wg_q, wg_k, wg_v, gq, came_in, came_out
        )

        def finish_sum(keep, came):
            return jnp.where(same, keep, came), over_eh(jnp.where(same, came, keep))

        mine_in, far_in = finish_sum(parts_in[0], came_in)
        (block_out,) = call(
            output_kernel,
            [token_low],
            [column, residual, result_a, result_b],
            scratch=[pltpu.VMEM((slots, width), BF)],
        )
        grad_images, small_one = call(
            image_kernel,
            [token_wide, ((8, width), F32)],
            [gq, gk, gv, w_query, w_key, w_value, tokens, resid, gain_one],
        )

        stacked = jnp.concatenate([wg_out, wg_q, wg_k, wg_v])
        pieces = scatter_hl(stacked.reshape(half_h, -1, width))
        pieces = to_all(pieces.reshape(experts, -1, width), group)
        pieces, far_in, came_out, block_out, small_one = together(
            pieces, far_in, came_out, block_out, small_one
        )
        mine_out, far_out = finish_sum(parts_out[0], came_out)
        piece = jnp.sum(pieces.astype(F32), axis=0)
        piece = (piece + over_eh(piece.astype(BF)).astype(F32)).astype(BF)
        pieces = to_all(jnp.broadcast_to(piece, (experts,) + piece.shape), group)
        small = jnp.concatenate([small_one[:2], small_two[:2], wg_router[:experts]])
        small = jnp.sum(to_all(jnp.broadcast_to(small, (experts,) + small.shape), group), axis=0)
        small = small + over_eh(small)
        for bit in range(half_h.bit_length() - 1):
            small = small + swap(small, "hl", half_h, 1 << bit)
        pieces, far_out, small = together(pieces, far_out, small)
        total = gather_hl(pieces.reshape(1, -1, width)).reshape(stacked.shape).astype(F32)
        sum_output, sum_query, sum_key, sum_value = jnp.split(total, 4)
        sum_in = mine_in.astype(F32) + far_in.astype(F32)
        sum_out = mine_out.astype(F32) + far_out.astype(F32)
        return (
            block_out.reshape(images.shape),
            grad_images.reshape(images.shape),
            small[0],
            small[1],
            sum_query,
            sum_key,
            sum_value,
            sum_output,
            small[2],
            small[3],
            small[4:].T,
            sum_in[None],
            sum_out[None],
        )

    return on_device


def solution(mesh):
    experts, hidden = mesh.shape["expert"], mesh.shape["hidden"]
    names = ("eh", "el", "hh", "hl")
    places = mesh.devices.reshape(2, experts // 2, 2, hidden // 2)
    tokens = (P(names, None, None), P(names), P(names, None), P(names, None, None), P(names, None, None))
    weights = (P(("eh", "el"), None, ("hh", "hl")), P(("eh", "el"), ("hh", "hl"), None))
    return jax.shard_map(
        make_on_device(experts, hidden),
        mesh=jax.sharding.Mesh(places, names),
        in_specs=tokens + (P(),) * 9 + weights,
        out_specs=(P(names, None, None),) * 2 + (P(),) * 9 + weights,
        check_vma=False,
    )
```

time: 645 us -> 344 us (0.53); the launches traced: 633 us -> 343 us
  matrix products: 167 us -> 0 us
  Pallas kernels: 0 us -> 128 us
  local copies, waits for them, and re-layouts: 134 us -> 14.9 us
  starting transfers between devices: 137 us -> 79 us
  other arithmetic: 64.2 us -> 19.8 us
  waiting for transfers between devices: 128 us -> 100 us
    dot_general x32 -> x0, matrix products: 167 us -> none  [mm(): return jnp.einsum(spec, left, right, preferred_element_type=F32)]
    pallas_call x0 -> x8, Pallas kernels: none -> 128 us  [the longest x5 68.5 us: call(): pl.pallas_call(functools.partial(kernel, **names) if names else kernel, o...]
    ppermute x76 -> x21, starting transfers between devices: 137 us -> 26.1 us  [the longest x6 19 us: moves(): return [lax.ppermute(own, axes, pairs) for pairs in paths]]
    ppermute x76 -> x21, waiting for transfers between devices: 128 us -> 66.8 us  [the longest x15 42.6 us: swap(): return lax.ppermute(value, axis, [(i, i ^ flip) for i in range(size)])]
    all_to_all x0 -> x10, starting transfers between devices: none -> 52.9 us  [to_all(): return lax.all_to_all(blocks, axes, split_axis=0, concat_axis=0, tiled=True)]
    reshape x12 -> x1, local copies, waits for them, and re-layouts: 40.3 us -> 0.69 us  [on_device(): top_experts.reshape(rows, TOPK)]
    all_to_all x0 -> x10, waiting for transfers between devices: none -> 33.6 us  [to_all(): return lax.all_to_all(blocks, axes, split_axis=0, concat_axis=0, tiled=True)]
    unnamed x233 -> x50, local copies, waits for them, and re-layouts: 34.6 us -> 3.56 us
  transfers between devices with their start and end apart: 76 -> 31, of which waited for: 19 -> 13; matrix products, arithmetic and copies ran while one was open for 32% -> 7% of each run, Pallas kernels for 0% -> 35%
where the time goes in v2:
time: 344 us; the launch traced here: 343 us
  Pallas kernels  128 us (37%)
  waiting for transfers between devices  100 us (29%)
  starting transfers between devices  79 us (23%)
  other arithmetic  19.8 us (6%)
  local copies, waits for them, and re-layouts  14.9 us (4%)
    pallas_call x5, Pallas kernels, call(): pl.pallas_call(functools.partial(kernel, **names) if names else kernel, o...  68.5 us
    all_to_all x10, starting transfers between devices, to_all(): return lax.all_to_all(blocks, axes, split_axis=0, concat_axis=0, tiled=True)  52.9 us
    pallas_call x2, Pallas kernels, serve(): pl.pallas_call(functools.partial(expert_kernel, begin=begin), grid=(exper...  42.8 us
    ppermute x15, waiting for transfers between devices, swap(): return lax.ppermute(value, axis, [(i, i ^ flip) for i in range(size)])  42.6 us
    all_to_all x10, waiting for transfers between devices, to_all(): return lax.all_to_all(blocks, axes, split_axis=0, concat_axis=0, tiled=True)  33.6 us
    ppermute x6, waiting for transfers between devices, moves(): return [lax.ppermute(own, axes, pairs) for pairs in paths]  24.1 us
    ppermute x6, starting transfers between devices, moves(): return [lax.ppermute(own, axes, pairs) for pairs in paths]  19 us
    pallas_call x1, Pallas kernels, on_device(): pl.pallas_call(expert_grad_kernel, grid=(hidden,), out_shape=[jax.ShapeDt...  16.4 us
  transfers between devices with their start and end apart: 31, of which 13 were waited for; matrix products, arithmetic and copies ran while one was open for 7% of the time, Pallas kernels for 35%

profile of v2, /device:TPU:0, one launch (start us, length us, event | category | flops | bytes accessed | tf_op | source)
XLA Modules:
  0.0 342.8 jit_solution(11585286770027493333)
XLA Ops:
  2.0 7.2 %shard_map.255 = (s32[1008,128]{1,0:T(8,128)}, s32[8,1008]{1,0:T(8,128)}, bf16[8,272,512]{2,1,0:T(8,128)(2,1)}) custom-call(s32[7]{0:T(128)} %len_ref.3, s32[1,1008]{1,0:T(1,128)} %pri_ref.1, s32[2,1008]{1,0:T(2,128)} %bitcast.82, bf16[1008,512]{1,0:T(8,128)(2,1)} %bitcast.69), custom_call_target="tpu_custom_call" | custom-call | tf_op jit(solution)/shard_map/pallas_call | solution.py:435
  9.3 6.3 %all-to-all-start = ((bf16[8,272,512]{2,1,0:T(8,128)(2,1)}), bf16[8,272,512]{2,1,0:T(8,128)(2,1)S(1)}, u32[]{:S(2)}, u32[]{:S(2)}) async-start(bf16[8,272,512]{2,1,0:T(8,128)(2,1)} %get-tuple-element.85), calls=%async_computation | async-start | bytes 4456448 | tf_op jit(solution)/shard_map/all_to_all | solution.py:25
  15.6 4.5 %collective-permute-start = (bf16[512,512]{1,0:T(8,128)(2,1)S(1)}, bf16[512,512]{1,0:T(8,128)(2,1)S(1)}, u32[]{:S(2)}, u32[]{:S(2)}) collective-permute-start(bf16[512,512]{1,0:T(8,128)(2,1)S(1)} %bitcast.76), channel_id=1, source_target_pairs={{0,16},{18,2},{1,17},{19,3},{4,20},{22,6},{5,21},{23,7},{8,24},{26... | collective-permute-start | bytes 1572872 | tf_op jit(solution)/shard_map/ppermute | solution.py:456
  20.1 1.3 collective-permute-start.1
  21.4 1.5 collective-permute-start.2
  22.9 8.9 %collective-permute-start.3 = (bf16[512,512]{1,0:T(8,128)(2,1)S(1)}, bf16[512,512]{1,0:T(8,128)(2,1)}, u32[]{:S(2)}, u32[]{:S(2)}) collective-permute-start(bf16[512,512]{1,0:T(8,128)(2,1)S(1)} %bitcast.79), channel_id=1, source_target_pairs={{0,16},{18,2},{1,17},{19,3},{4,20},{22,6},{5,21},{23,7},{8,24},{26... | collective-permute-start | bytes 1572872 | tf_op jit(solution)/shard_map/ppermute | solution.py:456
  31.9 1.3 collective-permute-start.4
  33.1 24.1 %collective-permute-done = bf16[512,512]{1,0:T(8,128)(2,1)S(1)} collective-permute-done((bf16[512,512]{1,0:T(8,128)(2,1)S(1)}, bf16[512,512]{1,0:T(8,128)(2,1)S(1)}, u32[]{:S(2)}, u32[]{:S(2)}) %collective-permute-start) | collective-permute-done | bytes 524320 | tf_op jit(solution)/shard_map/ppermute | solution.py:456
  58.1 1.5 collective-permute-start.5
  60.4 18.9 %shard_map.256 = (bf16[1008,512]{1,0:T(8,128)(2,1)}, bf16[1008,512]{1,0:T(8,128)(2,1)}, bf16[1008,512]{1,0:T(8,128)(2,1)}, bf16[1008,512]{1,0:T(8,128)(2,1)}, bf...) custom-call(s32[7]{0:T(128)} %len_ref.3, ...), custom_call_target="tpu_custom_call" | custom-call | tf_op jit(solution)/shard_map/pallas_call | solution.py:435
  79.4 11.1 %all-to-all-start.2 = ((bf16[8,128,512]{2,1,0:T(8,128)(2,1)}), bf16[8,128,512]{2,1,0:T(8,128)(2,1)S(1)}, u32[]{:S(2)}, u32[]{:S(2)}) async-start(bf16[8,128,512]{2,1,0:T(8,128)(2,1)} %get-tuple-element.96), calls=%async_computation.2 | async-start | bytes 2097152 | tf_op jit(solution)/shard_map/all_to_all | solution.py:25
  90.5 15.1 %all-to-all-done.2.x_ref = bf16[8,128,512]{2,1,0:T(8,128)(2,1)S(1)} async-done(((bf16[8,128,512]{2,1,0:T(8,128)(2,1)}), bf16[8,128,512]{2,1,0:T(8,128)(2,1)S(1)}, u32[]{:S(2)}, u32[]{:S(2)}) %all-to-all-start.2) | async-done | bytes 1048608 | tf_op jit(solution)/shard_map/all_to_all | solution.py:25
  106.5 3.7 %all-to-all-start.1 = ((bf16[8,144,512]{2,1,0:T(8,128)(2,1)}), bf16[8,144,512]{2,1,0:T(8,128)(2,1)S(1)}, u32[]{:S(2)}, u32[]{:S(2)}) async-start(bf16[8,144,512]{2,1,0:T(8,128)(2,1)} %get-tuple-element.86), calls=%async_computation.1 | async-start | bytes 2359296 | tf_op jit(solution)/shard_map/all_to_all | solution.py:25
  110.3 1.2 broadcast_select_fusion.refs_5_
  111.6 1.2 broadcast_select_fusion.2.refs_1_
  117.2 20.7 %shard_map.258 = (bf16[8,128,512]{2,1,0:T(8,128)(2,1)}, bf16[8,128,512]{2,1,0:T(8,128)(2,1)}, bf16[8,128,2048]{2,1,0:T(8,128)(2,1)}, bf16[8,128,2048]{2,1,0:T(8,128)(2,1)}, bf16[8,128,512]{2,1,0:T(8,128)(2,1)}) custom-call(bf16[8,128,512]{2,1,0:T(8,128)(2,1)} %copy-done.2, bf16[8,272,512]{2,1,0:T(8,128)(2,1)} %copy-done, bf16[512,512]{1,0:T(8,128)(2,1)} %copy-done.7, ...), custom_call_target="tpu_custom_call" | custom-call | tf_op jit(solution)/shard_map/pallas_call | solution.py:582
  137.9 5.2 %all-to-all-start.4 = ((bf16[8,128,512]{2,1,0:T(8,128)(2,1)}), bf16[8,128,512]{2,1,0:T(8,128)(2,1)S(1)}, u32[]{:S(2)}, u32[]{:S(2)}) async-start(bf16[8,128,512]{2,1,0:T(8,128)(2,1)} %get-tuple-element.99), calls=%async_computation.4 | async-start | bytes 2097152 | tf_op jit(solution)/shard_map/all_to_all | solution.py:25
  143.1 22.1 %shard_map.257 = (bf16[8,144,512]{2,1,0:T(8,128)(2,1)}, bf16[8,144,512]{2,1,0:T(8,128)(2,1)}, bf16[8,144,2048]{2,1,0:T(8,128)(2,1)}, bf16[8,144,2048]{2,1,0:T(8,128)(2,1)}, bf16[8,144,512]{2,1,0:T(8,128)(2,1)}) custom-call(bf16[8,144,512]{2,1,0:T(8,128)(2,1)} %copy-done.1, bf16[8,272,512]{2,1,0:T(8,128)(2,1)} %copy-done, bf16[512,512]{1,0:T(8,128)(2,1)} %copy-done.7, ...), custom_call_target="tpu_custom_call" | custom-call | tf_op jit(solution)/shard_map/pallas_call | solution.py:582
  165.2 5.1 %all-to-all-start.3 = ((bf16[8,144,512]{2,1,0:T(8,128)(2,1)}), bf16[8,144,512]{2,1,0:T(8,128)(2,1)}, u32[]{:S(2)}, u32[]{:S(2)}) async-start(bf16[8,144,512]{2,1,0:T(8,128)(2,1)} %get-tuple-element.98), calls=%async_computation.3 | async-start | bytes 2359296 | tf_op jit(solution)/shard_map/all_to_all | solution.py:25
  170.4 16.4 %shard_map.259 = (bf16[2,512,512]{2,1,0:T(8,128)(2,1)}, bf16[2,512,512]{2,1,0:T(8,128)(2,1)}, bf16[2,512,512]{2,1,0:T(8,128)(2,1)}, bf16[2,512,512]{2,1,0:T(8,128)(2,1)}) custom-call(bf16[1152,512]{1,0:T(8,128)(2,1)} %bitcast.58, bf16[1024,512]{1,0:T(8,128)(2,1)} %bitcast.59, bf16[1152,2048]{1,0:T(8,128)(2,1)} %bitcast.63, bf16[1024,2048]{1,0:T(8,128)(2,1)} %bitcast.68, ...), custom_call_target="tpu_custom_call" | custom-call | tf_op jit(solution)/shard_map/pallas_call | solution.py:613
  187.3 2.4 collective-permute-done.11
  189.7 1.5 add_convert_fusion
  191.6 5.1 %all-to-all-start.7 = ((bf16[8,128,512]{2,1,0:T(8,128)(2,1)}), bf16[8,128,512]{2,1,0:T(8,128)(2,1)S(1)}, u32[]{:S(2)}, u32[]{:S(2)}) async-start(bf16[8,128,512]{2,1,0:T(8,128)(2,1)} %get-tuple-element.136), calls=%async_computation.7 | async-start | bytes 2097152 | tf_op jit(solution)/shard_map/all_to_all | solution.py:25
  197.5 2.0 collective-permute-start.12
  200.3 13.4 %all-to-all-done.7.res_b = bf16[8,128,512]{2,1,0:T(8,128)(2,1)S(1)} async-done(((bf16[8,128,512]{2,1,0:T(8,128)(2,1)}), bf16[8,128,512]{2,1,0:T(8,128)(2,1)S(1)}, u32[]{:S(2)}, u32[]{:S(2)}) %all-to-all-start.7) | async-done | bytes 1048608 | tf_op jit(solution)/shard_map/all_to_all | solution.py:25
  213.7 4.5 %all-to-all-start.6 = ((bf16[8,144,512]{2,1,0:T(8,128)(2,1)}), bf16[8,144,512]{2,1,0:T(8,128)(2,1)}, u32[]{:S(2)}, u32[]{:S(2)}) async-start(bf16[8,144,512]{2,1,0:T(8,128)(2,1)} %get-tuple-element.135), calls=%async_computation.6 | async-start | bytes 2359296 | tf_op jit(solution)/shard_map/all_to_all | solution.py:25
  218.2 27.5 %shard_map.260 = (f32[1008,512]{1,0:T(8,128)}, bf16[1008,512]{1,0:T(8,128)(2,1)}, bf16[1008,512]{1,0:T(8,128)(2,1)}, bf16[1008,512]{1,0:T(8,128)(2,1)}, bf16[512...) custom-call(bf16[8,144,512]{2,1,0:T(8,128)(2,1)} %all-to-all-done.3., ...), custom_call_target="tpu_custom_call" | custom-call | tf_op jit(solution)/shard_map/pallas_call | solution.py:435
  245.8 1.7 pad_maximum_fusion
  248.5 3.0 collective-permute-done.14
  251.5 2.5 fusion
  254.0 4.9 %all-to-all-start.5 = ((bf16[8,128,512]{2,1,0:T(8,128)(2,1)}), bf16[8,128,512]{2,1,0:T(8,128)(2,1)S(1)}, u32[]{:S(2)}, u32[]{:S(2)}) async-start(bf16[8,128,512]{2,1,0:T(8,128)(2,1)} %bitcast.66), calls=%async_computation.5 | async-start | bytes 2097152 | tf_op jit(solution)/shard_map/all_to_all | solution.py:25
  258.9 1.1 bitcast_select_fusion.3
  261.5 7.4 %shard_map.262 = (f32[1008,512]{1,0:T(8,128)}, f32[8,512]{1,0:T(8,128)}) custom-call(bf16[1008,512]{1,0:T(8,128)(2,1)} %get-tuple-element.137.gq_ref, bf16[1008,512]{1,0:T(8,128)(2,1)} %get-tuple-element.138.gk_ref, bf16[1008,512]{1,0:T(8,128)(2,1)} %get-tuple-element.139.gv_ref, bf16[512,512]{1,0:T(8,128)(2,1)} %wq_ref.3, bf16[512,512]{1,0:T(8,128)(2,1)} %wk_ref.3, ...), custom_call_target="tpu_custom_call" | custom-call | tf_op jit(solution)/shard_map/pallas_call | solution.py:435
  268.9 7.4 %shard_map.261 = bf16[1008,512]{1,0:T(8,128)(2,1)} custom-call(s32[1008,128]{1,0:T(8,128)} %get-tuple-element.112.refs_2_.col_ref, f32[1008,512]{1,0:T(8,128)} %get-tuple-element.114.refs_4_.residual_ref, bf16[8,144,512]{2,1,0:T(8,128)(2,1)} %all-to-all-done.6.res_a, bf16[8,128,512]{2,1,0:T(8,128)(2,1)} %copy-done.10), custom_call_target="tpu_custom_call" | custom-call | tf_op jit(solution)/shard_map/pallas_call | solution.py:435
  276.3 11.1 %collective-permute-done.15 = bf16[512,512]{1,0:T(8,128)(2,1)} collective-permute-done((bf16[512,512]{1,0:T(8,128)(2,1)S(1)}, bf16[512,512]{1,0:T(8,128)(2,1)}, u32[]{:S(2)}, u32[]{:S(2)}) %collective-permute-start.15) | collective-permute-done | bytes 524320 | tf_op jit(solution)/shard_map/ppermute | solution.py:21
  289.2 3.4 all-to-all-start.9
  292.6 1.7 collective-permute-done.16
  294.3 5.1 %all-to-all-done.9 = f32[8,12,512]{2,1,0:T(8,128)S(1)} async-done(((f32[8,12,512]{2,1,0:T(8,128)}), f32[8,12,512]{2,1,0:T(8,128)S(1)}, u32[]{:S(2)}, u32[]{:S(2)}) %all-to-all-start.9) | async-done | bytes 196640 | tf_op jit(solution)/shard_map/all_to_all | solution.py:25
  300.5 3.6 %all-to-all-start.8 = ((bf16[8,128,512]{2,1,0:T(8,128)(2,1)}), bf16[8,128,512]{2,1,0:T(8,128)(2,1)S(1)}, u32[]{:S(2)}, u32[]{:S(2)}) async-start(bf16[8,128,512]{2,1,0:T(8,128)(2,1)} %broadcast_in_dim.12), calls=%async_computation.8 | async-start | bytes 2097152 | tf_op jit(solution)/shard_map/all_to_all | solution.py:25
  304.1 1.9 bitcast_select_fusion.1
  306.0 1.9 collective-permute-start.17
  308.9 1.1 collective-permute-start.18
  310.0 21.0 %collective-permute-done.18 = f32[12,512]{1,0:T(8,128)S(1)} collective-permute-done((f32[12,512]{1,0:T(8,128)S(1)}, f32[12,512]{1,0:T(8,128)S(1)}, u32[]{:S(2)}, u32[]{:S(2)}) %collective-permute-start.18) | collective-permute-done | bytes 24608 | tf_op jit(solution)/shard_map/ppermute | solution.py:21
  331.0 1.2 collective-permute-done.19
  332.4 2.2 add_bitcast_fusion.1
  335.8 2.2 add_bitcast_fusion
  338.0 2.0 maximum_select_fusion
  340.8 2.1 fusion.1
  (106 shorter events, 19.5 us)
Async XLA Ops:
  9.3 6.3 %copy-start.17 = (bf16[1,512,512]{2,1,0:T(8,128)(2,1)S(1)}, bf16[1,512,512]{2,1,0:T(8,128)(2,1)}, u32[]{:S(2)}) copy-start(bf16[1,512,512]{2,1,0:T(8,128)(2,1)} %param.30) | copy-start | bytes 1572868
  9.3 13.7 %copy-start.19 = (bf16[1,512,512]{2,1,0:T(8,128)(2,1)S(1)}, bf16[1,512,512]{2,1,0:T(8,128)(2,1)}, u32[]{:S(2)}) copy-start(bf16[1,512,512]{2,1,0:T(8,128)(2,1)} %param.31) | copy-start | bytes 1572868
  9.3 50.3 %copy-start.23 = (bf16[512,8]{0,1:T(8,128)(2,1)S(1)}, bf16[512,8]{0,1:T(8,128)(2,1)}, u32[]{:S(2)}) copy-start(bf16[512,8]{0,1:T(8,128)(2,1)} %param.29) | copy-start | bytes 24580
  9.3 70.1 %all-to-all-start = ((bf16[8,272,512]{2,1,0:T(8,128)(2,1)}), bf16[8,272,512]{2,1,0:T(8,128)(2,1)S(1)}, u32[]{:S(2)}, u32[]{:S(2)}) async-start(bf16[8,272,512]{2,1,0:T(8,128)(2,1)} %get-tuple-element.85), calls=%async_computation | async-start | bytes 4456448 | tf_op jit(solution)/shard_map/all_to_all | solution.py:25
  15.6 41.7 %collective-permute-start = (bf16[512,512]{1,0:T(8,128)(2,1)S(1)}, bf16[512,512]{1,0:T(8,128)(2,1)S(1)}, u32[]{:S(2)}, u32[]{:S(2)}) collective-permute-start(bf16[512,512]{1,0:T(8,128)(2,1)S(1)} %bitcast.76), channel_id=1, source_target_pairs={{0,16},{18,2},{1,17},{19,3},{4,20},{22,6},{5,21},{23,7},{8,24},{26... | collective-permute-start | bytes 1572872 | tf_op jit(solution)/shard_map/ppermute | solution.py:456
  20.1 59.2 %collective-permute-start.1 = (bf16[512,512]{1,0:T(8,128)(2,1)S(1)}, bf16[512,512]{1,0:T(8,128)(2,1)}, u32[]{:S(2)}, u32[]{:S(2)}) collective-permute-start(bf16[512,512]{1,0:T(8,128)(2,1)S(1)} %bitcast.77), channel_id=1, source_target_pairs={{2,0},{16,18},{3,1},{17,19},{6,4},{20,22},{7,5},{21,23},{10,8},{24... | collective-permute-start | bytes 1572872 | tf_op jit(solution)/shard_map/ppermute | solution.py:456
  21.4 57.9 %collective-permute-start.2 = (bf16[512,512]{1,0:T(8,128)(2,1)S(1)}, bf16[512,512]{1,0:T(8,128)(2,1)}, u32[]{:S(2)}, u32[]{:S(2)}) collective-permute-start(bf16[512,512]{1,0:T(8,128)(2,1)S(1)} %bitcast.78), channel_id=1, source_target_pairs={{2,16},{16,2},{3,17},{17,3},{6,20},{20,6},{7,21},{21,7},{10,24},{2... | collective-permute-start | bytes 1572872 | tf_op jit(solution)/shard_map/ppermute | solution.py:456
  22.9 56.4 %collective-permute-start.3 = (bf16[512,512]{1,0:T(8,128)(2,1)S(1)}, bf16[512,512]{1,0:T(8,128)(2,1)}, u32[]{:S(2)}, u32[]{:S(2)}) collective-permute-start(bf16[512,512]{1,0:T(8,128)(2,1)S(1)} %bitcast.79), channel_id=1, source_target_pairs={{0,16},{18,2},{1,17},{19,3},{4,20},{22,6},{5,21},{23,7},{8,24},{26... | collective-permute-start | bytes 1572872 | tf_op jit(solution)/shard_map/ppermute | solution.py:456
  31.9 47.5 %collective-permute-start.4 = (bf16[512,512]{1,0:T(8,128)(2,1)S(1)}, bf16[512,512]{1,0:T(8,128)(2,1)}, u32[]{:S(2)}, u32[]{:S(2)}) collective-permute-start(bf16[512,512]{1,0:T(8,128)(2,1)S(1)} %bitcast.80), channel_id=1, source_target_pairs={{2,0},{16,18},{3,1},{17,19},{6,4},{20,22},{7,5},{21,23},{10,8},{24... | collective-permute-start | bytes 1572872 | tf_op jit(solution)/shard_map/ppermute | solution.py:456
  58.1 21.3 %collective-permute-start.5 = (bf16[512,512]{1,0:T(8,128)(2,1)S(1)}, bf16[512,512]{1,0:T(8,128)(2,1)}, u32[]{:S(2)}, u32[]{:S(2)}) collective-permute-start(bf16[512,512]{1,0:T(8,128)(2,1)S(1)} %bitcast.81), channel_id=1, source_target_pairs={{2,16},{16,2},{3,17},{17,3},{6,20},{20,6},{7,21},{21,7},{10,24},{2... | collective-permute-start | bytes 1572872 | tf_op jit(solution)/shard_map/ppermute | solution.py:456
  79.3 27.2 %copy-start = (bf16[8,272,512]{2,1,0:T(8,128)(2,1)}, bf16[8,272,512]{2,1,0:T(8,128)(2,1)S(1)}, u32[]{:S(2)}) copy-start(bf16[8,272,512]{2,1,0:T(8,128)(2,1)S(1)} %all-to-all-done.cot_ref) | copy-start | bytes 6684676
  79.4 26.2 %all-to-all-start.2 = ((bf16[8,128,512]{2,1,0:T(8,128)(2,1)}), bf16[8,128,512]{2,1,0:T(8,128)(2,1)S(1)}, u32[]{:S(2)}, u32[]{:S(2)}) async-start(bf16[8,128,512]{2,1,0:T(8,128)(2,1)} %get-tuple-element.96), calls=%async_computation.2 | async-start | bytes 2097152 | tf_op jit(solution)/shard_map/all_to_all | solution.py:25
  106.5 31.4 %all-to-all-start.1 = ((bf16[8,144,512]{2,1,0:T(8,128)(2,1)}), bf16[8,144,512]{2,1,0:T(8,128)(2,1)S(1)}, u32[]{:S(2)}, u32[]{:S(2)}) async-start(bf16[8,144,512]{2,1,0:T(8,128)(2,1)} %get-tuple-element.86), calls=%async_computation.1 | async-start | bytes 2359296 | tf_op jit(solution)/shard_map/all_to_all | solution.py:25
  110.3 3.0 copy-start.18
  110.3 3.0 copy-start.22
  110.3 3.3 copy-start.20
  111.5 2.6 collective-permute-start.9
  112.8 3.5 %copy-start.6 = (bf16[512,512]{1,0:T(8,128)(2,1)}, bf16[512,512]{1,0:T(8,128)(2,1)S(1)}, u32[]{:S(2)}) copy-start(bf16[512,512]{1,0:T(8,128)(2,1)S(1)} %broadcast_select_fusion.2.refs_1_) | copy-start | bytes 1572868
  112.9 2.0 collective-permute-start.7
  113.4 3.0 copy-start.7
  113.4 2.2 collective-permute-start.6
  113.7 2.7 copy-start.8
  113.7 2.7 collective-permute-start.8
  114.1 2.2 copy-start.11
  137.9 5.2 %copy-start.1 = (bf16[8,144,512]{2,1,0:T(8,128)(2,1)}, bf16[8,144,512]{2,1,0:T(8,128)(2,1)S(1)}, u32[]{:S(2)}) copy-start(bf16[8,144,512]{2,1,0:T(8,128)(2,1)S(1)} %all-to-all-done.1.x_ref) | copy-start | bytes 3538948
  137.9 27.3 %all-to-all-start.4 = ((bf16[8,128,512]{2,1,0:T(8,128)(2,1)}), bf16[8,128,512]{2,1,0:T(8,128)(2,1)S(1)}, u32[]{:S(2)}, u32[]{:S(2)}) async-start(bf16[8,128,512]{2,1,0:T(8,128)(2,1)} %get-tuple-element.99), calls=%async_computation.4 | async-start | bytes 2097152 | tf_op jit(solution)/shard_map/all_to_all | solution.py:25
  165.2 21.5 %copy-start.9 = (bf16[8,128,512]{2,1,0:T(8,128)(2,1)}, bf16[8,128,512]{2,1,0:T(8,128)(2,1)S(1)}, u32[]{:S(2)}) copy-start(bf16[8,128,512]{2,1,0:T(8,128)(2,1)S(1)} %all-to-all-done.4.refs_1_) | copy-start | bytes 3145732
  165.2 26.3 %all-to-all-start.3 = ((bf16[8,144,512]{2,1,0:T(8,128)(2,1)}), bf16[8,144,512]{2,1,0:T(8,128)(2,1)}, u32[]{:S(2)}, u32[]{:S(2)}) async-start(bf16[8,144,512]{2,1,0:T(8,128)(2,1)} %get-tuple-element.98), calls=%async_computation.3 | async-start | bytes 2359296 | tf_op jit(solution)/shard_map/all_to_all | solution.py:25
  186.7 4.5 %copy-start.15 = (bf16[2,512,512]{2,1,0:T(8,128)(2,1)S(1)}, bf16[2,512,512]{2,1,0:T(8,128)(2,1)}, u32[]{:S(2)}) copy-start(bf16[2,512,512]{2,1,0:T(8,128)(2,1)} %get-tuple-element.106) | copy-start | bytes 3145732
  186.7 2.9 collective-permute-start.11
  186.8 4.4 %collective-permute-start.10 = (bf16[2,512,512]{2,1,0:T(8,128)(2,1)}, bf16[2,512,512]{2,1,0:T(8,128)(2,1)S(1)}, u32[]{:S(2)}, u32[]{:S(2)}) collective-permute-start(bf16[2,512,512]{2,1,0:T(8,128)(2,1)} %get-tuple-element.107), channel_id=1, source_target_pairs={{0,1},{1,0},{2,3},{3,2},{4,5},{5,4},{6,7},{7,6},{8,9},{9,8},{10,11... | collective-permute-start | bytes 3145736 | tf_op jit(solution)/shard_map/ppermute | solution.py:21
  191.5 8.8 %copy-start.3 = (bf16[2,512,512]{2,1,0:T(8,128)(2,1)}, bf16[2,512,512]{2,1,0:T(8,128)(2,1)S(1)}, u32[]{:S(2)}) copy-start(bf16[2,512,512]{2,1,0:T(8,128)(2,1)S(1)} %add_convert_fusion.1) | copy-start | bytes 3145732
  191.6 22.2 %all-to-all-start.7 = ((bf16[8,128,512]{2,1,0:T(8,128)(2,1)}), bf16[8,128,512]{2,1,0:T(8,128)(2,1)S(1)}, u32[]{:S(2)}, u32[]{:S(2)}) async-start(bf16[8,128,512]{2,1,0:T(8,128)(2,1)} %get-tuple-element.136), calls=%async_computation.7 | async-start | bytes 2097152 | tf_op jit(solution)/shard_map/all_to_all | solution.py:25
  197.5 48.3 %collective-permute-start.12 = (bf16[512,512]{1,0:T(8,128)(2,1)}, bf16[512,512]{1,0:T(8,128)(2,1)}, u32[]{:S(2)}, u32[]{:S(2)}) collective-permute-start(bf16[512,512]{1,0:T(8,128)(2,1)} %slice_bitcast_fusion.1), channel_id=1, source_target_pairs={{0,2},{2,0},{1,3},{3,1},{4,6},{6,4},{5,7},{7,5},{8,10},{10,8},{9,1... | collective-permute-start | bytes 1572872 | tf_op jit(solution)/shard_map/ppermute | solution.py:21
  200.3 45.5 %collective-permute-start.13 = (bf16[512,512]{1,0:T(8,128)(2,1)}, bf16[512,512]{1,0:T(8,128)(2,1)}, u32[]{:S(2)}, u32[]{:S(2)}) collective-permute-start(bf16[512,512]{1,0:T(8,128)(2,1)} %slice_bitcast_fusion), channel_id=1, source_target_pairs={{0,2},{2,0},{1,3},{3,1},{4,6},{6,4},{5,7},{7,5},{8,10},{10,8},{9,1... | collective-permute-start | bytes 1572872 | tf_op jit(solution)/shard_map/ppermute | solution.py:21
  213.7 32.1 %copy-start.10 = (bf16[8,128,512]{2,1,0:T(8,128)(2,1)}, bf16[8,128,512]{2,1,0:T(8,128)(2,1)S(1)}, u32[]{:S(2)}) copy-start(bf16[8,128,512]{2,1,0:T(8,128)(2,1)S(1)} %all-to-all-done.7.res_b) | copy-start | bytes 3145732
  213.7 40.3 %all-to-all-start.6 = ((bf16[8,144,512]{2,1,0:T(8,128)(2,1)}), bf16[8,144,512]{2,1,0:T(8,128)(2,1)}, u32[]{:S(2)}, u32[]{:S(2)}) async-start(bf16[8,144,512]{2,1,0:T(8,128)(2,1)} %get-tuple-element.135), calls=%async_computation.6 | async-start | bytes 2359296 | tf_op jit(solution)/shard_map/all_to_all | solution.py:25
  248.5 3.0 collective-permute-start.14
  254.0 4.9 %copy-start.4 = (bf16[2,512,512]{2,1,0:T(8,128)(2,1)S(1)}, bf16[2,512,512]{2,1,0:T(8,128)(2,1)}, u32[]{:S(2)}) copy-start(bf16[2,512,512]{2,1,0:T(8,128)(2,1)} %copy-done.3) | copy-start | bytes 3145732
  254.0 33.4 %all-to-all-start.5 = ((bf16[8,128,512]{2,1,0:T(8,128)(2,1)}), bf16[8,128,512]{2,1,0:T(8,128)(2,1)S(1)}, u32[]{:S(2)}, u32[]{:S(2)}) async-start(bf16[8,128,512]{2,1,0:T(8,128)(2,1)} %bitcast.66), calls=%async_computation.5 | async-start | bytes 2097152 | tf_op jit(solution)/shard_map/all_to_all | solution.py:25
  260.0 27.4 %collective-permute-start.15 = (bf16[512,512]{1,0:T(8,128)(2,1)S(1)}, bf16[512,512]{1,0:T(8,128)(2,1)}, u32[]{:S(2)}, u32[]{:S(2)}) collective-permute-start(bf16[512,512]{1,0:T(8,128)(2,1)S(1)} %bitcast_select_fusion.3), channel_id=1, source_target_pairs={{0,16},{16,0},{1,17},{17,1},{2,18},{18,2},{3,19},{19,3},{4,20},{20... | collective-permute-start | bytes 1572872 | tf_op jit(solution)/shard_map/ppermute | solution.py:21
  288.3 6.0 %collective-permute-start.16 = (bf16[128,512]{1,0:T(8,128)(2,1)S(1)}, bf16[128,512]{1,0:T(8,128)(2,1)S(1)}, u32[]{:S(2)}, u32[]{:S(2)}) collective-permute-start(bf16[128,512]{1,0:T(8,128)(2,1)S(1)} %convert_element_type.81), channel_id=1, source_target_pairs={{0,16},{16,0},{1,17},{17,1},{2,18},{18,2},{3,19},{19,3},{4,20},{20... | collective-permute-start | bytes 393224 | tf_op jit(solution)/shard_map/ppermute | solution.py:21
  289.2 10.3 %all-to-all-start.9 = ((f32[8,12,512]{2,1,0:T(8,128)}), f32[8,12,512]{2,1,0:T(8,128)S(1)}, u32[]{:S(2)}, u32[]{:S(2)}) async-start(f32[8,12,512]{2,1,0:T(8,128)} %broadcast_in_dim.13), calls=%async_computation.9 | async-start | bytes 524288 | tf_op jit(solution)/shard_map/all_to_all | solution.py:25
  300.5 31.6 %all-to-all-start.8 = ((bf16[8,128,512]{2,1,0:T(8,128)(2,1)}), bf16[8,128,512]{2,1,0:T(8,128)(2,1)S(1)}, u32[]{:S(2)}, u32[]{:S(2)}) async-start(bf16[8,128,512]{2,1,0:T(8,128)(2,1)} %broadcast_in_dim.12), calls=%async_computation.8 | async-start | bytes 2097152 | tf_op jit(solution)/shard_map/all_to_all | solution.py:25
  306.0 26.2 %collective-permute-start.17 = (bf16[512,512]{1,0:T(8,128)(2,1)}, bf16[512,512]{1,0:T(8,128)(2,1)}, u32[]{:S(2)}, u32[]{:S(2)}) collective-permute-start(bf16[512,512]{1,0:T(8,128)(2,1)} %bitcast_select_fusion.1), channel_id=1, source_target_pairs={{0,16},{16,0},{1,17},{17,1},{2,18},{18,2},{3,19},{19,3},{4,20},{20... | collective-permute-start | bytes 1572872 | tf_op jit(solution)/shard_map/ppermute | solution.py:21
  308.9 22.1 %collective-permute-start.18 = (f32[12,512]{1,0:T(8,128)S(1)}, f32[12,512]{1,0:T(8,128)S(1)}, u32[]{:S(2)}, u32[]{:S(2)}) collective-permute-start(f32[12,512]{1,0:T(8,128)S(1)} %reduce_sum.19), channel_id=1, source_target_pairs={{0,16},{16,0},{1,17},{17,1},{2,18},{18,2},{3,19},{19,3},{4,20},{20... | collective-permute-start | bytes 73736 | tf_op jit(solution)/shard_map/ppermute | solution.py:21
  331.0 1.2 collective-permute-start.19
  332.2 5.9 %collective-permute-start.20 = (bf16[1,1024,512]{2,1,0:T(8,128)(2,1)S(1)}, bf16[1,1024,512]{2,1,0:T(8,128)(2,1)}, u32[]{:S(2)}, u32[]{:S(2)}) collective-permute-start(bf16[1,1024,512]{2,1,0:T(8,128)(2,1)S(1)} %bitcast.64), channel_id=1, source_target_pairs={{0,1},{1,0},{2,3},{3,2},{4,5},{5,4},{6,7},{7,6},{8,9},{9,8},{10,11... | collective-permute-start | bytes 3145736 | tf_op jit(solution)/shard_map/ppermute | solution.py:21
  (7 other events, 8.0 us)

commit v3 on v2

--- a/solution.py
+++ b/solution.py
@@ -70,14 +70,16 @@
 
 
 def cumulative(value):
-    size = jnp.abs(value)
-    base = 1.0 + 0.23164188 * size
-    guess = pl.reciprocal(base, approx=True)
-    t = guess * (2.0 - base * guess)
-    bell = jnp.exp(-0.5 * value * value)
-    poly = t * (0.127414796 + t * (-0.142248368 + t * (0.7107068705 + t * (-0.7265760135 + t * 0.5307027145))))
+    t = pl.reciprocal(1.0 + 0.23164188 * jnp.abs(value), approx=True)
+    bell = jnp.exp2(value * (value * -0.7213475204444817) - 1.3257480647361593)
+    poly = t * (0.31938153 + t * (-0.356563782 + t * (1.781477937 + t * (-1.821255978 + t * 1.330274429))))
     tail = poly * bell
-    return jnp.where(value >= 0.0, 1.0 - tail, tail), bell * 0.3989422804014327
+    return jnp.where(value >= 0.0, 1.0 - tail, tail), bell
+
+
+def served(place, experts):
+    top = experts // 2
+    return place ^ ((place & (top // 2)) * 2)
 
 
 def dispatch(targets, data, start, count):
@@ -126,7 +128,7 @@
 
     lax.fori_loop(0, rows // step, compare, 0)
     label = iota((2 * experts, rows), 0)
-    tops = [top_ref[0:1, :], top_ref[1:2, :]]
+    tops = [served(top_ref[j : j + 1, :], experts) for j in range(TOPK)]
     hot = ((label == tops[0]) | (label == tops[1] + experts)) & present
     hot = jnp.where(hot, 1.0, 0.0)
     counts = dot(hot.astype(BF), early_ref[...])
@@ -146,23 +148,24 @@
     targets = targets.astype(jnp.int32)
     row_ref[...] = targets
     for e in range(experts):
-        send_ref[e] = dispatch(targets, cot_ref[...], e * stride, stride).astype(BF)
+        send_ref[e] = dispatch(targets, cot_ref[...], e * stride, send_ref.shape[1]).astype(BF)
 
 
 def put_rows(ref, e, block, column):
     count, width = block.shape
     eye = iota((count, width), 0) == iota((count, width), 1)
     high, low = high_low(jnp.sum(jnp.where(eye, column, 0.0), axis=0, keepdims=True))
-    ref[e, 0 : count - 16, :] = block[0 : count - 16].astype(BF)
+    ref[e, 0 : count - 16, 0:width] = block[0 : count - 16].astype(BF)
     tail = iota((16, width), 0)
     last = block[count - 16 :]
     last = jnp.where(tail == 14, high.astype(F32), jnp.where(tail == 15, low.astype(F32), last))
-    ref[e, count - 16 :, :] = last.astype(BF)
-
-
-def get_column(ref, e):
-    count, width = ref.shape[1:]
-    last = jnp.where(iota((16, width), 0) >= 14, ref[e, count - 16 :, :].astype(F32), 0.0)
+    ref[e, count - 16 :, 0:width] = last.astype(BF)
+
+
+def get_column(ref, e, width):
+    count = ref.shape[1]
+    last = ref[e, count - 16 :, 0:width].astype(F32)
+    last = jnp.where(iota((16, width), 0) >= 14, last, 0.0)
     eye = iota((count, width), 0) == iota((count, width), 1)
     return jnp.sum(jnp.where(eye, jnp.sum(last, axis=0, keepdims=True), 0.0), axis=1, keepdims=True)
 
@@ -183,7 +186,7 @@
 
 
 def forward_kernel(
-    len_ref, image_ref, gain_one, shift_one, wq_ref, wk_ref, wv_ref, wo_ref, gain_two, shift_two,
+    len_ref, image_ref, cot_ref, gain_one, shift_one, wq_ref, wk_ref, wv_ref, wo_ref, gain_two, shift_two,
     router_ref, row_ref, normed_ref, q_ref, k_ref, v_ref, prob_ref, mixed_ref, residual_ref, two_ref,
     soft_ref, send_a, send_b, side_ref, *, experts, stride, patches, group,
 ):
@@ -253,58 +256,61 @@
             hot = jnp.where(hit, 1.0, 0.0).astype(BF)
             side = dot(hot, side_ref[...])
             side = side[:, 0:128] + side[:, 128:256]
-            gate = jnp.sum(jnp.where(iota(side.shape, 1) == e, side, 0.0), axis=1, keepdims=True)
+            gate = jnp.sum(jnp.where(iota(side.shape, 1) == served(e, experts), side, 0.0), axis=1, keepdims=True)
             put_rows(send_ref, e, dot(hot, two_ref[...]), gate)
+            if begin:
+                send_ref[e, :, width:] = dot(hot, cot_ref[...]).astype(BF)
         begin += count
 
 
-def expert_kernel(x_ref, cot_ref, *refs, begin):
-    weights, (res_ref, back_ref, act_ref, pre_ref, grad_ref) = refs[:-5], refs[-5:]
-    pieces = len(weights) // 2
-    chunks, count, width = x_ref.shape
-    units = weights[0].shape[1]
-    gates = [get_column(x_ref, c) for c in range(chunks)]
-    gate = jnp.concatenate(gates)
+def expert_kernel(x_ref, *refs, begin):
+    first_ref, weights, outs = refs[0], refs[1:-5], refs[-5:]
+    back_ref, res_ref, act_ref, pre_ref, grad_ref = outs
+    chunks, count, width = back_ref.shape
+    if begin:
+        x_ref, cot_ref = x_ref.at[:, :, 0:width], x_ref.at[:, :, width:]
+        res_ref[:, 0:begin, :] = first_ref[...]
+    else:
+        cot_ref = first_ref
+    units = weights[0].shape[0] // 2
+    gate = jnp.concatenate([get_column(x_ref, c, width) for c in range(chunks)])
     x = x_ref[...].reshape(chunks * count, width)
-    cot = cot_ref[:, begin : begin + count, :].reshape(chunks * count, width).astype(F32)
+    cot = cot_ref[...].reshape(chunks * count, width).astype(F32)
     grad = (gate * cot).astype(BF)
     grad_ref[...] = grad.reshape(chunks, count, width)
-    result = jnp.zeros((chunks * count, width), F32)
-    back = jnp.zeros((chunks * count, width), F32)
-    for s in range(pieces):
+    for s, weight in enumerate(weights):
         cols = pl.ds(s * units, units)
-        first, second = weights[s], weights[pieces + s]
-        hidden = dot(x, first[...])
+        hidden = dot_nt(x, weight[0:units, :])
         below, bell = cumulative(hidden)
-        act = (hidden * below).astype(BF)
-        act_ref[:, :, cols] = act.reshape(chunks, count, units)
-        result = result + dot(act, second[...])
-        pre = (dot_nt(grad, second[...]) * (below + hidden * bell)).astype(BF)
+        act_ref[:, :, cols] = (hidden * below).astype(BF).reshape(chunks, count, units)
+        pre = (dot_nt(grad, weight[units:, :]) * (below + hidden * bell)).astype(BF)
         pre_ref[:, :, cols] = pre.reshape(chunks, count, units)
-        back = back + dot_nt(pre, first[...])
-    res_ref[...] = (gate * result).astype(BF).reshape(chunks, count, width)
+    act = act_ref[...].reshape(chunks * count, -1)
+    pre = pre_ref[...].reshape(chunks * count, -1)
+    result = dot(act, jnp.concatenate([w[units:, :] for w in weights]))
+    back = dot(pre, jnp.concatenate([w[0:units, :] for w in weights]))
+    res_ref[:, begin : begin + count, :] = (gate * result).astype(BF).reshape(chunks, count, width)
     along = jnp.sum(cot * result, axis=1, keepdims=True)
     for c in range(chunks):
         here = slice(c * count, (c + 1) * count)
         put_rows(back_ref, c, back[here], along[here])
 
 
-def expert_grad_kernel(
-    x_a, x_b, pre_a, pre_b, act_a, act_b, grad_a, grad_b, in_near, in_far, out_near, out_far
-):
+def expert_grad_kernel(x_a, x_b, pre_a, pre_b, act_a, act_b, grad_a, grad_b, near_ref, far_in, far_out):
+    units = pre_a.shape[1]
     near = pl.program_id(0) < pl.num_programs(0) // 2
-    grad_in = (dot_tn(x_a[...], pre_a[...]) + dot_tn(x_b[...], pre_b[...])).astype(BF)
+    grad_in = (dot_tn(pre_a[...], x_a[...]) + dot_tn(pre_b[...], x_b[...])).astype(BF)
     grad_out = (dot_tn(act_a[...], grad_a[...]) + dot_tn(act_b[...], grad_b[...])).astype(BF)
 
     @pl.when(near)
     def _():
-        in_near[0] = grad_in
-        out_near[0] = grad_out
+        near_ref[0, 0:units, :] = grad_in
+        near_ref[0, units:, :] = grad_out
 
     @pl.when(jnp.logical_not(near))
     def _():
-        in_far[0] = grad_in
-        out_far[0] = grad_out
+        far_in[0] = grad_in
+        far_out[0] = grad_out
 
 
 def hot_of(col_ref, here, slots):
@@ -314,15 +320,12 @@
     return jnp.where(hit, 1.0, 0.0).astype(BF)
 
 
-def backward_kernel(*refs, experts, stride, patches, group):
-    (back_a, back_b, col_ref, soft_ref, residual_ref, cot_ref, two_ref, mixed_ref, normed_ref, q_ref, k_ref, v_ref, prob_ref,
-     gain_two, router_ref, wo_ref,
-     resid_ref, gq_ref, gk_ref, gv_ref, wg_out_ref, wg_q_ref, wg_k_ref, wg_v_ref, wg_router_ref, small_ref,
-     slots_ref, attn_ref, gm_ref, logit_ref) = refs
+def combine_kernel(
+    back_a, back_b, col_ref, soft_ref, residual_ref, cot_ref, two_ref, mixed_ref, gain_two, router_ref, wo_ref,
+    resid_ref, gm_ref, wg_out_ref, wg_router_ref, small_ref, slots_ref, attn_ref, logit_ref, *, experts, stride,
+):
     rows, width = cot_ref.shape
-    size = width // HEADS
-    lanes = group * size
-    step = 144
+    step = row_block(rows)
     slots = experts * stride
     for e in range(experts):
         base = e * stride
@@ -330,9 +333,9 @@
             here = slice(base, base + back_ref.shape[1])
             base += back_ref.shape[1]
             slots_ref[here, 0:width] = back_ref[e]
-            along = get_column(back_ref, e)
+            along = get_column(back_ref, e, width)
             label = iota((along.shape[0], 128), 1)
-            high, low = high_low(jnp.where(label == e, along, 0.0))
+            high, low = high_low(jnp.where(label == served(e, experts), along, 0.0))
             slots_ref[here, width : width + 128] = high
             slots_ref[here, width + 128 : width + 256] = low
 
@@ -364,6 +367,15 @@
     wg_router_ref[...] = dot_tn(logit_ref[...], two_ref[...])
     wg_out_ref[...] = dot_tn(mixed_ref[...], attn_ref[...]).astype(BF)
 
+
+def attention_back_kernel(
+    side_ref, gm_ref, normed_ref, q_ref, k_ref, v_ref, prob_ref, wo_ref, gq_ref, gk_ref, gv_ref, near_ref, far_one, far_two,
+    *, patches, group,
+):
+    rows, width = gm_ref.shape
+    size = width // HEADS
+    lanes = group * size
+
     def attend(image, carry):
         here = pl.ds(pl.multiple_of(image * patches, 16), patches)
         for g in range(HEADS // group):
@@ -382,26 +394,34 @@
         return carry
 
     lax.fori_loop(0, rows // patches, attend, 0)
-    wg_q_ref[...] = dot_tn(normed_ref[...], gq_ref[...]).astype(BF)
-    wg_k_ref[...] = dot_tn(normed_ref[...], gk_ref[...]).astype(BF)
-    wg_v_ref[...] = dot_tn(normed_ref[...], gv_ref[...]).astype(BF)
-
-
-def output_kernel(col_ref, residual_ref, res_a, res_b, out_ref, slots_ref):
-    step = 144
-    base = 0
-    for e in range(res_a.shape[0]):
-        for res_ref in (res_a, res_b):
-            slots_ref[base : base + res_ref.shape[1], :] = res_ref[e]
-            base += res_ref.shape[1]
+    upper = side_ref[0] == 1
+    lower = jnp.logical_not(upper)
+
+    def put(n, value):
+        @pl.when(upper if n // 2 else lower)
+        def _():
+            near_ref[n % 2] = value
+
+        @pl.when(lower if n // 2 else upper)
+        def _():
+            (far_one, far_two)[n % 2][...] = value
+
+    put(0, wo_ref[...])
+    for n, grad_ref in enumerate((gq_ref, gk_ref, gv_ref)):
+        put(n + 1, dot_tn(normed_ref[...], grad_ref[...]).astype(BF))
+
+
+def output_kernel(col_ref, residual_ref, res_ref, out_ref):
+    rows = residual_ref.shape[0]
+    step = row_block(rows)
 
     def combine(block, carry):
         here = pl.ds(pl.multiple_of(block * step, 16), step)
-        moe = dot(hot_of(col_ref, here, slots_ref.shape[0]), slots_ref[...])
+        moe = dot(hot_of(col_ref, here, res_ref.shape[0]), res_ref[...])
         out_ref[here, :] = (residual_ref[here, :] + moe).astype(BF)
         return carry
 
-    lax.fori_loop(0, residual_ref.shape[0] // step, combine, 0)
+    lax.fori_loop(0, rows // step, combine, 0)
 
 
 def image_kernel(gq_ref, gk_ref, gv_ref, wq_ref, wk_ref, wv_ref, image_ref, resid_ref, gain_one, out_ref, small_ref):
@@ -426,7 +446,23 @@
     small_ref[...] = jnp.where(which == 0, gain_sum, jnp.where(which == 1, shift_sum, 0.0))
 
 
-COST = pl.CostEstimate(flops=0, bytes_accessed=0, transcendentals=0)
+LENGTH = {
+    "route": 7,
+    "forward": 19,
+    "expert": 21,
+    "expert_grad": 16,
+    "combine": 17,
+    "attention_back": 1,
+    "output": 1,
+    "image": 1,
+}
+
+
+def cost(name):
+    length = LENGTH[name]
+    return pl.CostEstimate(flops=int(length * 1.1e9), bytes_accessed=int(length * 3.4e6), transcendentals=0)
+
+
 SCALAR = pl.BlockSpec(memory_space=pltpu.SMEM)
 VECTOR = pl.BlockSpec(memory_space=pltpu.VMEM)
 
@@ -439,24 +475,29 @@
         out_specs=[VECTOR] * len(outs),
         scratch_shapes=scratch,
         compiler_params=pltpu.CompilerParams(vmem_limit_bytes=56 << 20),
-        cost_estimate=COST,
+        cost_estimate=cost(kernel.__name__.removesuffix("_kernel")),
+        name=kernel.__name__,
     )(*args)
 
 
 def make_on_device(experts, hidden):
-    group = ("hh", "el")
-    half_e, half_h = experts // 2, hidden // 2
+    group = ("hh", "em", "el")
+    half_h = hidden // 2
+    places = [(eh, em, hh) for eh in range(2) for em in range(2) for hh in range(2)]
+
+    def step(value, home, eh, hh):
+        pairs = [
+            (places.index(p), places.index((p[0] ^ eh, p[1], p[2] ^ hh)))
+            for p in places
+            if (p[0] == p[1] ^ p[2]) == home
+        ]
+        return lax.ppermute(value, ("eh", "em", "hh"), pairs)
+
+    def over_hh(value):
+        return swap(value, "hh", 2, 1)
 
     def over_eh(value):
         return swap(value, "eh", 2, 1)
-
-    def moves(own):
-        axes = ("eh", "hh")
-        paths = ([(0, 2), (3, 1)], [(1, 0), (2, 3)], [(1, 2), (2, 1)])
-        return [lax.ppermute(own, axes, pairs) for pairs in paths]
-
-    def over_hh(value):
-        return swap(value, "hh", 2, 1)
 
     def fold_hl(parts):
         for bit in reversed(range(half_h.bit_length() - 2)):
@@ -465,9 +506,9 @@
             parts = (parts[:count].astype(F32) + far.astype(F32)).astype(BF)
         return parts
 
-    def gather_hl(parts):
+    def gather_hl(parts, count):
         index = lax.axis_index("hl")
-        for bit in range(half_h.bit_length() - 1):
+        for bit in range(count.bit_length() - 1):
             far = swap(parts, "hl", half_h, 1 << bit)
             odd = ((index >> bit) & 1) == 1
             parts = jnp.where(odd, jnp.concatenate([far, parts]), jnp.concatenate([parts, far]))
@@ -475,7 +516,7 @@
 
     def scatter_hl(parts):
         index = lax.axis_index("hl")
-        for bit in reversed(range(half_h.bit_length() - 1)):
+        for bit in reversed(range(parts.shape[0].bit_length() - 1)):
             pairs = parts.reshape((2, -1) + parts.shape[1:])
             odd = (index >> bit) & 1
             keep = lax.dynamic_index_in_dim(pairs, odd, 0, keepdims=False)
@@ -509,24 +550,23 @@
         hidden_all = units * hidden
         capacity = (21 * rows * TOPK + 20 * experts - 1) // (20 * experts)
         stride = (capacity + 4 + 15) // 16 * 16
-        count_a = (stride // 2 + 15) // 16 * 16
+        count_a = stride // 2 // 16 * 16
         slots = experts * stride
         hh = lax.axis_index("hh")
-        same = lax.axis_index("eh") == hh
-
-        block = ((experts, stride, width), BF)
+        home = lax.axis_index("eh") == hh ^ lax.axis_index("em")
+
         block_a = ((experts, count_a, width), BF)
-        block_b = ((experts, stride - count_a, width), BF)
+        block_b = ((experts, stride - count_a, 2 * width), BF)
         token_low = ((rows, width), BF)
         token_wide = ((rows, width), F32)
 
-        own_in, own_out = w_expert_in[0], w_expert_out[0]
-        moved_in, moved_out = moves(own_in), moves(own_out)
+        own = jnp.concatenate([w_expert_in[0].T, w_expert_out[0]])
+        moved = [step(own, True, 1, 0), step(own, False, 0, 1), step(own, False, 1, 1)]
 
         cot = out_grad.reshape(rows, width)
-        column, row, cot_send = call(
+        column, row, cot_a = call(
             route_kernel,
-            [((rows, 128), I32), ((8, rows), I32), block],
+            [((rows, 128), I32), ((8, rows), I32), block_a],
             [lengths, priority, top_experts.reshape(rows, TOPK).T, cot],
             scalars=1,
             scratch=[pltpu.VMEM((rows, 128), F32), pltpu.VMEM((rows, rows), BF)],
@@ -536,7 +576,7 @@
             stride=stride,
             patches=patches,
         )
-        cot_in = to_all(cot_send, group)
+        cot_a = to_all(cot_a, group)
 
         gain_one, shift_one, gain_two, shift_two = (
             v.reshape(1, width) for v in (first_gain, first_shift, second_gain, second_shift)
@@ -548,7 +588,7 @@
             [token_low] * 4
             + [((image_count, HEADS // GROUP, patches, GROUP * patches), BF), token_low, token_wide]
             + [token_low, ((rows, 128), F32), block_a, block_b],
-            [lengths, tokens, gain_one, shift_one, w_query, w_key, w_value, w_output]
+            [lengths, tokens, cot, gain_one, shift_one, w_query, w_key, w_value, w_output]
             + [gain_two, shift_two, router, row],
             scalars=1,
             scratch=[pltpu.VMEM((rows, 256), BF)],
@@ -558,42 +598,43 @@
             group=GROUP,
         )
 
-        send_a, cot_in = together(send_a, cot_in)
+        send_a, cot_a, moved = together(send_a, cot_a, moved)
         x_a = to_all(send_a, group)
-        send_b, moved_in, moved_out = together(send_b, moved_in, moved_out)
+        send_b, moved = together(send_b, moved)
         x_b = to_all(send_b, group)
 
-        def pieces_of(own, moved):
-            by_eh, by_hh, by_both = moved
-            pieces = [jnp.where(same, own, by_eh), jnp.where(same, by_hh, by_both)]
-            for bit in range(half_h.bit_length() - 1):
-                pieces = pieces + [swap(p, "hl", half_h, 1 << bit) for p in pieces]
-            return pieces
-
-        weights = pieces_of(own_in, moved_in) + pieces_of(own_out, moved_out)
-
-        def serve(x, begin):
-            count = x.shape[1]
+        by_eh, by_hh, by_both = moved
+        weights = [jnp.where(home, own, by_eh), jnp.where(home, by_hh, by_both)]
+        for bit in range(half_h.bit_length() - 1):
+            weights = weights + [swap(w, "hl", half_h, 1 << bit) for w in weights]
+
+        def serve(begin, *arrays):
+            count = arrays[0].shape[1]
 
             def spec(rows_here, lanes):
                 return pl.BlockSpec((2, rows_here, lanes), lambda i: (i, 0, 0))
 
-            lanes_out = (width, width, hidden_all, hidden_all, width)
+            outs = [(count, n) for n in (width, width, hidden_all, hidden_all, width)]
+            outs[1] = (begin + count, width)
             return pl.pallas_call(
                 functools.partial(expert_kernel, begin=begin),
                 grid=(experts // 2,),
-                out_shape=[jax.ShapeDtypeStruct((experts, count, n), BF) for n in lanes_out],
-                in_specs=[spec(count, width), spec(stride, width)]
+                out_shape=[jax.ShapeDtypeStruct((experts,) + o, BF) for o in outs],
+                in_specs=[spec(*a.shape[1:]) for a in arrays]
                 + [pl.BlockSpec(w.shape, lambda i: (0, 0)) for w in weights],
-                out_specs=[spec(count, n) for n in lanes_out],
+                out_specs=[spec(*o) for o in outs],
                 compiler_params=pltpu.CompilerParams(vmem_limit_bytes=56 << 20),
-                cost_estimate=COST,
-            )(x, cot_in, *weights)
-
-        result_a, back_a, act_a, pre_a, grad_a = serve(x_a, 0)
+                cost_estimate=cost("expert"),
+                name="expert_kernel",
+            )(*arrays, *weights)
+
+        back_a, result, act_a, pre_a, grad_a = serve(0, x_a, cot_a)
         back_a = to_all(back_a, group)
-        result_b, back_b, act_b, pre_b, grad_b = serve(x_b, count_a)
+        back_b, result, act_b, pre_b, grad_b = serve(count_a, x_b, result)
+        back_a, back_b = together(back_a, back_b)
         back_b = to_all(back_b, group)
+        back_b, result = together(back_b, result)
+        result = to_all(result, group)
 
         half = hidden // 2
 
@@ -608,62 +649,51 @@
 
         pairs = [x_a, x_b, pre_a, pre_b, act_a, act_b, grad_a, grad_b]
         pairs = [rows_of(p) for p in pairs]
-        full = [pl.BlockSpec(p.shape, lambda f: (0, 0)) for p in pairs[:2]]
+        full = [pl.BlockSpec((p.shape[0], width), lambda f: (0, 0)) for p in pairs[:2]]
         part = [pl.BlockSpec((p.shape[0], units), lambda f: (0, f)) for p in pairs[:2]]
-        in_near, in_far, out_near, out_far = pl.pallas_call(
+        grads_near, *grads_far = pl.pallas_call(
             expert_grad_kernel,
             grid=(hidden,),
-            out_shape=[jax.ShapeDtypeStruct((half, width, units), BF)] * 2
-            + [jax.ShapeDtypeStruct((half, units, width), BF)] * 2,
+            out_shape=[jax.ShapeDtypeStruct((half, n, width), BF) for n in (2 * units, units, units)],
             in_specs=full + part + part + full,
-            out_specs=[pl.BlockSpec((1, width, units), near), pl.BlockSpec((1, width, units), far)]
-            + [pl.BlockSpec((1, units, width), near), pl.BlockSpec((1, units, width), far)],
+            out_specs=[pl.BlockSpec((1, 2 * units, width), near)] + [pl.BlockSpec((1, units, width), far)] * 2,
             compiler_params=pltpu.CompilerParams(vmem_limit_bytes=56 << 20),
-            cost_estimate=COST,
+            cost_estimate=cost("expert_grad"),
+            name="expert_grad_kernel",
         )(*pairs)
 
-        def fold_far(near_parts, far_parts):
-            came = swap(far_parts, "hl", half_h, half_h // 2)
-            return fold_hl((near_parts.astype(F32) + came.astype(F32)).astype(BF))
-
-        parts_in, parts_out = fold_far(in_near, in_far), fold_far(out_near, out_far)
-        result_a, result_b, back_a, back_b, parts_in, parts_out = together(
-            result_a, result_b, back_a, back_b, parts_in, parts_out
-        )
-        result_a, result_b = to_all(result_a, group), to_all(result_b, group)
-        came_in, came_out = over_hh(parts_in[1]), over_hh(parts_out[1])
-
-        resid, gq, gk, gv, wg_out, wg_q, wg_k, wg_v, wg_router, small_two = call(
-            backward_kernel,
-            [token_wide] + [token_low] * 3 + [((width, width), BF)] * 4
-            + [((128, width), F32), ((8, width), F32)],
-            [back_a, back_b, column, soft, residual, cot, two, mixed, normed, queries, keys, values, probs]
-            + [gain_two, router, w_output],
+        came = [swap(g, "hl", half_h, half_h // 2) for g in grads_far]
+        came = jnp.concatenate(came, axis=1)
+        parts = fold_hl((grads_near.astype(F32) + came.astype(F32)).astype(BF))
+        passed = over_hh(parts[1])
+        mine, theirs = jnp.where(home, parts[0], passed), jnp.where(home, passed, parts[0])
+
+        resid, grad_mixed, wg_out, wg_router, small_two = call(
+            combine_kernel,
+            [token_wide, token_low, ((width, width), BF), ((128, width), F32), ((8, width), F32)],
+            [back_a, back_b, column, soft, residual, cot, two, mixed, gain_two, router, w_output],
             scratch=[
                 pltpu.VMEM((slots, width + 256), BF),
-                pltpu.VMEM((rows, width), BF),
                 pltpu.VMEM((rows, width), BF),
                 pltpu.VMEM((rows, 128), BF),
             ],
             experts=experts,
             stride=stride,
+        )
+        side = (lax.axis_index("hl") // (half_h // 2)).reshape(1)
+        gq, gk, gv, wg_near, *wg_far = call(
+            attention_back_kernel,
+            [token_low] * 3 + [((2, width, width), BF)] + [((width, width), BF)] * 2,
+            [side, grad_mixed, normed, queries, keys, values, probs, wg_out],
+            scalars=1,
             patches=patches,
             group=GROUP,
         )
 
-        wg_out, wg_q, wg_k, wg_v, gq, came_in, came_out = together(
-            wg_out, wg_q, wg_k, wg_v, gq, came_in, came_out
-        )
-
-        def finish_sum(keep, came):
-            return jnp.where(same, keep, came), over_eh(jnp.where(same, came, keep))
-
-        mine_in, far_in = finish_sum(parts_in[0], came_in)
         (block_out,) = call(
             output_kernel,
             [token_low],
-            [column, residual, result_a, result_b],
-            scratch=[pltpu.VMEM((slots, width), BF)],
+            [column, residual, result.reshape(slots, width)],
         )
         grad_images, small_one = call(
             image_kernel,
@@ -671,35 +701,37 @@
             [gq, gk, gv, w_query, w_key, w_value, tokens, resid, gain_one],
         )
 
-        stacked = jnp.concatenate([wg_out, wg_q, wg_k, wg_v])
-        pieces = scatter_hl(stacked.reshape(half_h, -1, width))
+        came = jnp.stack([swap(w, "hl", half_h, half_h // 2) for w in wg_far])
+        pieces = (wg_near.astype(F32) + came.astype(F32)).astype(BF)
+        pieces = scatter_hl(pieces.reshape(half_h // 2, -1, width))
+        pieces, theirs = together(pieces, theirs)
         pieces = to_all(pieces.reshape(experts, -1, width), group)
-        pieces, far_in, came_out, block_out, small_one = together(
-            pieces, far_in, came_out, block_out, small_one
-        )
-        mine_out, far_out = finish_sum(parts_out[0], came_out)
+        far_in = over_eh(theirs[:units])
+        pieces, far_in, theirs, block_out, grad_images = together(pieces, far_in, theirs, block_out, grad_images)
+        far_out = over_eh(theirs[units:])
         piece = jnp.sum(pieces.astype(F32), axis=0)
         piece = (piece + over_eh(piece.astype(BF)).astype(F32)).astype(BF)
         pieces = to_all(jnp.broadcast_to(piece, (experts,) + piece.shape), group)
+        sum_in = (mine[:units].astype(F32) + far_in.astype(F32)).T
+        sum_out = mine[units:].astype(F32) + far_out.astype(F32)
         small = jnp.concatenate([small_one[:2], small_two[:2], wg_router[:experts]])
-        small = jnp.sum(to_all(jnp.broadcast_to(small, (experts,) + small.shape), group), axis=0)
-        small = small + over_eh(small)
-        for bit in range(half_h.bit_length() - 1):
-            small = small + swap(small, "hl", half_h, 1 << bit)
-        pieces, far_out, small = together(pieces, far_out, small)
-        total = gather_hl(pieces.reshape(1, -1, width)).reshape(stacked.shape).astype(F32)
-        sum_output, sum_query, sum_key, sum_value = jnp.split(total, 4)
-        sum_in = mine_in.astype(F32) + far_in.astype(F32)
-        sum_out = mine_out.astype(F32) + far_out.astype(F32)
+        for axis, size in (("hl", half_h), ("el", experts // 4), ("hh", 2), ("em", 2), ("eh", 2)):
+            for bit in range(size.bit_length() - 1):
+                small = small + swap(small, axis, size, 1 << bit)
+        pieces, small, sum_in, sum_out = together(pieces, small, sum_in, sum_out)
+        pieces = gather_hl(pieces.reshape(1, -1, width), half_h // 2)
+        came = swap(pieces, "hl", half_h, half_h // 2)
+        lower = jnp.where(side[0] == 0, pieces, came).reshape(2, width, width).astype(F32)
+        upper = jnp.where(side[0] == 0, came, pieces).reshape(2, width, width).astype(F32)
         return (
             block_out.reshape(images.shape),
             grad_images.reshape(images.shape),
             small[0],
             small[1],
-            sum_query,
-            sum_key,
-            sum_value,
-            sum_output,
+            lower[1],
+            upper[0],
+            upper[1],
+            lower[0],
             small[2],
             small[3],
             small[4:].T,
@@ -712,10 +744,10 @@
 
 def solution(mesh):
     experts, hidden = mesh.shape["expert"], mesh.shape["hidden"]
-    names = ("eh", "el", "hh", "hl")
-    places = mesh.devices.reshape(2, experts // 2, 2, hidden // 2)
+    names = ("eh", "em", "el", "hh", "hl")
+    places = mesh.devices.reshape(2, 2, experts // 4, 2, hidden // 2)
     tokens = (P(names, None, None), P(names), P(names, None), P(names, None, None), P(names, None, None))
-    weights = (P(("eh", "el"), None, ("hh", "hl")), P(("eh", "el"), ("hh", "hl"), None))
+    weights = (P(names[:3], None, names[3:]), P(names[:3], names[3:], None))
     return jax.shard_map(
         make_on_device(experts, hidden),
         mesh=jax.sharding.Mesh(places, names),

time: 344 us -> 303 us (0.88)
  waiting for transfers between devices: 100 us -> 83.6 us
  starting transfers between devices: 79 us -> 69.6 us
  other arithmetic: 19.8 us -> 13 us
  Pallas kernels: 128 us -> 122 us
    ppermute x6 -> x3, waiting for transfers between devices: 24.1 us -> 0.01 us  [step(): return lax.ppermute(value, ('eh', 'em', 'hh'), pairs)]
    ppermute x15 -> x16, starting transfers between devices: 7.12 us -> 20.4 us  [swap(): return lax.ppermute(value, axis, [(i, i ^ flip) for i in range(size)])]
    all_to_all x10 -> x8, starting transfers between devices: 52.9 us -> 40.3 us  [to_all(): return lax.all_to_all(blocks, axes, split_axis=0, concat_axis=0, tiled=True)]
    ppermute x6 -> x3, starting transfers between devices: 19 us -> 8.94 us  [step(): return lax.ppermute(value, ('eh', 'em', 'hh'), pairs)]
    all_to_all x10 -> x8, waiting for transfers between devices: 33.6 us -> 39.6 us  [to_all(): return lax.all_to_all(blocks, axes, split_axis=0, concat_axis=0, tiled=True)]
    pallas_call x2, Pallas kernels: 42.8 us -> 37 us  [serve(): pl.pallas_call(functools.partial(expert_kernel, begin=begin), grid=(exper...]
    select_n x7 -> x3, other arithmetic: 7.53 us -> 2.8 us  [the longest x2 1.69 us: on_device(): weights = [jnp.where(home, own, by_eh), jnp.where(home, by_hh, by_both)]]
    broadcast_in_dim x2 -> x0, other arithmetic: 4.42 us -> none  [the longest x1 2.21 us: on_device(): sum_in[None]]
  transfers between devices with their start and end apart: 31 -> 27, of which waited for: 13 -> 15; matrix products, arithmetic and copies ran while one was open for 7% -> 5% of each run, Pallas kernels for 35% -> 40%
where the time goes in v3:
time: 303 us; the launch traced here: 302 us
  Pallas kernels  122 us (40%)
  waiting for transfers between devices  83.6 us (28%)
  starting transfers between devices  69.6 us (23%)
  other arithmetic  13 us (4%)
  local copies, waits for them, and re-layouts  12.8 us (4%)
    pallas_call x6, Pallas kernels, call(): pl.pallas_call(functools.partial(kernel, **names) if names else kernel, o...  69.1 us
    ppermute x16, waiting for transfers between devices, swap(): return lax.ppermute(value, axis, [(i, i ^ flip) for i in range(size)])  44 us
    all_to_all x8, starting transfers between devices, to_all(): return lax.all_to_all(blocks, axes, split_axis=0, concat_axis=0, tiled=True)  40.3 us
    all_to_all x8, waiting for transfers between devices, to_all(): return lax.all_to_all(blocks, axes, split_axis=0, concat_axis=0, tiled=True)  39.6 us
    pallas_call x2, Pallas kernels, serve(): pl.pallas_call(functools.partial(expert_kernel, begin=begin), grid=(exper...  37 us
    ppermute x16, starting transfers between devices, swap(): return lax.ppermute(value, axis, [(i, i ^ flip) for i in range(size)])  20.4 us
    pallas_call x1, Pallas kernels, on_device(): pl.pallas_call(expert_grad_kernel, grid=(hidden,), out_shape=[jax.ShapeDt...  16.4 us
    ppermute x3, starting transfers between devices, step(): return lax.ppermute(value, ('eh', 'em', 'hh'), pairs)  8.94 us
  transfers between devices with their start and end apart: 27, of which 15 were waited for; matrix products, arithmetic and copies ran while one was open for 5% of the time, Pallas kernels for 40%

profile of v3, /device:TPU:0, one launch (start us, length us, event | category | flops | bytes accessed | tf_op | source)
XLA Modules:
  0.0 302.4 jit_solution(7122491604730122071)
XLA Ops:
  0.7 1.3 copy.35
  1.9 2.1 pad_maximum_fusion
  4.0 6.0 %collective-permute-start = (bf16[1024,512]{1,0:T(8,128)(2,1)}, bf16[1024,512]{1,0:T(8,128)(2,1)S(1)}, u32[]{:S(2)}, u32[]{:S(2)}) collective-permute-start(bf16[1024,512]{1,0:T(8,128)(2,1)} %pad_maximum_fusion), channel_id=1, source_target_pairs={{0,16},{10,26},{18,2},{24,8},{1,17},{11,27},{19,3},{25,9},{4,20},{... | collective-permute-start | bytes 3145736 | tf_op jit(solution)/shard_map/ppermute | solution.py:494
  10.0 1.3 collective-permute-start.1
  11.3 1.7 collective-permute-start.2
  13.6 5.5 %route_kernel.1 = (s32[1008,128]{1,0:T(8,128)}, s32[8,1008]{1,0:T(8,128)}, bf16[8,128,512]{2,1,0:T(8,128)(2,1)}) custom-call(s32[7]{0:T(128)} %len_ref.3, s32[1,1008]{1,0:T(1,128)} %pri_ref.1, s32[2,1008]{1,0:T(2,128)} %bitcast.74, bf16[1008,512]{1,0:T(8,128)(2,1)} %bitcast.82), custom_call_target="tpu_custom_call" | custom-call | flops 7699999744 | bytes 23800000 | tf_op jit(solution)/shard_map/route_kernel/pallas_call | solution.py:471
  19.2 7.6 %all-to-all-start = ((bf16[8,128,512]{2,1,0:T(8,128)(2,1)}), bf16[8,128,512]{2,1,0:T(8,128)(2,1)S(1)}, u32[]{:S(2)}, u32[]{:S(2)}) async-start(bf16[8,128,512]{2,1,0:T(8,128)(2,1)} %get-tuple-element.79), calls=%async_computation | async-start | bytes 2097152 | tf_op jit(solution)/shard_map/all_to_all | solution.py:25
  27.6 20.8 %forward_kernel.1 = (bf16[1008,512]{1,0:T(8,128)(2,1)}, bf16[1008,512]{1,0:T(8,128)(2,1)}, bf16[1008,512]{1,0:T(8,128)(2,1)}, bf16[1008,512]{1,0:T(8,128)(2,1)},...) custom-call(s32[7]{0:T(128)} %len_ref.3, ...), custom_call_target="tpu_custom_call" | custom-call | flops 20899999744 | bytes 64600000 | tf_op jit(solution)/shard_map/forward_kernel/pallas_call | solution.py:471
  48.4 13.9 %all-to-all-done.refs_0_ = bf16[8,128,512]{2,1,0:T(8,128)(2,1)S(1)} async-done(((bf16[8,128,512]{2,1,0:T(8,128)(2,1)}), bf16[8,128,512]{2,1,0:T(8,128)(2,1)S(1)}, u32[]{:S(2)}, u32[]{:S(2)}) %all-to-all-start) | async-done | bytes 1048608 | tf_op jit(solution)/shard_map/all_to_all | solution.py:25
  62.3 4.2 %all-to-all-start.1 = ((bf16[8,128,512]{2,1,0:T(8,128)(2,1)}), bf16[8,128,512]{2,1,0:T(8,128)(2,1)}, u32[]{:S(2)}, u32[]{:S(2)}) async-start(bf16[8,128,512]{2,1,0:T(8,128)(2,1)} %get-tuple-element.80), calls=%async_computation.1 | async-start | bytes 2097152 | tf_op jit(solution)/shard_map/all_to_all | solution.py:25
  66.6 14.1 %all-to-all-done.1.x_ref = bf16[8,128,512]{2,1,0:T(8,128)(2,1)} async-done(((bf16[8,128,512]{2,1,0:T(8,128)(2,1)}), bf16[8,128,512]{2,1,0:T(8,128)(2,1)}, u32[]{:S(2)}, u32[]{:S(2)}) %all-to-all-start.1) | async-done | bytes 1048608 | tf_op jit(solution)/shard_map/all_to_all | solution.py:25
  80.6 4.6 %all-to-all-start.3 = ((bf16[8,144,1024]{2,1,0:T(8,128)(2,1)}), bf16[8,144,1024]{2,1,0:T(8,128)(2,1)}, u32[]{:S(2)}, u32[]{:S(2)}) async-start(bf16[8,144,1024]{2,1,0:T(8,128)(2,1)} %get-tuple-element.90), calls=%async_computation.3 | async-start | bytes 4718592 | tf_op jit(solution)/shard_map/all_to_all | solution.py:25
  85.2 1.4 broadcast_select_fusion.2.refs_2_
  87.6 1.8 collective-permute-done.4.refs_4_
  89.4 1.5 collective-permute-done.3.refs_3_
  91.9 17.2 %expert_kernel.2 = (bf16[8,128,512]{2,1,0:T(8,128)(2,1)}, bf16[8,128,512]{2,1,0:T(8,128)(2,1)}, bf16[8,128,2048]{2,1,0:T(8,128)(2,1)}, bf16[8,128,2048]{2,1,0:T(8,128)(2,1)}, bf16[8,128,512]{2,1,0:T(8,128)(2,1)}) custom-call(bf16[8,128,512]{2,1,0:T(8,128)(2,1)} %all-to-all-done.1.x_ref, bf16[8,128,512]{2,1,0:T(8,128)(2,1)} %copy-done.5, ...), custom_call_target="tpu_custom_call" | custom-call | flops 23100000256 | bytes 71400000 | tf_op jit(solution)/shard_map/expert_kernel/pallas_call | solution.py:619
  109.1 6.8 %all-to-all-done.3.x_ref = bf16[8,144,1024]{2,1,0:T(8,128)(2,1)} async-done(((bf16[8,144,1024]{2,1,0:T(8,128)(2,1)}), bf16[8,144,1024]{2,1,0:T(8,128)(2,1)}, u32[]{:S(2)}, u32[]{:S(2)}) %all-to-all-start.3) | async-done | bytes 2359328 | tf_op jit(solution)/shard_map/all_to_all | solution.py:25
  115.9 5.8 %all-to-all-start.2 = ((bf16[8,128,512]{2,1,0:T(8,128)(2,1)}), bf16[8,128,512]{2,1,0:T(8,128)(2,1)S(1)}, u32[]{:S(2)}, u32[]{:S(2)}) async-start(bf16[8,128,512]{2,1,0:T(8,128)(2,1)} %get-tuple-element.89), calls=%async_computation.2 | async-start | bytes 2097152 | tf_op jit(solution)/shard_map/all_to_all | solution.py:25
  121.7 19.8 %expert_kernel.3 = (bf16[8,144,512]{2,1,0:T(8,128)(2,1)}, bf16[8,272,512]{2,1,0:T(8,128)(2,1)}, bf16[8,144,2048]{2,1,0:T(8,128)(2,1)}, bf16[8,144,2048]{2,1,0:T(8,128)(2,1)}, bf16[8,144,512]{2,1,0:T(8,128)(2,1)}) custom-call(bf16[8,144,1024]{2,1,0:T(8,128)(2,1)} %all-to-all-done.3.x_ref, bf16[8,128,512]{2,1,0:T(8,128)(2,1)} %get-tuple-element.91.refs_0_, ...), custom_call_target="tpu_custom_call" | custom-call | flops 23100000256 | bytes 71400000 | tf_op jit(solution)/shard_map/expert_kernel/pallas_call | solution.py:619
  141.5 5.1 %all-to-all-start.4 = ((bf16[8,144,512]{2,1,0:T(8,128)(2,1)}), bf16[8,144,512]{2,1,0:T(8,128)(2,1)S(1)}, u32[]{:S(2)}, u32[]{:S(2)}) async-start(bf16[8,144,512]{2,1,0:T(8,128)(2,1)} %get-tuple-element.94), calls=%async_computation.4 | async-start | bytes 2359296 | tf_op jit(solution)/shard_map/all_to_all | solution.py:25
  146.7 16.4 %expert_grad_kernel.1 = (bf16[2,1024,512]{2,1,0:T(8,128)(2,1)}, bf16[2,512,512]{2,1,0:T(8,128)(2,1)}, bf16[2,512,512]{2,1,0:T(8,128)(2,1)}) custom-call(bf16[1024,512]{1,0:T(8,128)(2,1)} %bitcast.14.x_a, bf16[1152,1024]{1,0:T(8,128)(2,1)} %bitcast.15.x_b, bf16[1024,2048]{1,0:T(8,128)(2,1)} %bitcast.92, bf16[1152,2048]{1,0:T(8,128)(2,1)} %bitcast.90, ...), custom_call_target="tpu_custom_call" | custom-call | flops 17600000000 | bytes 54400000 | tf_op jit(solution)/shard_map/expert_grad_kernel/pallas_call | solution.py:654
  164.6 5.1 %all-to-all-start.6 = ((bf16[8,272,512]{2,1,0:T(8,128)(2,1)}), bf16[8,272,512]{2,1,0:T(8,128)(2,1)S(1)}, u32[]{:S(2)}, u32[]{:S(2)}) async-start(bf16[8,272,512]{2,1,0:T(8,128)(2,1)} %get-tuple-element.123), calls=%async_computation.6 | async-start | bytes 4456448 | tf_op jit(solution)/shard_map/all_to_all | solution.py:25
  169.8 2.8 add_convert_fusion
  172.6 2.1 collective-permute-start.9
  174.7 13.9 %combine_kernel.1 = (f32[1008,512]{1,0:T(8,128)}, bf16[1008,512]{1,0:T(8,128)(2,1)}, bf16[512,512]{1,0:T(8,128)(2,1)}, f32[128,512]{1,0:T(8,128)}, f32[8,512]{1,0:T(8,128)}) custom-call(bf16[8,128,512]{2,1,0:T(8,128)(2,1)} %copy-done.6, bf16[8,144,512]{2,1,0:T(8,128)(2,1)} %copy-done.3, s32[1008,128]{1,0:T(8,128)} %get-tuple-element.97.col_ref, ...), custom_call_target="tpu_custom_call" | custom-call | flops 18699999232 | bytes 57800000 | tf_op jit(solution)/shard_map/combine_kernel/pallas_call | solution.py:471
  188.6 14.9 %attention_back_kernel.1 = (bf16[1008,512]{1,0:T(8,128)(2,1)}, bf16[1008,512]{1,0:T(8,128)(2,1)}, bf16[1008,512]{1,0:T(8,128)(2,1)}, bf16[2,512,512]{2,1,0:T(8,1...) custom-call(s32[1]{0:T(128)} %bitcast.side_ref, bf16[1008,512]{1,0:T(8,128)(2,1)} %get-tuple-element.102.gm_ref, ...), custom_call_target="tpu_custom_call" | custom-call | flops 1100000000 | bytes 3400000 | tf_op jit(solution)/shard_map/attention_back_kernel/pallas_call | solution.py:471
  204.0 14.7 %collective-permute-done.9 = bf16[1024,512]{1,0:T(8,128)(2,1)S(1)} collective-permute-done((bf16[1024,512]{1,0:T(8,128)(2,1)S(1)}, bf16[1024,512]{1,0:T(8,128)(2,1)S(1)}, u32[]{:S(2)}, u32[]{:S(2)}) %collective-permute-start.9) | collective-permute-done | bytes 1048608 | tf_op jit(solution)/shard_map/ppermute | solution.py:21
  221.1 4.2 %all-to-all-start.5 = ((bf16[8,128,512]{2,1,0:T(8,128)(2,1)}), bf16[8,128,512]{2,1,0:T(8,128)(2,1)}, u32[]{:S(2)}, u32[]{:S(2)}) async-start(bf16[8,128,512]{2,1,0:T(8,128)(2,1)} %bitcast.64), calls=%async_computation.5 | async-start | bytes 2097152 | tf_op jit(solution)/shard_map/all_to_all | solution.py:25
  225.4 3.7 %collective-permute-start.10 = (bf16[512,512]{1,0:T(8,128)(2,1)S(1)}, bf16[512,512]{1,0:T(8,128)(2,1)}, u32[]{:S(2)}, u32[]{:S(2)}) collective-permute-start(bf16[512,512]{1,0:T(8,128)(2,1)S(1)} %slice.61), channel_id=1, source_target_pairs={{0,16},{16,0},{1,17},{17,1},{2,18},{18,2},{3,19},{19,3},{4,20},{20... | collective-permute-start | bytes 1572872 | tf_op jit(solution)/shard_map/ppermute | solution.py:21
  229.1 7.4 %image_kernel.1 = (f32[1008,512]{1,0:T(8,128)}, f32[8,512]{1,0:T(8,128)}) custom-call(bf16[1008,512]{1,0:T(8,128)(2,1)} %get-tuple-element.124.gq_ref, bf16[1008,512]{1,0:T(8,128)(2,1)} %get-tuple-element.125.gk_ref, bf16[1008,512]{1,0:T(8,128)(2,1)} %get-tuple-element.126.gv_ref, bf16[512,512]{1,0:T(8,128)(2,1)} %wq_ref.3, bf16[512,512]{1,0:T(8,128)(2,1)} %wk_ref.3, ...), custom_call_target="tpu_custom_call" | custom-call | flops 1100000000 | bytes 3400000 | tf_op jit(solution)/shard_map/image_kernel/pallas_call | solution.py:471
  236.5 6.5 %output_kernel.1 = bf16[1008,512]{1,0:T(8,128)(2,1)} custom-call(s32[1008,128]{1,0:T(8,128)} %get-tuple-element.97.col_ref, f32[1008,512]{1,0:T(8,128)} %get-tuple-element.99.residual_ref, bf16[2176,512]{1,0:T(8,128)(2,1)} %bitcast.59), custom_call_target="tpu_custom_call" | custom-call | flops 1100000000 | bytes 3400000 | tf_op jit(solution)/shard_map/output_kernel/pallas_call | solution.py:471
  243.0 4.6 %collective-permute-done.10 = bf16[512,512]{1,0:T(8,128)(2,1)} collective-permute-done((bf16[512,512]{1,0:T(8,128)(2,1)S(1)}, bf16[512,512]{1,0:T(8,128)(2,1)}, u32[]{:S(2)}, u32[]{:S(2)}) %collective-permute-start.10) | collective-permute-done | bytes 524320 | tf_op jit(solution)/shard_map/ppermute | solution.py:21
  247.6 4.8 %all-to-all-done.5 = bf16[8,128,512]{2,1,0:T(8,128)(2,1)} async-done(((bf16[8,128,512]{2,1,0:T(8,128)(2,1)}), bf16[8,128,512]{2,1,0:T(8,128)(2,1)}, u32[]{:S(2)}, u32[]{:S(2)}) %all-to-all-start.5) | async-done | bytes 1048608 | tf_op jit(solution)/shard_map/all_to_all | solution.py:25
  252.4 1.4 convert_reduce_fusion
  253.9 7.3 %collective-permute-done.11 = bf16[128,512]{1,0:T(8,128)(2,1)S(1)} collective-permute-done((bf16[128,512]{1,0:T(8,128)(2,1)S(1)}, bf16[128,512]{1,0:T(8,128)(2,1)S(1)}, u32[]{:S(2)}, u32[]{:S(2)}) %collective-permute-start.11) | collective-permute-done | bytes 131104 | tf_op jit(solution)/shard_map/ppermute | solution.py:21
  262.2 3.7 %all-to-all-start.7 = ((bf16[8,128,512]{2,1,0:T(8,128)(2,1)}), bf16[8,128,512]{2,1,0:T(8,128)(2,1)S(1)}, u32[]{:S(2)}, u32[]{:S(2)}) async-start(bf16[8,128,512]{2,1,0:T(8,128)(2,1)} %broadcast_in_dim.9), calls=%async_computation.7 | async-start | bytes 2097152 | tf_op jit(solution)/shard_map/all_to_all | solution.py:25
  266.0 2.0 collective-permute-start.17
  271.4 2.1 collective-permute-start.13
  273.5 1.9 collective-permute-done.13
  275.4 2.0 collective-permute-start.14
  277.4 1.9 collective-permute-done.14
  279.3 2.9 collective-permute-start.15
  282.2 7.1 %collective-permute-done.15 = f32[12,512]{1,0:T(8,128)S(1)} collective-permute-done((f32[12,512]{1,0:T(8,128)S(1)}, f32[12,512]{1,0:T(8,128)S(1)}, u32[]{:S(2)}, u32[]{:S(2)}) %collective-permute-start.15) | collective-permute-done | bytes 24608 | tf_op jit(solution)/shard_map/ppermute | solution.py:21
  289.4 3.7 %collective-permute-start.16 = (f32[12,512]{1,0:T(8,128)S(1)}, f32[12,512]{1,0:T(8,128)S(1)}, u32[]{:S(2)}, u32[]{:S(2)}) collective-permute-start(f32[12,512]{1,0:T(8,128)S(1)} %add.39), channel_id=1, source_target_pairs={{0,16},{16,0},{1,17},{17,1},{2,18},{18,2},{3,19},{19,3},{4,20},{20... | collective-permute-start | bytes 73736 | tf_op jit(solution)/shard_map/ppermute | solution.py:21
  293.1 1.9 collective-permute-done.16
  295.0 2.3 convert_add_fusion
  297.3 1.3 copy.36
  300.3 2.1 slice_bitcast_fusion
  (74 shorter events, 14.4 us)
Async XLA Ops:
  0.6 12.3 %copy-start.9 = (s32[7,144,2]{1,2,0:T(2,128)S(1)}, s32[7,144,2]{1,2,0:T(2,128)}, u32[]{:S(2)}) copy-start(s32[7,144,2]{1,2,0:T(2,128)} %param.19) | copy-start | bytes 24196
  4.0 44.4 %collective-permute-start = (bf16[1024,512]{1,0:T(8,128)(2,1)}, bf16[1024,512]{1,0:T(8,128)(2,1)S(1)}, u32[]{:S(2)}, u32[]{:S(2)}) collective-permute-start(bf16[1024,512]{1,0:T(8,128)(2,1)} %pad_maximum_fusion), channel_id=1, source_target_pairs={{0,16},{10,26},{18,2},{24,8},{1,17},{11,27},{19,3},{25,9},{4,20},{... | collective-permute-start | bytes 3145736 | tf_op jit(solution)/shard_map/ppermute | solution.py:494
  10.0 38.4 %collective-permute-start.1 = (bf16[1024,512]{1,0:T(8,128)(2,1)}, bf16[1024,512]{1,0:T(8,128)(2,1)}, u32[]{:S(2)}, u32[]{:S(2)}) collective-permute-start(bf16[1024,512]{1,0:T(8,128)(2,1)} %pad_maximum_fusion), channel_id=1, source_target_pairs={{2,0},{8,10},{16,18},{26,24},{3,1},{9,11},{17,19},{27,25},{6,4},{1... | collective-permute-start | bytes 3145736 | tf_op jit(solution)/shard_map/ppermute | solution.py:494
  11.3 37.1 %collective-permute-start.2 = (bf16[1024,512]{1,0:T(8,128)(2,1)}, bf16[1024,512]{1,0:T(8,128)(2,1)}, u32[]{:S(2)}, u32[]{:S(2)}) collective-permute-start(bf16[1024,512]{1,0:T(8,128)(2,1)} %pad_maximum_fusion), channel_id=1, source_target_pairs={{2,16},{8,26},{16,2},{26,8},{3,17},{9,27},{17,3},{27,9},{6,20},{12... | collective-permute-start | bytes 3145736 | tf_op jit(solution)/shard_map/ppermute | solution.py:494
  19.2 7.6 %copy-start.10 = (bf16[512,8]{0,1:T(8,128)(2,1)S(1)}, bf16[512,8]{0,1:T(8,128)(2,1)}, u32[]{:S(2)}) copy-start(bf16[512,8]{0,1:T(8,128)(2,1)} %param.29) | copy-start | bytes 24580
  19.2 43.2 %all-to-all-start = ((bf16[8,128,512]{2,1,0:T(8,128)(2,1)}), bf16[8,128,512]{2,1,0:T(8,128)(2,1)S(1)}, u32[]{:S(2)}, u32[]{:S(2)}) async-start(bf16[8,128,512]{2,1,0:T(8,128)(2,1)} %get-tuple-element.79), calls=%async_computation | async-start | bytes 2097152 | tf_op jit(solution)/shard_map/all_to_all | solution.py:25
  62.3 18.3 %copy-start.5 = (bf16[8,128,512]{2,1,0:T(8,128)(2,1)}, bf16[8,128,512]{2,1,0:T(8,128)(2,1)S(1)}, u32[]{:S(2)}) copy-start(bf16[8,128,512]{2,1,0:T(8,128)(2,1)S(1)} %all-to-all-done.refs_0_) | copy-start | bytes 3145732
  62.3 18.3 %all-to-all-start.1 = ((bf16[8,128,512]{2,1,0:T(8,128)(2,1)}), bf16[8,128,512]{2,1,0:T(8,128)(2,1)}, u32[]{:S(2)}, u32[]{:S(2)}) async-start(bf16[8,128,512]{2,1,0:T(8,128)(2,1)} %get-tuple-element.80), calls=%async_computation.1 | async-start | bytes 2097152 | tf_op jit(solution)/shard_map/all_to_all | solution.py:25
  80.6 35.3 %all-to-all-start.3 = ((bf16[8,144,1024]{2,1,0:T(8,128)(2,1)}), bf16[8,144,1024]{2,1,0:T(8,128)(2,1)}, u32[]{:S(2)}, u32[]{:S(2)}) async-start(bf16[8,144,1024]{2,1,0:T(8,128)(2,1)} %get-tuple-element.90), calls=%async_computation.3 | async-start | bytes 4718592 | tf_op jit(solution)/shard_map/all_to_all | solution.py:25
  85.2 1.5 copy-start.2
  86.6 4.2 %copy-start.7 = (bf16[1024,512]{1,0:T(8,128)(2,1)}, bf16[1024,512]{1,0:T(8,128)(2,1)S(1)}, u32[]{:S(2)}) copy-start(bf16[1024,512]{1,0:T(8,128)(2,1)S(1)} %broadcast_select_fusion.2.refs_2_) | copy-start | bytes 3145732
  86.6 2.7 collective-permute-start.4
  87.0 3.8 %copy-start.8 = (bf16[1024,512]{1,0:T(8,128)(2,1)}, bf16[1024,512]{1,0:T(8,128)(2,1)S(1)}, u32[]{:S(2)}) copy-start(bf16[1024,512]{1,0:T(8,128)(2,1)S(1)} %broadcast_select_fusion.3.refs_1_) | copy-start | bytes 3145732
  87.0 3.8 %collective-permute-start.3 = (bf16[1024,512]{1,0:T(8,128)(2,1)S(1)}, bf16[1024,512]{1,0:T(8,128)(2,1)S(1)}, u32[]{:S(2)}, u32[]{:S(2)}) collective-permute-start(bf16[1024,512]{1,0:T(8,128)(2,1)S(1)} %broadcast_select_fusion.3.refs_1_), channel_id=1, source_target_pairs={{0,1},{1,0},{2,3},{3,2},{4,5},{5,4},{6,7},{7,6},{8,9},{9,8},{10,11... | collective-permute-start | bytes 3145736 | tf_op jit(solution)/shard_map/ppermute | solution.py:21
  89.4 1.5 copy-start.11
  90.9 1.0 copy-start.12
  115.9 25.6 %all-to-all-start.2 = ((bf16[8,128,512]{2,1,0:T(8,128)(2,1)}), bf16[8,128,512]{2,1,0:T(8,128)(2,1)S(1)}, u32[]{:S(2)}, u32[]{:S(2)}) async-start(bf16[8,128,512]{2,1,0:T(8,128)(2,1)} %get-tuple-element.89), calls=%async_computation.2 | async-start | bytes 2097152 | tf_op jit(solution)/shard_map/all_to_all | solution.py:25
  141.5 21.5 %copy-start.6 = (bf16[8,128,512]{2,1,0:T(8,128)(2,1)}, bf16[8,128,512]{2,1,0:T(8,128)(2,1)S(1)}, u32[]{:S(2)}) copy-start(bf16[8,128,512]{2,1,0:T(8,128)(2,1)S(1)} %all-to-all-done.2.back_a) | copy-start | bytes 3145732
  141.5 22.1 %all-to-all-start.4 = ((bf16[8,144,512]{2,1,0:T(8,128)(2,1)}), bf16[8,144,512]{2,1,0:T(8,128)(2,1)S(1)}, u32[]{:S(2)}, u32[]{:S(2)}) async-start(bf16[8,144,512]{2,1,0:T(8,128)(2,1)} %get-tuple-element.94), calls=%async_computation.4 | async-start | bytes 2359296 | tf_op jit(solution)/shard_map/all_to_all | solution.py:25
  163.0 6.7 %collective-permute-start.7 = (bf16[2,512,512]{2,1,0:T(8,128)(2,1)}, bf16[2,512,512]{2,1,0:T(8,128)(2,1)}, u32[]{:S(2)}, u32[]{:S(2)}) collective-permute-start(bf16[2,512,512]{2,1,0:T(8,128)(2,1)} %get-tuple-element.119), channel_id=1, source_target_pairs={{0,1},{1,0},{2,3},{3,2},{4,5},{5,4},{6,7},{7,6},{8,9},{9,8},{10,11... | collective-permute-start | bytes 3145736 | tf_op jit(solution)/shard_map/ppermute | solution.py:21
  163.1 6.6 %collective-permute-start.8 = (bf16[2,512,512]{2,1,0:T(8,128)(2,1)}, bf16[2,512,512]{2,1,0:T(8,128)(2,1)}, u32[]{:S(2)}, u32[]{:S(2)}) collective-permute-start(bf16[2,512,512]{2,1,0:T(8,128)(2,1)} %get-tuple-element.120), channel_id=1, source_target_pairs={{0,1},{1,0},{2,3},{3,2},{4,5},{5,4},{6,7},{7,6},{8,9},{9,8},{10,11... | collective-permute-start | bytes 3145736 | tf_op jit(solution)/shard_map/ppermute | solution.py:21
  163.6 1.0 copy-start.3
  164.6 56.4 %all-to-all-start.6 = ((bf16[8,272,512]{2,1,0:T(8,128)(2,1)}), bf16[8,272,512]{2,1,0:T(8,128)(2,1)S(1)}, u32[]{:S(2)}, u32[]{:S(2)}) async-start(bf16[8,272,512]{2,1,0:T(8,128)(2,1)} %get-tuple-element.123), calls=%async_computation.6 | async-start | bytes 4456448 | tf_op jit(solution)/shard_map/all_to_all | solution.py:25
  172.6 46.1 %collective-permute-start.9 = (bf16[1024,512]{1,0:T(8,128)(2,1)S(1)}, bf16[1024,512]{1,0:T(8,128)(2,1)S(1)}, u32[]{:S(2)}, u32[]{:S(2)}) collective-permute-start(bf16[1024,512]{1,0:T(8,128)(2,1)S(1)} %slice_bitcast_fusion.5), channel_id=1, source_target_pairs={{0,2},{2,0},{1,3},{3,1},{4,6},{6,4},{5,7},{7,5},{8,10},{10,8},{9,1... | collective-permute-start | bytes 3145736 | tf_op jit(solution)/shard_map/ppermute | solution.py:21
  203.5 16.3 %collective-permute-start.5 = (bf16[512,512]{1,0:T(8,128)(2,1)}, bf16[512,512]{1,0:T(8,128)(2,1)S(1)}, u32[]{:S(2)}, u32[]{:S(2)}) collective-permute-start(bf16[512,512]{1,0:T(8,128)(2,1)} %get-tuple-element.110), channel_id=1, source_target_pairs={{0,1},{1,0},{2,3},{3,2},{4,5},{5,4},{6,7},{7,6},{8,9},{9,8},{10,11... | collective-permute-start | bytes 1572872 | tf_op jit(solution)/shard_map/ppermute | solution.py:21
  203.5 16.3 %copy-start.4 = (bf16[2,512,512]{2,1,0:T(8,128)(2,1)S(1)}, bf16[2,512,512]{2,1,0:T(8,128)(2,1)}, u32[]{:S(2)}) copy-start(bf16[2,512,512]{2,1,0:T(8,128)(2,1)} %get-tuple-element.109) | copy-start | bytes 3145732
  203.5 16.3 %collective-permute-start.6 = (bf16[512,512]{1,0:T(8,128)(2,1)}, bf16[512,512]{1,0:T(8,128)(2,1)S(1)}, u32[]{:S(2)}, u32[]{:S(2)}) collective-permute-start(bf16[512,512]{1,0:T(8,128)(2,1)} %get-tuple-element.111), channel_id=1, source_target_pairs={{0,1},{1,0},{2,3},{3,2},{4,5},{5,4},{6,7},{7,6},{8,9},{9,8},{10,11... | collective-permute-start | bytes 1572872 | tf_op jit(solution)/shard_map/ppermute | solution.py:21
  221.1 15.4 %copy-start = (bf16[8,272,512]{2,1,0:T(8,128)(2,1)}, bf16[8,272,512]{2,1,0:T(8,128)(2,1)S(1)}, u32[]{:S(2)}) copy-start(bf16[8,272,512]{2,1,0:T(8,128)(2,1)S(1)} %all-to-all-done.6) | copy-start | bytes 6684676
  221.1 31.3 %all-to-all-start.5 = ((bf16[8,128,512]{2,1,0:T(8,128)(2,1)}), bf16[8,128,512]{2,1,0:T(8,128)(2,1)}, u32[]{:S(2)}, u32[]{:S(2)}) async-start(bf16[8,128,512]{2,1,0:T(8,128)(2,1)} %bitcast.64), calls=%async_computation.5 | async-start | bytes 2097152 | tf_op jit(solution)/shard_map/all_to_all | solution.py:25
  225.4 22.2 %collective-permute-start.10 = (bf16[512,512]{1,0:T(8,128)(2,1)S(1)}, bf16[512,512]{1,0:T(8,128)(2,1)}, u32[]{:S(2)}, u32[]{:S(2)}) collective-permute-start(bf16[512,512]{1,0:T(8,128)(2,1)S(1)} %slice.61), channel_id=1, source_target_pairs={{0,16},{16,0},{1,17},{17,1},{2,18},{18,2},{3,19},{19,3},{4,20},{20... | collective-permute-start | bytes 1572872 | tf_op jit(solution)/shard_map/ppermute | solution.py:21
  253.8 7.3 %collective-permute-start.11 = (bf16[128,512]{1,0:T(8,128)(2,1)S(1)}, bf16[128,512]{1,0:T(8,128)(2,1)S(1)}, u32[]{:S(2)}, u32[]{:S(2)}) collective-permute-start(bf16[128,512]{1,0:T(8,128)(2,1)S(1)} %convert_element_type.59), channel_id=1, source_target_pairs={{0,16},{16,0},{1,17},{17,1},{2,18},{18,2},{3,19},{19,3},{4,20},{20... | collective-permute-start | bytes 393224 | tf_op jit(solution)/shard_map/ppermute | solution.py:21
  262.2 32.8 %copy-start.1 = (bf16[1024,512]{1,0:T(8,128)(2,1)S(1)}, bf16[1024,512]{1,0:T(8,128)(2,1)}, u32[]{:S(2)}) copy-start(bf16[1024,512]{1,0:T(8,128)(2,1)} %get-tuple-element.167) | copy-start | bytes 3145732
  262.2 35.1 %all-to-all-start.7 = ((bf16[8,128,512]{2,1,0:T(8,128)(2,1)}), bf16[8,128,512]{2,1,0:T(8,128)(2,1)S(1)}, u32[]{:S(2)}, u32[]{:S(2)}) async-start(bf16[8,128,512]{2,1,0:T(8,128)(2,1)} %broadcast_in_dim.9), calls=%async_computation.7 | async-start | bytes 2097152 | tf_op jit(solution)/shard_map/all_to_all | solution.py:25
  266.0 29.0 %collective-permute-start.17 = (bf16[512,512]{1,0:T(8,128)(2,1)S(1)}, bf16[512,512]{1,0:T(8,128)(2,1)S(1)}, u32[]{:S(2)}, u32[]{:S(2)}) collective-permute-start(bf16[512,512]{1,0:T(8,128)(2,1)S(1)} %slice.67), channel_id=1, source_target_pairs={{0,16},{16,0},{1,17},{17,1},{2,18},{18,2},{3,19},{19,3},{4,20},{20... | collective-permute-start | bytes 1572872 | tf_op jit(solution)/shard_map/ppermute | solution.py:21
  270.1 1.3 collective-permute-start.12
  271.4 4.0 %collective-permute-start.13 = (f32[12,512]{1,0:T(8,128)S(1)}, f32[12,512]{1,0:T(8,128)S(1)}, u32[]{:S(2)}, u32[]{:S(2)}) collective-permute-start(f32[12,512]{1,0:T(8,128)S(1)} %fusion), channel_id=1, source_target_pairs={{0,4},{4,0},{1,5},{5,1},{2,6},{6,2},{3,7},{7,3},{8,12},{12,8},{9,1... | collective-permute-start | bytes 73736 | tf_op jit(solution)/shard_map/ppermute | solution.py:21
  275.4 3.9 %collective-permute-start.14 = (f32[12,512]{1,0:T(8,128)S(1)}, f32[12,512]{1,0:T(8,128)S(1)}, u32[]{:S(2)}, u32[]{:S(2)}) collective-permute-start(f32[12,512]{1,0:T(8,128)S(1)} %add.37), channel_id=1, source_target_pairs={{0,2},{2,0},{1,3},{3,1},{4,6},{6,4},{5,7},{7,5},{8,10},{10,8},{9,1... | collective-permute-start | bytes 73736 | tf_op jit(solution)/shard_map/ppermute | solution.py:21
  279.3 10.0 %collective-permute-start.15 = (f32[12,512]{1,0:T(8,128)S(1)}, f32[12,512]{1,0:T(8,128)S(1)}, u32[]{:S(2)}, u32[]{:S(2)}) collective-permute-start(f32[12,512]{1,0:T(8,128)S(1)} %add.38), channel_id=1, source_target_pairs={{0,8},{8,0},{1,9},{9,1},{2,10},{10,2},{3,11},{11,3},{4,12},{12,4},... | collective-permute-start | bytes 73736 | tf_op jit(solution)/shard_map/ppermute | solution.py:21
  289.4 5.6 %collective-permute-start.16 = (f32[12,512]{1,0:T(8,128)S(1)}, f32[12,512]{1,0:T(8,128)S(1)}, u32[]{:S(2)}, u32[]{:S(2)}) collective-permute-start(f32[12,512]{1,0:T(8,128)S(1)} %add.39), channel_id=1, source_target_pairs={{0,16},{16,0},{1,17},{17,1},{2,18},{18,2},{3,19},{19,3},{4,20},{20... | collective-permute-start | bytes 73736 | tf_op jit(solution)/shard_map/ppermute | solution.py:21
  297.3 2.7 collective-permute-start.18

commit v4 on v3

--- a/solution.py
+++ b/solution.py
@@ -296,11 +296,17 @@
         put_rows(back_ref, c, back[here], along[here])
 
 
-def expert_grad_kernel(x_a, x_b, pre_a, pre_b, act_a, act_b, grad_a, grad_b, near_ref, far_in, far_out):
-    units = pre_a.shape[1]
+def first_grad_kernel(x_ref, pre_ref, act_ref, grad_ref, out_ref):
+    units = pre_ref.shape[1]
+    out_ref[0, 0:units, :] = dot_tn(pre_ref[...], x_ref[...]).astype(BF)
+    out_ref[0, units:, :] = dot_tn(act_ref[...], grad_ref[...]).astype(BF)
+
+
+def second_grad_kernel(x_ref, pre_ref, act_ref, grad_ref, first_ref, near_ref, far_in, far_out):
+    units = pre_ref.shape[1]
     near = pl.program_id(0) < pl.num_programs(0) // 2
-    grad_in = (dot_tn(pre_a[...], x_a[...]) + dot_tn(pre_b[...], x_b[...])).astype(BF)
-    grad_out = (dot_tn(act_a[...], grad_a[...]) + dot_tn(act_b[...], grad_b[...])).astype(BF)
+    grad_in = (dot_tn(pre_ref[...], x_ref[...]) + first_ref[0, 0:units, :].astype(F32)).astype(BF)
+    grad_out = (dot_tn(act_ref[...], grad_ref[...]) + first_ref[0, units:, :].astype(F32)).astype(BF)
 
     @pl.when(near)
     def _():
@@ -322,93 +328,96 @@
 
 def combine_kernel(
     back_a, back_b, col_ref, soft_ref, residual_ref, cot_ref, two_ref, mixed_ref, gain_two, router_ref, wo_ref,
-    resid_ref, gm_ref, wg_out_ref, wg_router_ref, small_ref, slots_ref, attn_ref, logit_ref, *, experts, stride,
+    resid_ref, gm_ref, wg_out_ref, wg_router_ref, small_ref, slots_ref, total_ref, *, experts, stride,
 ):
-    rows, width = cot_ref.shape
-    step = row_block(rows)
-    slots = experts * stride
-    for e in range(experts):
-        base = e * stride
-        for back_ref in (back_a, back_b):
-            here = slice(base, base + back_ref.shape[1])
-            base += back_ref.shape[1]
-            slots_ref[here, 0:width] = back_ref[e]
-            along = get_column(back_ref, e, width)
-            label = iota((along.shape[0], 128), 1)
-            high, low = high_low(jnp.where(label == served(e, experts), along, 0.0))
-            slots_ref[here, width : width + 128] = high
-            slots_ref[here, width + 128 : width + 256] = low
-
-    def combine(block, carry):
-        gain_sum, shift_sum = carry
-        here = pl.ds(pl.multiple_of(block * step, 16), step)
-        both = dot(hot_of(col_ref, here, slots), slots_ref[...])
-        grad_two = both[:, 0:width]
-        grad_gate = both[:, width : width + 128] + both[:, width + 128 : width + 256]
-        soft = soft_ref[here, :]
-        inner = jnp.sum(soft * grad_gate, axis=1, keepdims=True)
-        logits = (soft * (grad_gate - inner)).astype(BF)
-        logit_ref[here, :] = logits
-        grad_two = grad_two + dot_nt(logits, router_ref[...])
-        xhat, rstd = normalise(residual_ref[here, :])
-        grad = cot_ref[here, :].astype(F32) + norm_back(grad_two, xhat, rstd, gain_two[...])
-        resid_ref[here, :] = grad
-        low = grad.astype(BF)
-        attn_ref[here, :] = low
-        gm_ref[here, :] = dot_nt(low, wo_ref[...]).astype(BF)
-        gain_sum = gain_sum + jnp.sum(grad_two * xhat, axis=0, keepdims=True)
-        shift_sum = shift_sum + jnp.sum(grad_two, axis=0, keepdims=True)
-        return gain_sum, shift_sum
-
-    zero = jnp.zeros((1, width), F32)
-    gain_sum, shift_sum = lax.fori_loop(0, rows // step, combine, (zero, zero))
-    which = iota((8, width), 0)
-    small_ref[...] = jnp.where(which == 0, gain_sum, jnp.where(which == 1, shift_sum, 0.0))
-    wg_router_ref[...] = dot_tn(logit_ref[...], two_ref[...])
-    wg_out_ref[...] = dot_tn(mixed_ref[...], attn_ref[...]).astype(BF)
+    at = pl.program_id(0)
+    width = cot_ref.shape[1]
+
+    @pl.when(at == 0)
+    def _():
+        for e in range(experts):
+            base = e * stride
+            for back_ref in (back_a, back_b):
+                here = slice(base, base + back_ref.shape[1])
+                base += back_ref.shape[1]
+                slots_ref[here, 0:width] = back_ref[e]
+                along = get_column(back_ref, e, width)
+                label = iota((along.shape[0], 128), 1)
+                high, low = high_low(jnp.where(label == served(e, experts), along, 0.0))
+                slots_ref[here, width : width + 128] = high
+                slots_ref[here, width + 128 : width + 256] = low
+        small_ref[...] = jnp.zeros(small_ref.shape, F32)
+        wg_router_ref[...] = jnp.zeros(wg_router_ref.shape, F32)
+        total_ref[...] = jnp.zeros(total_ref.shape, F32)
+
+    both = dot(hot_of(col_ref, slice(None), experts * stride), slots_ref[...])
+    grad_two = both[:, 0:width]
+    grad_gate = both[:, width : width + 128] + both[:, width + 128 : width + 256]
+    soft = soft_ref[...]
+    inner = jnp.sum(soft * grad_gate, axis=1, keepdims=True)
+    logits = (soft * (grad_gate - inner)).astype(BF)
+    grad_two = grad_two + dot_nt(logits, router_ref[...])
+    xhat, rstd = normalise(residual_ref[...])
+    grad = cot_ref[...].astype(F32) + norm_back(grad_two, xhat, rstd, gain_two[...])
+    resid_ref[...] = grad
+    low = grad.astype(BF)
+    gm_ref[...] = dot_nt(low, wo_ref[...]).astype(BF)
+    which = iota(small_ref.shape, 0)
+    gain_sum = jnp.sum(grad_two * xhat, axis=0, keepdims=True)
+    shift_sum = jnp.sum(grad_two, axis=0, keepdims=True)
+    small_ref[...] += jnp.where(which == 0, gain_sum, jnp.where(which == 1, shift_sum, 0.0))
+    wg_router_ref[...] += dot_tn(logits, two_ref[...])
+    total_ref[...] += dot_tn(mixed_ref[...], low)
+
+    @pl.when(at == pl.num_programs(0) - 1)
+    def _():
+        wg_out_ref[...] = total_ref[...].astype(BF)
 
 
 def attention_back_kernel(
-    side_ref, gm_ref, normed_ref, q_ref, k_ref, v_ref, prob_ref, wo_ref, gq_ref, gk_ref, gv_ref, near_ref, far_one, far_two,
-    *, patches, group,
+    side_ref, gm_ref, q_ref, k_ref, v_ref, prob_ref, normed_ref, wo_ref, gq_ref, gk_ref, gv_ref, near_ref,
+    far_0, far_1, far_2, far_3, gq_all, gk_all, gv_all, *, group,
 ):
-    rows, width = gm_ref.shape
+    patches, width = gm_ref.shape
     size = width // HEADS
     lanes = group * size
-
-    def attend(image, carry):
-        here = pl.ds(pl.multiple_of(image * patches, 16), patches)
-        for g in range(HEADS // group):
-            cols = pl.ds(g * lanes, lanes)
-            probs = prob_ref[image, g]
-            wide = probs.astype(F32)
-            mixed = stack_heads(gm_ref[here, cols], group, size)
-            keys = k_ref[here, cols]
-            grad_probs = dot_nt(v_ref[here, cols], mixed)
-            inner = jnp.sum(grad_probs * wide, axis=0, keepdims=True)
-            scores = (wide * (grad_probs - inner)).astype(BF)
-            gv_ref[here, cols] = dot(probs, mixed).astype(BF)
-            gk_ref[here, cols] = dot(scores, stack_heads(q_ref[here, cols], group, size)).astype(BF)
-            queries = take_heads(dot_tn(scores, keys), group, size)
-            gq_ref[here, cols] = (queries * size**-0.5).astype(BF)
-        return carry
-
-    lax.fori_loop(0, rows // patches, attend, 0)
-    upper = side_ref[0] == 1
-    lower = jnp.logical_not(upper)
-
-    def put(n, value):
-        @pl.when(upper if n // 2 else lower)
-        def _():
-            near_ref[n % 2] = value
-
-        @pl.when(lower if n // 2 else upper)
-        def _():
-            (far_one, far_two)[n % 2][...] = value
-
-    put(0, wo_ref[...])
-    for n, grad_ref in enumerate((gq_ref, gk_ref, gv_ref)):
-        put(n + 1, dot_tn(normed_ref[...], grad_ref[...]).astype(BF))
+    here = pl.ds(pl.multiple_of(pl.program_id(0) * patches, 16), patches)
+    for g in range(HEADS // group):
+        cols = pl.ds(g * lanes, lanes)
+        probs = prob_ref[0, g]
+        wide = probs.astype(F32)
+        mixed = stack_heads(gm_ref[:, cols], group, size)
+        grad_probs = dot_nt(v_ref[:, cols], mixed)
+        inner = jnp.sum(grad_probs * wide, axis=0, keepdims=True)
+        scores = (wide * (grad_probs - inner)).astype(BF)
+        queries = take_heads(dot_tn(scores, k_ref[:, cols]), group, size)
+        for all_ref, one_ref, value in (
+            (gv_all, gv_ref, dot(probs, mixed)),
+            (gk_all, gk_ref, dot(scores, stack_heads(q_ref[:, cols], group, size))),
+            (gq_all, gq_ref, queries * size**-0.5),
+        ):
+            low = value.astype(BF)
+            all_ref[here, cols] = low
+            one_ref[:, cols] = low
+
+    @pl.when(pl.program_id(0) == pl.num_programs(0) - 1)
+    def _():
+        upper = side_ref[0] == 1
+        lower = jnp.logical_not(upper)
+
+        def put(n, value):
+            @pl.when(upper if n // 2 else lower)
+            def _():
+                near_ref[n % 2] = value
+
+            @pl.when(lower if n // 2 else upper)
+            def _():
+                for part, ref in enumerate(((far_0, far_1), (far_2, far_3))[n % 2]):
+                    ref[...] = value[part * ref.shape[0] : (part + 1) * ref.shape[0]]
+
+        put(0, wo_ref[...])
+        for n, grad_ref in enumerate((gq_all, gk_all, gv_all)):
+            put(n + 1, dot_tn(normed_ref[...], grad_ref[...]).astype(BF))
 
 
 def output_kernel(col_ref, residual_ref, res_ref, out_ref):
@@ -450,7 +459,8 @@
     "route": 7,
     "forward": 19,
     "expert": 21,
-    "expert_grad": 16,
+    "first_grad": 9,
+    "second_grad": 9,
     "combine": 17,
     "attention_back": 1,
     "output": 1,
@@ -495,6 +505,11 @@
 
     def over_hh(value):
         return swap(value, "hh", 2, 1)
+
+    def with_three(value, axes, size):
+        low, high = 1, size // 2
+        one, two, three = (swap(value, axes, size, flip) for flip in (low, high, low | high))
+        return (value + one) + (two + three)
 
     def over_eh(value):
         return swap(value, "eh", 2, 1)
@@ -600,13 +615,12 @@
 
         send_a, cot_a, moved = together(send_a, cot_a, moved)
         x_a = to_all(send_a, group)
-        send_b, moved = together(send_b, moved)
-        x_b = to_all(send_b, group)
-
         by_eh, by_hh, by_both = moved
         weights = [jnp.where(home, own, by_eh), jnp.where(home, by_hh, by_both)]
         for bit in range(half_h.bit_length() - 1):
             weights = weights + [swap(w, "hl", half_h, 1 << bit) for w in weights]
+        send_b, weights = together(send_b, weights)
+        x_b = to_all(send_b, group)
 
         def serve(begin, *arrays):
             count = arrays[0].shape[1]
@@ -628,67 +642,98 @@
                 name="expert_kernel",
             )(*arrays, *weights)
 
+        half = hidden // 2
+
+        def near(f):
+            return (jnp.minimum(f, half - 1), 0, 0)
+
+        def far(f):
+            return (jnp.maximum(f - half, 0), 0, 0)
+
+        def weight_grads(kernel, x, pre, act, grad, outs, *first):
+            arrays = [a.reshape(-1, a.shape[2]) for a in (x, pre, act, grad)]
+            count = arrays[0].shape[0]
+            full = pl.BlockSpec((count, width), lambda f: (0, 0))
+            part = pl.BlockSpec((count, units), lambda f: (0, f))
+            piece = [pl.BlockSpec((1,) + a.shape[1:], lambda f: (f, 0, 0)) for a in first]
+            return pl.pallas_call(
+                kernel,
+                grid=(hidden,),
+                out_shape=[jax.ShapeDtypeStruct((n, rows_here, width), BF) for n, rows_here, _ in outs],
+                in_specs=[full, part, part, full] + piece,
+                out_specs=[pl.BlockSpec((1, rows_here, width), at) for _, rows_here, at in outs],
+                compiler_params=pltpu.CompilerParams(vmem_limit_bytes=56 << 20),
+                cost_estimate=cost(kernel.__name__.removesuffix("_kernel")),
+                name=kernel.__name__,
+            )(*arrays, *first)
+
         back_a, result, act_a, pre_a, grad_a = serve(0, x_a, cot_a)
         back_a = to_all(back_a, group)
+        (first,) = weight_grads(
+            first_grad_kernel, x_a, pre_a, act_a, grad_a, [(hidden, 2 * units, lambda f: (f, 0, 0))]
+        )
+        x_b, first = together(x_b, first)
         back_b, result, act_b, pre_b, grad_b = serve(count_a, x_b, result)
         back_a, back_b = together(back_a, back_b)
         back_b = to_all(back_b, group)
         back_b, result = together(back_b, result)
         result = to_all(result, group)
-
-        half = hidden // 2
-
-        def near(f):
-            return (jnp.minimum(f, half - 1), 0, 0)
-
-        def far(f):
-            return (jnp.maximum(f - half, 0), 0, 0)
-
-        def rows_of(array):
-            return array.reshape(-1, array.shape[2])
-
-        pairs = [x_a, x_b, pre_a, pre_b, act_a, act_b, grad_a, grad_b]
-        pairs = [rows_of(p) for p in pairs]
-        full = [pl.BlockSpec((p.shape[0], width), lambda f: (0, 0)) for p in pairs[:2]]
-        part = [pl.BlockSpec((p.shape[0], units), lambda f: (0, f)) for p in pairs[:2]]
-        grads_near, *grads_far = pl.pallas_call(
-            expert_grad_kernel,
-            grid=(hidden,),
-            out_shape=[jax.ShapeDtypeStruct((half, n, width), BF) for n in (2 * units, units, units)],
-            in_specs=full + part + part + full,
-            out_specs=[pl.BlockSpec((1, 2 * units, width), near)] + [pl.BlockSpec((1, units, width), far)] * 2,
-            compiler_params=pltpu.CompilerParams(vmem_limit_bytes=56 << 20),
-            cost_estimate=cost("expert_grad"),
-            name="expert_grad_kernel",
-        )(*pairs)
+        outs = [(half, 2 * units, near), (half, units, far), (half, units, far)]
+        grads_near, *grads_far = weight_grads(
+            second_grad_kernel, x_b, pre_b, act_b, grad_b, outs, first
+        )
 
         came = [swap(g, "hl", half_h, half_h // 2) for g in grads_far]
         came = jnp.concatenate(came, axis=1)
         parts = fold_hl((grads_near.astype(F32) + came.astype(F32)).astype(BF))
-        passed = over_hh(parts[1])
-        mine, theirs = jnp.where(home, parts[0], passed), jnp.where(home, passed, parts[0])
-
-        resid, grad_mixed, wg_out, wg_router, small_two = call(
-            combine_kernel,
-            [token_wide, token_low, ((width, width), BF), ((128, width), F32), ((8, width), F32)],
-            [back_a, back_b, column, soft, residual, cot, two, mixed, gain_two, router, w_output],
-            scratch=[
-                pltpu.VMEM((slots, width + 256), BF),
-                pltpu.VMEM((rows, width), BF),
-                pltpu.VMEM((rows, 128), BF),
-            ],
-            experts=experts,
-            stride=stride,
-        )
+        cut = units * 48 // 32
+        passed_one, passed_two = over_hh(parts[1, :cut]), over_hh(parts[1, cut:])
+
+        def split(keep, passed):
+            return jnp.where(home, keep, passed), jnp.where(home, passed, keep)
+
+        def blocks_of(*arrays):
+            step = row_block(rows)
+            return [
+                pl.BlockSpec((step, a.shape[1]), lambda i: (i, 0))
+                if a.shape[0] == rows
+                else pl.BlockSpec(a.shape, lambda i, n=len(a.shape): (0,) * n)
+                for a in arrays
+            ]
+
+        arrays = [back_a, back_b, column, soft, residual, cot, two, mixed, gain_two, router, w_output]
+        outs = [token_wide, token_low, ((width, width), BF), ((128, width), F32), ((8, width), F32)]
+        outs = [jax.ShapeDtypeStruct(*o) for o in outs]
+        resid, grad_mixed, wg_out, wg_router, small_two = pl.pallas_call(
+            functools.partial(combine_kernel, experts=experts, stride=stride),
+            grid=(rows // row_block(rows),),
+            out_shape=outs,
+            in_specs=blocks_of(*arrays),
+            out_specs=blocks_of(*outs),
+            scratch_shapes=[pltpu.VMEM((slots, width + 256), BF), pltpu.VMEM((width, width), F32)],
+            compiler_params=pltpu.CompilerParams(vmem_limit_bytes=56 << 20),
+            cost_estimate=cost("combine"),
+            name="combine_kernel",
+        )(*arrays)
         side = (lax.axis_index("hl") // (half_h // 2)).reshape(1)
-        gq, gk, gv, wg_near, *wg_far = call(
-            attention_back_kernel,
-            [token_low] * 3 + [((2, width, width), BF)] + [((width, width), BF)] * 2,
-            [side, grad_mixed, normed, queries, keys, values, probs, wg_out],
-            scalars=1,
-            patches=patches,
-            group=GROUP,
-        )
+        one = pl.BlockSpec((patches, width), lambda i: (i, 0))
+        whole = pl.BlockSpec((rows, width), lambda i: (0, 0))
+        square = pl.BlockSpec((width, width), lambda i: (0, 0))
+        gq, gk, gv, wg_near, *wg_far = pl.pallas_call(
+            functools.partial(attention_back_kernel, group=GROUP),
+            grid=(image_count,),
+            out_shape=[jax.ShapeDtypeStruct((rows, width), BF)] * 3
+            + [jax.ShapeDtypeStruct((2, width, width), BF)]
+            + [jax.ShapeDtypeStruct((width // 2, width), BF)] * 4,
+            in_specs=[SCALAR, one, one, one, one]
+            + [pl.BlockSpec((1,) + probs.shape[1:], lambda i: (i, 0, 0, 0)), whole, square],
+            out_specs=[one] * 3 + [pl.BlockSpec((2, width, width), lambda i: (0, 0, 0))]
+            + [pl.BlockSpec((width // 2, width), lambda i: (0, 0))] * 4,
+            scratch_shapes=[pltpu.VMEM((rows, width), BF)] * 3,
+            compiler_params=pltpu.CompilerParams(vmem_limit_bytes=56 << 20),
+            cost_estimate=cost("attention_back"),
+            name="attention_back_kernel",
+        )(side, grad_mixed, queries, keys, values, probs, normed, wg_out)
 
         (block_out,) = call(
             output_kernel,
@@ -701,23 +746,34 @@
             [gq, gk, gv, w_query, w_key, w_value, tokens, resid, gain_one],
         )
 
-        came = jnp.stack([swap(w, "hl", half_h, half_h // 2) for w in wg_far])
+        small = jnp.concatenate([small_one[:2], small_two[:2], wg_router[:experts]])
+        others = [swap(small, ("eh", "em"), 4, flip) for flip in (1, 2, 3)]
+        others, block_out = together(others, block_out)
+        small = (small + others[0]) + (others[1] + others[2])
+
+        came = jnp.concatenate([swap(w, "hl", half_h, half_h // 2) for w in wg_far]).reshape(wg_near.shape)
         pieces = (wg_near.astype(F32) + came.astype(F32)).astype(BF)
         pieces = scatter_hl(pieces.reshape(half_h // 2, -1, width))
-        pieces, theirs = together(pieces, theirs)
+        pieces, passed_one = together(pieces, passed_one)
         pieces = to_all(pieces.reshape(experts, -1, width), group)
-        far_in = over_eh(theirs[:units])
-        pieces, far_in, theirs, block_out, grad_images = together(pieces, far_in, theirs, block_out, grad_images)
-        far_out = over_eh(theirs[units:])
+        mine_one, theirs_one = split(parts[0, :cut], passed_one)
+        far_one = over_eh(theirs_one)
+        pieces, far_one, passed_two, block_out, grad_images, small = together(
+            pieces, far_one, passed_two, block_out, grad_images, small
+        )
+        mine_two, theirs_two = split(parts[0, cut:], passed_two)
+        far_two = over_eh(theirs_two)
         piece = jnp.sum(pieces.astype(F32), axis=0)
         piece = (piece + over_eh(piece.astype(BF)).astype(F32)).astype(BF)
         pieces = to_all(jnp.broadcast_to(piece, (experts,) + piece.shape), group)
-        sum_in = (mine[:units].astype(F32) + far_in.astype(F32)).T
-        sum_out = mine[units:].astype(F32) + far_out.astype(F32)
-        small = jnp.concatenate([small_one[:2], small_two[:2], wg_router[:experts]])
-        for axis, size in (("hl", half_h), ("el", experts // 4), ("hh", 2), ("em", 2), ("eh", 2)):
-            for bit in range(size.bit_length() - 1):
-                small = small + swap(small, axis, size, 1 << bit)
+        sums = [mine_one.astype(F32) + far_one.astype(F32), mine_two.astype(F32) + far_two.astype(F32)]
+        sums = jnp.concatenate(sums)
+        sum_in, sum_out = sums[:units].T, sums[units:]
+        for bit in range(half_h.bit_length() - 1):
+            small = small + swap(small, "hl", half_h, 1 << bit)
+        for bit in range((experts // 8).bit_length() - 1):
+            small = small + swap(small, "el", experts // 4, 1 << bit)
+        small = with_three(small, ("el", "hh"), experts // 2)
         pieces, small, sum_in, sum_out = together(pieces, small, sum_in, sum_out)
         pieces = gather_hl(pieces.reshape(1, -1, width), half_h // 2)
         came = swap(pieces, "hl", half_h, half_h // 2)

time: 303 us -> 296 us (0.977)
  waiting for transfers between devices: 83.6 us -> 71.3 us
  Pallas kernels: 122 us -> 127 us
    pallas_call x1 -> x4, Pallas kernels: 16.4 us -> 49.4 us  [the longest x2 20.8 us: weight_grads(): pl.pallas_call(kernel, grid=(hidden,), out_shape=[jax.ShapeDtypeStruct((n...]
    pallas_call x6 -> x4, Pallas kernels: 69.1 us -> 40.4 us  [call(): pl.pallas_call(functools.partial(kernel, **names) if names else kernel, o...]
    ppermute x16 -> x21, waiting for transfers between devices: 44 us -> 36 us  [swap(): return lax.ppermute(value, axis, [(i, i ^ flip) for i in range(size)])]
    ppermute x16 -> x21, starting transfers between devices: 20.4 us -> 25.2 us  [swap(): return lax.ppermute(value, axis, [(i, i ^ flip) for i in range(size)])]
    all_to_all x8, starting transfers between devices: 40.3 us -> 36 us  [to_all(): return lax.all_to_all(blocks, axes, split_axis=0, concat_axis=0, tiled=True)]
    all_to_all x8, waiting for transfers between devices: 39.6 us -> 35.3 us  [to_all(): return lax.all_to_all(blocks, axes, split_axis=0, concat_axis=0, tiled=True)]
  transfers between devices with their start and end apart: 27 -> 32, of which waited for: 15 -> 19; matrix products, arithmetic and copies ran while one was open for 5% -> 5% of each run, Pallas kernels for 40% -> 43%
where the time goes in v4:
time: 296 us; the launch traced here: 294 us
  Pallas kernels  127 us (43%)
  waiting for transfers between devices  71.3 us (24%)
  starting transfers between devices  71.1 us (24%)
  local copies, waits for them, and re-layouts  13.4 us (5%)
  other arithmetic  10.7 us (4%)
    pallas_call x4, Pallas kernels, call(): pl.pallas_call(functools.partial(kernel, **names) if names else kernel, o...  40.4 us
    pallas_call x2, Pallas kernels, serve(): pl.pallas_call(functools.partial(expert_kernel, begin=begin), grid=(exper...  37.1 us
    all_to_all x8, starting transfers between devices, to_all(): return lax.all_to_all(blocks, axes, split_axis=0, concat_axis=0, tiled=True)  36 us
    ppermute x21, waiting for transfers between devices, swap(): return lax.ppermute(value, axis, [(i, i ^ flip) for i in range(size)])  36 us
    all_to_all x8, waiting for transfers between devices, to_all(): return lax.all_to_all(blocks, axes, split_axis=0, concat_axis=0, tiled=True)  35.3 us
    ppermute x21, starting transfers between devices, swap(): return lax.ppermute(value, axis, [(i, i ^ flip) for i in range(size)])  25.2 us
    pallas_call x2, Pallas kernels, weight_grads(): pl.pallas_call(kernel, grid=(hidden,), out_shape=[jax.ShapeDtypeStruct((n...  20.8 us
    pallas_call x1, Pallas kernels, on_device(): pl.pallas_call(functools.partial(combine_kernel, experts=experts, stride=...  14.5 us
  transfers between devices with their start and end apart: 32, of which 19 were waited for; matrix products, arithmetic and copies ran while one was open for 5% of the time, Pallas kernels for 43%

profile of v4, /device:TPU:0, one launch (start us, length us, event | category | flops | bytes accessed | tf_op | source)
XLA Modules:
  0.0 294.4 jit_solution(14905757711510913157)
XLA Ops:
  1.9 2.1 pad_maximum_fusion.1
  4.0 6.9 %collective-permute-start = (bf16[1024,512]{1,0:T(8,128)(2,1)}, bf16[1024,512]{1,0:T(8,128)(2,1)}, u32[]{:S(2)}, u32[]{:S(2)}) collective-permute-start(bf16[1024,512]{1,0:T(8,128)(2,1)} %pad_maximum_fusion.1), channel_id=1, source_target_pairs={{0,16},{10,26},{18,2},{24,8},{1,17},{11,27},{19,3},{25,9},{4,20},{... | collective-permute-start | bytes 3145736 | tf_op jit(solution)/shard_map/ppermute | solution.py:504
  10.9 1.3 collective-permute-start.1
  12.2 1.7 collective-permute-start.2
  14.6 5.5 %route_kernel.1 = (s32[1008,128]{1,0:T(8,128)}, s32[8,1008]{1,0:T(8,128)}, bf16[8,128,512]{2,1,0:T(8,128)(2,1)}) custom-call(s32[7]{0:T(128)} %len_ref.3, s32[1,1008]{1,0:T(1,128)} %pri_ref.1, s32[2,1008]{1,0:T(2,128)} %bitcast.80, bf16[1008,512]{1,0:T(8,128)(2,1)} %bitcast.88), custom_call_target="tpu_custom_call" | custom-call | flops 7699999744 | bytes 23800000 | tf_op jit(solution)/shard_map/route_kernel/pallas_call | solution.py:481
  20.1 6.7 %all-to-all-start = ((bf16[8,128,512]{2,1,0:T(8,128)(2,1)}), bf16[8,128,512]{2,1,0:T(8,128)(2,1)S(1)}, u32[]{:S(2)}, u32[]{:S(2)}) async-start(bf16[8,128,512]{2,1,0:T(8,128)(2,1)} %get-tuple-element.89), calls=%async_computation | async-start | bytes 2097152 | tf_op jit(solution)/shard_map/all_to_all | solution.py:25
  27.6 20.9 %forward_kernel.1 = (bf16[1008,512]{1,0:T(8,128)(2,1)}, bf16[1008,512]{1,0:T(8,128)(2,1)}, bf16[1008,512]{1,0:T(8,128)(2,1)}, bf16[1008,512]{1,0:T(8,128)(2,1)},...) custom-call(s32[7]{0:T(128)} %len_ref.3, ...), custom_call_target="tpu_custom_call" | custom-call | flops 20899999744 | bytes 64600000 | tf_op jit(solution)/shard_map/forward_kernel/pallas_call | solution.py:481
  48.5 13.8 %all-to-all-done.refs_0_ = bf16[8,128,512]{2,1,0:T(8,128)(2,1)S(1)} async-done(((bf16[8,128,512]{2,1,0:T(8,128)(2,1)}), bf16[8,128,512]{2,1,0:T(8,128)(2,1)S(1)}, u32[]{:S(2)}, u32[]{:S(2)}) %all-to-all-start) | async-done | bytes 1048608 | tf_op jit(solution)/shard_map/all_to_all | solution.py:25
  62.4 4.2 %all-to-all-start.1 = ((bf16[8,128,512]{2,1,0:T(8,128)(2,1)}), bf16[8,128,512]{2,1,0:T(8,128)(2,1)}, u32[]{:S(2)}, u32[]{:S(2)}) async-start(bf16[8,128,512]{2,1,0:T(8,128)(2,1)} %get-tuple-element.90), calls=%async_computation.1 | async-start | bytes 2097152 | tf_op jit(solution)/shard_map/all_to_all | solution.py:25
  67.9 1.8 collective-permute-done.3.refs_3_
  69.7 1.5 collective-permute-done.4.refs_4_
  72.1 8.5 %all-to-all-done.1.x_ref = bf16[8,128,512]{2,1,0:T(8,128)(2,1)} async-done(((bf16[8,128,512]{2,1,0:T(8,128)(2,1)}), bf16[8,128,512]{2,1,0:T(8,128)(2,1)}, u32[]{:S(2)}, u32[]{:S(2)}) %all-to-all-start.1) | async-done | bytes 1048608 | tf_op jit(solution)/shard_map/all_to_all | solution.py:25
  80.7 3.8 %all-to-all-start.3 = ((bf16[8,144,1024]{2,1,0:T(8,128)(2,1)}), bf16[8,144,1024]{2,1,0:T(8,128)(2,1)S(1)}, u32[]{:S(2)}, u32[]{:S(2)}) async-start(bf16[8,144,1024]{2,1,0:T(8,128)(2,1)} %get-tuple-element.101), calls=%async_computation.3 | async-start | bytes 4718592 | tf_op jit(solution)/shard_map/all_to_all | solution.py:25
  84.5 17.3 %expert_kernel.2 = (bf16[8,128,512]{2,1,0:T(8,128)(2,1)}, bf16[8,128,512]{2,1,0:T(8,128)(2,1)}, bf16[8,128,2048]{2,1,0:T(8,128)(2,1)}, bf16[8,128,2048]{2,1,0:T(8,128)(2,1)}, bf16[8,128,512]{2,1,0:T(8,128)(2,1)}) custom-call(bf16[8,128,512]{2,1,0:T(8,128)(2,1)} %all-to-all-done.1.x_ref, bf16[8,128,512]{2,1,0:T(8,128)(2,1)} %copy-done.4, ...), custom_call_target="tpu_custom_call" | custom-call | flops 23100000256 | bytes 71400000 | tf_op jit(solution)/shard_map/expert_kernel/pallas_call | solution.py:633
  101.7 9.1 %first_grad_kernel.1.first_ref = bf16[4,1024,512]{2,1,0:T(8,128)(2,1)} custom-call(bf16[1024,512]{1,0:T(8,128)(2,1)} %bitcast.11.x_ref, bf16[1024,2048]{1,0:T(8,128)(2,1)} %bitcast.98, bf16[1024,2048]{1,0:T(8,128)(2,1)} %bitcast.97, bf16[1024,512]{1,0:T(8,128)(2,1)} %bitcast.100), custom_call_target="tpu_custom_call" | custom-call | flops 9900000256 | bytes 30600000 | tf_op jit(solution)/shard_map/first_grad_kernel/pallas_call | solution.py:659
  110.9 6.6 %all-to-all-done.3.x_ref = bf16[8,144,1024]{2,1,0:T(8,128)(2,1)S(1)} async-done(((bf16[8,144,1024]{2,1,0:T(8,128)(2,1)}), bf16[8,144,1024]{2,1,0:T(8,128)(2,1)S(1)}, u32[]{:S(2)}, u32[]{:S(2)}) %all-to-all-start.3) | async-done | bytes 2359328 | tf_op jit(solution)/shard_map/all_to_all | solution.py:25
  117.4 4.3 %all-to-all-start.2 = ((bf16[8,128,512]{2,1,0:T(8,128)(2,1)}), bf16[8,128,512]{2,1,0:T(8,128)(2,1)S(1)}, u32[]{:S(2)}, u32[]{:S(2)}) async-start(bf16[8,128,512]{2,1,0:T(8,128)(2,1)} %get-tuple-element.100), calls=%async_computation.2 | async-start | bytes 2097152 | tf_op jit(solution)/shard_map/all_to_all | solution.py:25
  121.8 19.8 %expert_kernel.3 = (bf16[8,144,512]{2,1,0:T(8,128)(2,1)}, bf16[8,272,512]{2,1,0:T(8,128)(2,1)}, bf16[8,144,2048]{2,1,0:T(8,128)(2,1)}, bf16[8,144,2048]{2,1,0:T(8,128)(2,1)}, bf16[8,144,512]{2,1,0:T(8,128)(2,1)}) custom-call(bf16[8,144,1024]{2,1,0:T(8,128)(2,1)} %copy-done, bf16[8,128,512]{2,1,0:T(8,128)(2,1)} %get-tuple-element.106.refs_0_, ...), custom_call_target="tpu_custom_call" | custom-call | flops 23100000256 | bytes 71400000 | tf_op jit(solution)/shard_map/expert_kernel/pallas_call | solution.py:633
  141.6 5.1 %all-to-all-start.4 = ((bf16[8,144,512]{2,1,0:T(8,128)(2,1)}), bf16[8,144,512]{2,1,0:T(8,128)(2,1)S(1)}, u32[]{:S(2)}, u32[]{:S(2)}) async-start(bf16[8,144,512]{2,1,0:T(8,128)(2,1)} %get-tuple-element.109), calls=%async_computation.4 | async-start | bytes 2359296 | tf_op jit(solution)/shard_map/all_to_all | solution.py:25
  146.7 11.7 %second_grad_kernel.1 = (bf16[2,1024,512]{2,1,0:T(8,128)(2,1)}, bf16[2,512,512]{2,1,0:T(8,128)(2,1)}, bf16[2,512,512]{2,1,0:T(8,128)(2,1)}) custom-call(bf16[1152,1024]{1,0:T(8,128)(2,1)} %bitcast.73, bf16[1152,2048]{1,0:T(8,128)(2,1)} %bitcast.96, bf16[1152,2048]{1,0:T(8,128)(2,1)} %bitcast.95, bf16[1152,512]{1,0:T(8,128)(2,1)} %bitcast.99, ...), custom_call_target="tpu_custom_call" | custom-call | flops 9900000256 | bytes 30600000 | tf_op jit(solution)/shard_map/second_grad_kernel/pallas_call | solution.py:659
  159.0 3.4 %all-to-all-done.4.back_b = bf16[8,144,512]{2,1,0:T(8,128)(2,1)S(1)} async-done(((bf16[8,144,512]{2,1,0:T(8,128)(2,1)}), bf16[8,144,512]{2,1,0:T(8,128)(2,1)S(1)}, u32[]{:S(2)}, u32[]{:S(2)}) %all-to-all-start.4) | async-done | bytes 1179680 | tf_op jit(solution)/shard_map/all_to_all | solution.py:25
  163.3 4.6 %all-to-all-start.6 = ((bf16[8,272,512]{2,1,0:T(8,128)(2,1)}), bf16[8,272,512]{2,1,0:T(8,128)(2,1)}, u32[]{:S(2)}, u32[]{:S(2)}) async-start(bf16[8,272,512]{2,1,0:T(8,128)(2,1)} %get-tuple-element.145), calls=%async_computation.6 | async-start | bytes 4456448 | tf_op jit(solution)/shard_map/all_to_all | solution.py:25
  167.9 2.4 add_convert_fusion
  170.4 1.7 collective-permute-start.11
  172.2 14.5 %combine_kernel.1 = (f32[1008,512]{1,0:T(8,128)}, bf16[1008,512]{1,0:T(8,128)(2,1)}, bf16[512,512]{1,0:T(8,128)(2,1)}, f32[128,512]{1,0:T(8,128)}, f32[8,512]{1,0:T(8,128)}) custom-call(bf16[8,128,512]{2,1,0:T(8,128)(2,1)} %copy-done.5, bf16[8,144,512]{2,1,0:T(8,128)(2,1)} %copy-done.2, s32[1008,128]{1,0:T(8,128)} %get-tuple-element.112.col_ref, ...), custom_call_target="tpu_custom_call" | custom-call | flops 18699999232 | bytes 57800000 | tf_op jit(solution)/shard_map/combine_kernel/pallas_call | solution.py:707
  186.7 14.0 %attention_back_kernel.1 = (bf16[1008,512]{1,0:T(8,128)(2,1)}, bf16[1008,512]{1,0:T(8,128)(2,1)}, bf16[1008,512]{1,0:T(8,128)(2,1)}, bf16[2,512,512]{2,1,0:T(8,1...) custom-call(s32[1]{0:T(128)} %bitcast.side_ref, ...), custom_call_target="tpu_custom_call" | custom-call | flops 1100000000 | bytes 3400000 | tf_op jit(solution)/shard_map/attention_back_kernel/pallas_call | solution.py:722
  203.8 1.3 fusion
  205.1 3.8 %collective-permute-done.11 = bf16[768,512]{1,0:T(8,128)(2,1)} collective-permute-done((bf16[768,512]{1,0:T(8,128)(2,1)S(1)}, bf16[768,512]{1,0:T(8,128)(2,1)}, u32[]{:S(2)}, u32[]{:S(2)}) %collective-permute-start.11) | collective-permute-done | bytes 786464 | tf_op jit(solution)/shard_map/ppermute | solution.py:21
  208.9 3.6 %all-to-all-start.5 = ((bf16[8,128,512]{2,1,0:T(8,128)(2,1)}), bf16[8,128,512]{2,1,0:T(8,128)(2,1)S(1)}, u32[]{:S(2)}, u32[]{:S(2)}) async-start(bf16[8,128,512]{2,1,0:T(8,128)(2,1)} %bitcast.22), calls=%async_computation.5 | async-start | bytes 2097152 | tf_op jit(solution)/shard_map/all_to_all | solution.py:25
  213.8 3.7 %collective-permute-start.12 = (bf16[768,512]{1,0:T(8,128)(2,1)S(1)}, bf16[768,512]{1,0:T(8,128)(2,1)}, u32[]{:S(2)}, u32[]{:S(2)}) collective-permute-start(bf16[768,512]{1,0:T(8,128)(2,1)S(1)} %broadcast_select_fusion.2), channel_id=1, source_target_pairs={{0,16},{16,0},{1,17},{17,1},{2,18},{18,2},{3,19},{19,3},{4,20},{20... | collective-permute-start | bytes 2359304 | tf_op jit(solution)/shard_map/ppermute | solution.py:21
  217.5 3.2 %collective-permute-start.13 = (bf16[256,512]{1,0:T(8,128)(2,1)S(1)}, bf16[256,512]{1,0:T(8,128)(2,1)S(1)}, u32[]{:S(2)}, u32[]{:S(2)}) collective-permute-start(bf16[256,512]{1,0:T(8,128)(2,1)S(1)} %slice_bitcast_fusion.8), channel_id=1, source_target_pairs={{0,2},{2,0},{1,3},{3,1},{4,6},{6,4},{5,7},{7,5},{8,10},{10,8},{9,1... | collective-permute-start | bytes 786440 | tf_op jit(solution)/shard_map/ppermute | solution.py:21
  222.1 7.5 %image_kernel.1 = (f32[1008,512]{1,0:T(8,128)}, f32[8,512]{1,0:T(8,128)}) custom-call(bf16[1008,512]{1,0:T(8,128)(2,1)} %get-tuple-element.138.gq_ref, bf16[1008,512]{1,0:T(8,128)(2,1)} %get-tuple-element.139.gk_ref, bf16[1008,512]{1,0:T(8,128)(2,1)} %get-tuple-element.140.gv_ref, bf16[512,512]{1,0:T(8,128)(2,1)} %wq_ref.3, bf16[512,512]{1,0:T(8,128)(2,1)} %wk_ref.3, ...), custom_call_target="tpu_custom_call" | custom-call | flops 1100000000 | bytes 3400000 | tf_op jit(solution)/shard_map/image_kernel/pallas_call | solution.py:481
  230.8 4.0 %collective-permute-start.16 = (f32[12,512]{1,0:T(8,128)S(1)}, f32[12,512]{1,0:T(8,128)S(1)}, u32[]{:S(2)}, u32[]{:S(2)}) collective-permute-start(f32[12,512]{1,0:T(8,128)S(1)} %pad_maximum_fusion.3), channel_id=1, source_target_pairs={{0,24},{8,16},{16,8},{24,0},{1,25},{9,17},{17,9},{25,1},{2,26},{10... | collective-permute-start | bytes 73736 | tf_op jit(solution)/shard_map/ppermute | solution.py:21
  234.8 6.5 %output_kernel.1 = bf16[1008,512]{1,0:T(8,128)(2,1)} custom-call(s32[1008,128]{1,0:T(8,128)} %get-tuple-element.112.col_ref, f32[1008,512]{1,0:T(8,128)} %get-tuple-element.114.residual_ref, bf16[2176,512]{1,0:T(8,128)(2,1)} %bitcast.25.res_ref), custom_call_target="tpu_custom_call" | custom-call | flops 1100000000 | bytes 3400000 | tf_op jit(solution)/shard_map/output_kernel/pallas_call | solution.py:481
  241.3 2.6 collective-permute-done.14
  243.9 10.4 %collective-permute-done.15 = f32[12,512]{1,0:T(8,128)S(1)} collective-permute-done((f32[12,512]{1,0:T(8,128)S(1)}, f32[12,512]{1,0:T(8,128)S(1)}, u32[]{:S(2)}, u32[]{:S(2)}) %collective-permute-start.15) | collective-permute-done | bytes 24608 | tf_op jit(solution)/shard_map/ppermute | solution.py:21
  254.5 4.5 %collective-permute-start.17 = (bf16[128,512]{1,0:T(8,128)(2,1)S(1)}, bf16[128,512]{1,0:T(8,128)(2,1)S(1)}, u32[]{:S(2)}, u32[]{:S(2)}) collective-permute-start(bf16[128,512]{1,0:T(8,128)(2,1)S(1)} %convert_element_type.63), channel_id=1, source_target_pairs={{0,16},{16,0},{1,17},{17,1},{2,18},{18,2},{3,19},{19,3},{4,20},{20... | collective-permute-start | bytes 393224 | tf_op jit(solution)/shard_map/ppermute | solution.py:21
  258.9 4.8 %collective-permute-done.17 = bf16[128,512]{1,0:T(8,128)(2,1)S(1)} collective-permute-done((bf16[128,512]{1,0:T(8,128)(2,1)S(1)}, bf16[128,512]{1,0:T(8,128)(2,1)S(1)}, u32[]{:S(2)}, u32[]{:S(2)}) %collective-permute-start.17) | collective-permute-done | bytes 131104 | tf_op jit(solution)/shard_map/ppermute | solution.py:21
  264.8 3.7 %all-to-all-start.7 = ((bf16[8,128,512]{2,1,0:T(8,128)(2,1)}), bf16[8,128,512]{2,1,0:T(8,128)(2,1)S(1)}, u32[]{:S(2)}, u32[]{:S(2)}) async-start(bf16[8,128,512]{2,1,0:T(8,128)(2,1)} %broadcast_in_dim.9), calls=%async_computation.7 | async-start | bytes 2097152 | tf_op jit(solution)/shard_map/all_to_all | solution.py:25
  268.5 2.4 collective-permute-start.22
  270.9 2.1 collective-permute-start.20
  273.0 1.5 collective-permute-start.21
  274.5 1.4 convert_add_fusion.1
  276.0 1.8 collective-permute-done.20
  278.9 6.3 %collective-permute-done.22 = bf16[256,512]{1,0:T(8,128)(2,1)S(1)} collective-permute-done((bf16[256,512]{1,0:T(8,128)(2,1)S(1)}, bf16[256,512]{1,0:T(8,128)(2,1)S(1)}, u32[]{:S(2)}, u32[]{:S(2)}) %collective-permute-start.22) | collective-permute-done | bytes 262176 | tf_op jit(solution)/shard_map/ppermute | solution.py:21
  286.4 3.0 %all-to-all-done.7 = bf16[8,128,512]{2,1,0:T(8,128)(2,1)S(1)} async-done(((bf16[8,128,512]{2,1,0:T(8,128)(2,1)}), bf16[8,128,512]{2,1,0:T(8,128)(2,1)S(1)}, u32[]{:S(2)}, u32[]{:S(2)}) %all-to-all-start.7) | async-done | bytes 1048608 | tf_op jit(solution)/shard_map/all_to_all | solution.py:25
  289.4 1.3 copy.36
  292.3 2.1 slice_bitcast_fusion
  (84 shorter events, 18.8 us)
Async XLA Ops:
  0.6 13.2 %copy-start.8 = (s32[7,144,2]{1,2,0:T(2,128)S(1)}, s32[7,144,2]{1,2,0:T(2,128)}, u32[]{:S(2)}) copy-start(s32[7,144,2]{1,2,0:T(2,128)} %param.19) | copy-start | bytes 24196
  4.0 44.5 %collective-permute-start = (bf16[1024,512]{1,0:T(8,128)(2,1)}, bf16[1024,512]{1,0:T(8,128)(2,1)}, u32[]{:S(2)}, u32[]{:S(2)}) collective-permute-start(bf16[1024,512]{1,0:T(8,128)(2,1)} %pad_maximum_fusion.1), channel_id=1, source_target_pairs={{0,16},{10,26},{18,2},{24,8},{1,17},{11,27},{19,3},{25,9},{4,20},{... | collective-permute-start | bytes 3145736 | tf_op jit(solution)/shard_map/ppermute | solution.py:504
  10.9 37.6 %collective-permute-start.1 = (bf16[1024,512]{1,0:T(8,128)(2,1)}, bf16[1024,512]{1,0:T(8,128)(2,1)S(1)}, u32[]{:S(2)}, u32[]{:S(2)}) collective-permute-start(bf16[1024,512]{1,0:T(8,128)(2,1)} %pad_maximum_fusion.1), channel_id=1, source_target_pairs={{2,0},{8,10},{16,18},{26,24},{3,1},{9,11},{17,19},{27,25},{6,4},{1... | collective-permute-start | bytes 3145736 | tf_op jit(solution)/shard_map/ppermute | solution.py:504
  12.2 36.3 %collective-permute-start.2 = (bf16[1024,512]{1,0:T(8,128)(2,1)}, bf16[1024,512]{1,0:T(8,128)(2,1)}, u32[]{:S(2)}, u32[]{:S(2)}) collective-permute-start(bf16[1024,512]{1,0:T(8,128)(2,1)} %pad_maximum_fusion.1), channel_id=1, source_target_pairs={{2,16},{8,26},{16,2},{26,8},{3,17},{9,27},{17,3},{27,9},{6,20},{12... | collective-permute-start | bytes 3145736 | tf_op jit(solution)/shard_map/ppermute | solution.py:504
  20.1 6.7 %copy-start.9 = (bf16[512,8]{0,1:T(8,128)(2,1)S(1)}, bf16[512,8]{0,1:T(8,128)(2,1)}, u32[]{:S(2)}) copy-start(bf16[512,8]{0,1:T(8,128)(2,1)} %param.29) | copy-start | bytes 24580
  20.1 42.3 %all-to-all-start = ((bf16[8,128,512]{2,1,0:T(8,128)(2,1)}), bf16[8,128,512]{2,1,0:T(8,128)(2,1)S(1)}, u32[]{:S(2)}, u32[]{:S(2)}) async-start(bf16[8,128,512]{2,1,0:T(8,128)(2,1)} %get-tuple-element.89), calls=%async_computation | async-start | bytes 2097152 | tf_op jit(solution)/shard_map/all_to_all | solution.py:25
  48.5 18.1 %copy-start.1 = (bf16[1,512,512]{2,1,0:T(8,128)(2,1)S(1)}, bf16[1,512,512]{2,1,0:T(8,128)(2,1)}, u32[]{:S(2)}) copy-start(bf16[1,512,512]{2,1,0:T(8,128)(2,1)} %param.31) | copy-start | bytes 1572868
  62.4 4.6 %copy-start.4 = (bf16[8,128,512]{2,1,0:T(8,128)(2,1)}, bf16[8,128,512]{2,1,0:T(8,128)(2,1)S(1)}, u32[]{:S(2)}) copy-start(bf16[8,128,512]{2,1,0:T(8,128)(2,1)S(1)} %all-to-all-done.refs_0_) | copy-start | bytes 3145732
  62.4 18.3 %all-to-all-start.1 = ((bf16[8,128,512]{2,1,0:T(8,128)(2,1)}), bf16[8,128,512]{2,1,0:T(8,128)(2,1)}, u32[]{:S(2)}, u32[]{:S(2)}) async-start(bf16[8,128,512]{2,1,0:T(8,128)(2,1)} %get-tuple-element.90), calls=%async_computation.1 | async-start | bytes 2097152 | tf_op jit(solution)/shard_map/all_to_all | solution.py:25
  66.9 1.0 copy-start.6
  66.9 2.7 collective-permute-start.3
  67.9 12.7 %copy-start.7 = (bf16[1024,512]{1,0:T(8,128)(2,1)}, bf16[1024,512]{1,0:T(8,128)(2,1)S(1)}, u32[]{:S(2)}) copy-start(bf16[1024,512]{1,0:T(8,128)(2,1)S(1)} %broadcast_select_fusion.refs_2_) | copy-start | bytes 3145732
  67.9 3.3 %collective-permute-start.4 = (bf16[1024,512]{1,0:T(8,128)(2,1)S(1)}, bf16[1024,512]{1,0:T(8,128)(2,1)S(1)}, u32[]{:S(2)}, u32[]{:S(2)}) collective-permute-start(bf16[1024,512]{1,0:T(8,128)(2,1)S(1)} %broadcast_select_fusion.refs_2_), channel_id=1, source_target_pairs={{0,1},{1,0},{2,3},{3,2},{4,5},{5,4},{6,7},{7,6},{8,9},{9,8},{10,11... | collective-permute-start | bytes 3145736 | tf_op jit(solution)/shard_map/ppermute | solution.py:21
  69.7 1.5 copy-start.10
  71.2 1.0 copy-start.11
  80.7 36.8 %all-to-all-start.3 = ((bf16[8,144,1024]{2,1,0:T(8,128)(2,1)}), bf16[8,144,1024]{2,1,0:T(8,128)(2,1)S(1)}, u32[]{:S(2)}, u32[]{:S(2)}) async-start(bf16[8,144,1024]{2,1,0:T(8,128)(2,1)} %get-tuple-element.101), calls=%async_computation.3 | async-start | bytes 4718592 | tf_op jit(solution)/shard_map/all_to_all | solution.py:25
  117.4 4.3 %copy-start = (bf16[8,144,1024]{2,1,0:T(8,128)(2,1)}, bf16[8,144,1024]{2,1,0:T(8,128)(2,1)S(1)}, u32[]{:S(2)}) copy-start(bf16[8,144,1024]{2,1,0:T(8,128)(2,1)S(1)} %all-to-all-done.3.x_ref) | copy-start | bytes 7077892
  117.4 24.2 %all-to-all-start.2 = ((bf16[8,128,512]{2,1,0:T(8,128)(2,1)}), bf16[8,128,512]{2,1,0:T(8,128)(2,1)S(1)}, u32[]{:S(2)}, u32[]{:S(2)}) async-start(bf16[8,128,512]{2,1,0:T(8,128)(2,1)} %get-tuple-element.100), calls=%async_computation.2 | async-start | bytes 2097152 | tf_op jit(solution)/shard_map/all_to_all | solution.py:25
  141.6 16.8 %copy-start.5 = (bf16[8,128,512]{2,1,0:T(8,128)(2,1)}, bf16[8,128,512]{2,1,0:T(8,128)(2,1)S(1)}, u32[]{:S(2)}) copy-start(bf16[8,128,512]{2,1,0:T(8,128)(2,1)S(1)} %all-to-all-done.2.back_a) | copy-start | bytes 3145732
  141.6 20.7 %all-to-all-start.4 = ((bf16[8,144,512]{2,1,0:T(8,128)(2,1)}), bf16[8,144,512]{2,1,0:T(8,128)(2,1)S(1)}, u32[]{:S(2)}, u32[]{:S(2)}) async-start(bf16[8,144,512]{2,1,0:T(8,128)(2,1)} %get-tuple-element.109), calls=%async_computation.4 | async-start | bytes 2359296 | tf_op jit(solution)/shard_map/all_to_all | solution.py:25
  158.4 9.5 %collective-permute-start.10 = (bf16[2,512,512]{2,1,0:T(8,128)(2,1)}, bf16[2,512,512]{2,1,0:T(8,128)(2,1)S(1)}, u32[]{:S(2)}, u32[]{:S(2)}) collective-permute-start(bf16[2,512,512]{2,1,0:T(8,128)(2,1)} %get-tuple-element.135), channel_id=1, source_target_pairs={{0,1},{1,0},{2,3},{3,2},{4,5},{5,4},{6,7},{7,6},{8,9},{9,8},{10,11... | collective-permute-start | bytes 3145736 | tf_op jit(solution)/shard_map/ppermute | solution.py:21
  158.5 9.5 %collective-permute-start.9 = (bf16[2,512,512]{2,1,0:T(8,128)(2,1)}, bf16[2,512,512]{2,1,0:T(8,128)(2,1)}, u32[]{:S(2)}, u32[]{:S(2)}) collective-permute-start(bf16[2,512,512]{2,1,0:T(8,128)(2,1)} %get-tuple-element.134), channel_id=1, source_target_pairs={{0,1},{1,0},{2,3},{3,2},{4,5},{5,4},{6,7},{7,6},{8,9},{9,8},{10,11... | collective-permute-start | bytes 3145736 | tf_op jit(solution)/shard_map/ppermute | solution.py:21
  162.3 1.0 copy-start.2
  163.3 45.6 %all-to-all-start.6 = ((bf16[8,272,512]{2,1,0:T(8,128)(2,1)}), bf16[8,272,512]{2,1,0:T(8,128)(2,1)}, u32[]{:S(2)}, u32[]{:S(2)}) async-start(bf16[8,272,512]{2,1,0:T(8,128)(2,1)} %get-tuple-element.145), calls=%async_computation.6 | async-start | bytes 4456448 | tf_op jit(solution)/shard_map/all_to_all | solution.py:25
  170.4 38.5 %collective-permute-start.11 = (bf16[768,512]{1,0:T(8,128)(2,1)S(1)}, bf16[768,512]{1,0:T(8,128)(2,1)}, u32[]{:S(2)}, u32[]{:S(2)}) collective-permute-start(bf16[768,512]{1,0:T(8,128)(2,1)S(1)} %slice_bitcast_fusion.6), channel_id=1, source_target_pairs={{0,2},{2,0},{1,3},{3,1},{4,6},{6,4},{5,7},{7,5},{8,10},{10,8},{9,1... | collective-permute-start | bytes 2359304 | tf_op jit(solution)/shard_map/ppermute | solution.py:21
  200.8 3.0 %copy-start.3 = (bf16[2,512,512]{2,1,0:T(8,128)(2,1)S(1)}, bf16[2,512,512]{2,1,0:T(8,128)(2,1)}, u32[]{:S(2)}) copy-start(bf16[2,512,512]{2,1,0:T(8,128)(2,1)} %get-tuple-element.124) | copy-start | bytes 3145732
  200.8 1.8 collective-permute-start.8
  200.9 2.1 collective-permute-start.7
  201.4 2.0 collective-permute-start.6
  201.5 2.3 collective-permute-start.5
  208.9 45.4 %all-to-all-start.5 = ((bf16[8,128,512]{2,1,0:T(8,128)(2,1)}), bf16[8,128,512]{2,1,0:T(8,128)(2,1)S(1)}, u32[]{:S(2)}, u32[]{:S(2)}) async-start(bf16[8,128,512]{2,1,0:T(8,128)(2,1)} %bitcast.22), calls=%async_computation.5 | async-start | bytes 2097152 | tf_op jit(solution)/shard_map/all_to_all | solution.py:25
  213.8 40.5 %collective-permute-start.12 = (bf16[768,512]{1,0:T(8,128)(2,1)S(1)}, bf16[768,512]{1,0:T(8,128)(2,1)}, u32[]{:S(2)}, u32[]{:S(2)}) collective-permute-start(bf16[768,512]{1,0:T(8,128)(2,1)S(1)} %broadcast_select_fusion.2), channel_id=1, source_target_pairs={{0,16},{16,0},{1,17},{17,1},{2,18},{18,2},{3,19},{19,3},{4,20},{20... | collective-permute-start | bytes 2359304 | tf_op jit(solution)/shard_map/ppermute | solution.py:21
  217.5 36.8 %collective-permute-start.13 = (bf16[256,512]{1,0:T(8,128)(2,1)S(1)}, bf16[256,512]{1,0:T(8,128)(2,1)S(1)}, u32[]{:S(2)}, u32[]{:S(2)}) collective-permute-start(bf16[256,512]{1,0:T(8,128)(2,1)S(1)} %slice_bitcast_fusion.8), channel_id=1, source_target_pairs={{0,2},{2,0},{1,3},{3,1},{4,6},{6,4},{5,7},{7,5},{8,10},{10,8},{9,1... | collective-permute-start | bytes 786440 | tf_op jit(solution)/shard_map/ppermute | solution.py:21
  230.3 13.6 %collective-permute-start.14 = (f32[12,512]{1,0:T(8,128)S(1)}, f32[12,512]{1,0:T(8,128)S(1)}, u32[]{:S(2)}, u32[]{:S(2)}) collective-permute-start(f32[12,512]{1,0:T(8,128)S(1)} %pad_maximum_fusion.3), channel_id=1, source_target_pairs={{0,8},{8,0},{16,24},{24,16},{1,9},{9,1},{17,25},{25,17},{2,10},{10... | collective-permute-start | bytes 73736 | tf_op jit(solution)/shard_map/ppermute | solution.py:21
  230.7 23.5 %collective-permute-start.15 = (f32[12,512]{1,0:T(8,128)S(1)}, f32[12,512]{1,0:T(8,128)S(1)}, u32[]{:S(2)}, u32[]{:S(2)}) collective-permute-start(f32[12,512]{1,0:T(8,128)S(1)} %pad_maximum_fusion.3), channel_id=1, source_target_pairs={{0,16},{8,24},{16,0},{24,8},{1,17},{9,25},{17,1},{25,9},{2,18},{10... | collective-permute-start | bytes 73736 | tf_op jit(solution)/shard_map/ppermute | solution.py:21
  230.8 23.5 %collective-permute-start.16 = (f32[12,512]{1,0:T(8,128)S(1)}, f32[12,512]{1,0:T(8,128)S(1)}, u32[]{:S(2)}, u32[]{:S(2)}) collective-permute-start(f32[12,512]{1,0:T(8,128)S(1)} %pad_maximum_fusion.3), channel_id=1, source_target_pairs={{0,24},{8,16},{16,8},{24,0},{1,25},{9,17},{17,9},{25,1},{2,26},{10... | collective-permute-start | bytes 73736 | tf_op jit(solution)/shard_map/ppermute | solution.py:21
  254.5 9.2 %collective-permute-start.17 = (bf16[128,512]{1,0:T(8,128)(2,1)S(1)}, bf16[128,512]{1,0:T(8,128)(2,1)S(1)}, u32[]{:S(2)}, u32[]{:S(2)}) collective-permute-start(bf16[128,512]{1,0:T(8,128)(2,1)S(1)} %convert_element_type.63), channel_id=1, source_target_pairs={{0,16},{16,0},{1,17},{17,1},{2,18},{18,2},{3,19},{19,3},{4,20},{20... | collective-permute-start | bytes 393224 | tf_op jit(solution)/shard_map/ppermute | solution.py:21
  264.8 24.6 %all-to-all-start.7 = ((bf16[8,128,512]{2,1,0:T(8,128)(2,1)}), bf16[8,128,512]{2,1,0:T(8,128)(2,1)S(1)}, u32[]{:S(2)}, u32[]{:S(2)}) async-start(bf16[8,128,512]{2,1,0:T(8,128)(2,1)} %broadcast_in_dim.9), calls=%async_computation.7 | async-start | bytes 2097152 | tf_op jit(solution)/shard_map/all_to_all | solution.py:25
  268.5 2.4 collective-permute-start.18
  268.5 16.6 %collective-permute-start.22 = (bf16[256,512]{1,0:T(8,128)(2,1)S(1)}, bf16[256,512]{1,0:T(8,128)(2,1)S(1)}, u32[]{:S(2)}, u32[]{:S(2)}) collective-permute-start(bf16[256,512]{1,0:T(8,128)(2,1)S(1)} %broadcast_select_fusion.3), channel_id=1, source_target_pairs={{0,16},{16,0},{1,17},{17,1},{2,18},{18,2},{3,19},{19,3},{4,20},{20... | collective-permute-start | bytes 786440 | tf_op jit(solution)/shard_map/ppermute | solution.py:21
  270.9 6.9 %collective-permute-start.20 = (f32[12,512]{1,0:T(8,128)S(1)}, f32[12,512]{1,0:T(8,128)S(1)}, u32[]{:S(2)}, u32[]{:S(2)}) collective-permute-start(f32[12,512]{1,0:T(8,128)S(1)} %add.45), channel_id=1, source_target_pairs={{0,4},{2,6},{4,0},{6,2},{1,5},{3,7},{5,1},{7,3},{8,12},{10,14},{12... | collective-permute-start | bytes 73736 | tf_op jit(solution)/shard_map/ppermute | solution.py:21
  273.0 5.9 %collective-permute-start.21 = (f32[12,512]{1,0:T(8,128)S(1)}, f32[12,512]{1,0:T(8,128)S(1)}, u32[]{:S(2)}, u32[]{:S(2)}) collective-permute-start(f32[12,512]{1,0:T(8,128)S(1)} %add.45), channel_id=1, source_target_pairs={{0,6},{2,4},{4,2},{6,0},{1,7},{3,5},{5,3},{7,1},{8,14},{10,12},{12... | collective-permute-start | bytes 73736 | tf_op jit(solution)/shard_map/ppermute | solution.py:21
  274.4 4.4 %collective-permute-start.19 = (f32[12,512]{1,0:T(8,128)S(1)}, f32[12,512]{1,0:T(8,128)S(1)}, u32[]{:S(2)}, u32[]{:S(2)}) collective-permute-start(f32[12,512]{1,0:T(8,128)S(1)} %add.45), channel_id=1, source_target_pairs={{0,2},{2,0},{4,6},{6,4},{1,3},{3,1},{5,7},{7,5},{8,10},{10,8},{12,... | collective-permute-start | bytes 73736 | tf_op jit(solution)/shard_map/ppermute | solution.py:21
  289.4 2.7 collective-permute-start.23

commit v5 on v4

--- a/solution.py
+++ b/solution.py
@@ -686,7 +686,7 @@
         came = [swap(g, "hl", half_h, half_h // 2) for g in grads_far]
         came = jnp.concatenate(came, axis=1)
         parts = fold_hl((grads_near.astype(F32) + came.astype(F32)).astype(BF))
-        cut = units * 48 // 32
+        cut = units * 44 // 32
         passed_one, passed_two = over_hh(parts[1, :cut]), over_hh(parts[1, cut:])
 
         def split(keep, passed):

time: 296 us -> 293 us (0.990)
  no operation moved by 1% of the time
where the time goes in v5:
time: 293 us; the launch traced here: 292 us
  Pallas kernels  127 us (43%)
  starting transfers between devices  71.1 us (24%)
  waiting for transfers between devices  68.5 us (23%)
  local copies, waits for them, and re-layouts  13.4 us (5%)
  other arithmetic  10.7 us (4%)
    pallas_call x4, Pallas kernels, call(): pl.pallas_call(functools.partial(kernel, **names) if names else kernel, o...  40.3 us
    pallas_call x2, Pallas kernels, serve(): pl.pallas_call(functools.partial(expert_kernel, begin=begin), grid=(exper...  37.1 us
    all_to_all x8, starting transfers between devices, to_all(): return lax.all_to_all(blocks, axes, split_axis=0, concat_axis=0, tiled=True)  36 us
    all_to_all x8, waiting for transfers between devices, to_all(): return lax.all_to_all(blocks, axes, split_axis=0, concat_axis=0, tiled=True)  35.3 us
    ppermute x21, waiting for transfers between devices, swap(): return lax.ppermute(value, axis, [(i, i ^ flip) for i in range(size)])  33.3 us
    ppermute x21, starting transfers between devices, swap(): return lax.ppermute(value, axis, [(i, i ^ flip) for i in range(size)])  25.2 us
    pallas_call x2, Pallas kernels, weight_grads(): pl.pallas_call(kernel, grid=(hidden,), out_shape=[jax.ShapeDtypeStruct((n...  20.8 us
    pallas_call x1, Pallas kernels, on_device(): pl.pallas_call(functools.partial(combine_kernel, experts=experts, stride=...  14.5 us
  transfers between devices with their start and end apart: 32, of which 19 were waited for; matrix products, arithmetic and copies ran while one was open for 5% of the time, Pallas kernels for 43%

profile of v5, /device:TPU:0, one launch (start us, length us, event | category | flops | bytes accessed | tf_op | source)
XLA Modules:
  0.0 291.6 jit_solution(15036658181352020784)
XLA Ops:
  0.7 1.3 copy.35
  1.9 2.1 pad_maximum_fusion.1
  4.0 6.9 %collective-permute-start = (bf16[1024,512]{1,0:T(8,128)(2,1)}, bf16[1024,512]{1,0:T(8,128)(2,1)}, u32[]{:S(2)}, u32[]{:S(2)}) collective-permute-start(bf16[1024,512]{1,0:T(8,128)(2,1)} %pad_maximum_fusion.1), channel_id=1, source_target_pairs={{0,16},{10,26},{18,2},{24,8},{1,17},{11,27},{19,3},{25,9},{4,20},{... | collective-permute-start | bytes 3145736 | tf_op jit(solution)/shard_map/ppermute | solution.py:504
  10.9 1.3 collective-permute-start.1
  12.2 1.7 collective-permute-start.2
  14.6 5.5 %route_kernel.1 = (s32[1008,128]{1,0:T(8,128)}, s32[8,1008]{1,0:T(8,128)}, bf16[8,128,512]{2,1,0:T(8,128)(2,1)}) custom-call(s32[7]{0:T(128)} %len_ref.3, s32[1,1008]{1,0:T(1,128)} %pri_ref.1, s32[2,1008]{1,0:T(2,128)} %bitcast.80, bf16[1008,512]{1,0:T(8,128)(2,1)} %bitcast.88), custom_call_target="tpu_custom_call" | custom-call | flops 7699999744 | bytes 23800000 | tf_op jit(solution)/shard_map/route_kernel/pallas_call | solution.py:481
  20.1 6.7 %all-to-all-start = ((bf16[8,128,512]{2,1,0:T(8,128)(2,1)}), bf16[8,128,512]{2,1,0:T(8,128)(2,1)S(1)}, u32[]{:S(2)}, u32[]{:S(2)}) async-start(bf16[8,128,512]{2,1,0:T(8,128)(2,1)} %get-tuple-element.89), calls=%async_computation | async-start | bytes 2097152 | tf_op jit(solution)/shard_map/all_to_all | solution.py:25
  27.6 20.9 %forward_kernel.1 = (bf16[1008,512]{1,0:T(8,128)(2,1)}, bf16[1008,512]{1,0:T(8,128)(2,1)}, bf16[1008,512]{1,0:T(8,128)(2,1)}, bf16[1008,512]{1,0:T(8,128)(2,1)},...) custom-call(s32[7]{0:T(128)} %len_ref.3, ...), custom_call_target="tpu_custom_call" | custom-call | flops 20899999744 | bytes 64600000 | tf_op jit(solution)/shard_map/forward_kernel/pallas_call | solution.py:481
  48.5 13.8 %all-to-all-done.refs_0_ = bf16[8,128,512]{2,1,0:T(8,128)(2,1)S(1)} async-done(((bf16[8,128,512]{2,1,0:T(8,128)(2,1)}), bf16[8,128,512]{2,1,0:T(8,128)(2,1)S(1)}, u32[]{:S(2)}, u32[]{:S(2)}) %all-to-all-start) | async-done | bytes 1048608 | tf_op jit(solution)/shard_map/all_to_all | solution.py:25
  62.4 4.2 %all-to-all-start.1 = ((bf16[8,128,512]{2,1,0:T(8,128)(2,1)}), bf16[8,128,512]{2,1,0:T(8,128)(2,1)}, u32[]{:S(2)}, u32[]{:S(2)}) async-start(bf16[8,128,512]{2,1,0:T(8,128)(2,1)} %get-tuple-element.90), calls=%async_computation.1 | async-start | bytes 2097152 | tf_op jit(solution)/shard_map/all_to_all | solution.py:25
  67.9 1.8 collective-permute-done.3.refs_3_
  69.7 1.5 collective-permute-done.4.refs_4_
  72.1 8.5 %all-to-all-done.1.x_ref = bf16[8,128,512]{2,1,0:T(8,128)(2,1)} async-done(((bf16[8,128,512]{2,1,0:T(8,128)(2,1)}), bf16[8,128,512]{2,1,0:T(8,128)(2,1)}, u32[]{:S(2)}, u32[]{:S(2)}) %all-to-all-start.1) | async-done | bytes 1048608 | tf_op jit(solution)/shard_map/all_to_all | solution.py:25
  80.7 3.8 %all-to-all-start.3 = ((bf16[8,144,1024]{2,1,0:T(8,128)(2,1)}), bf16[8,144,1024]{2,1,0:T(8,128)(2,1)S(1)}, u32[]{:S(2)}, u32[]{:S(2)}) async-start(bf16[8,144,1024]{2,1,0:T(8,128)(2,1)} %get-tuple-element.101), calls=%async_computation.3 | async-start | bytes 4718592 | tf_op jit(solution)/shard_map/all_to_all | solution.py:25
  84.5 17.3 %expert_kernel.2 = (bf16[8,128,512]{2,1,0:T(8,128)(2,1)}, bf16[8,128,512]{2,1,0:T(8,128)(2,1)}, bf16[8,128,2048]{2,1,0:T(8,128)(2,1)}, bf16[8,128,2048]{2,1,0:T(8,128)(2,1)}, bf16[8,128,512]{2,1,0:T(8,128)(2,1)}) custom-call(bf16[8,128,512]{2,1,0:T(8,128)(2,1)} %all-to-all-done.1.x_ref, bf16[8,128,512]{2,1,0:T(8,128)(2,1)} %copy-done.4, ...), custom_call_target="tpu_custom_call" | custom-call | flops 23100000256 | bytes 71400000 | tf_op jit(solution)/shard_map/expert_kernel/pallas_call | solution.py:633
  101.7 9.1 %first_grad_kernel.1.first_ref = bf16[4,1024,512]{2,1,0:T(8,128)(2,1)} custom-call(bf16[1024,512]{1,0:T(8,128)(2,1)} %bitcast.11.x_ref, bf16[1024,2048]{1,0:T(8,128)(2,1)} %bitcast.98, bf16[1024,2048]{1,0:T(8,128)(2,1)} %bitcast.97, bf16[1024,512]{1,0:T(8,128)(2,1)} %bitcast.100), custom_call_target="tpu_custom_call" | custom-call | flops 9900000256 | bytes 30600000 | tf_op jit(solution)/shard_map/first_grad_kernel/pallas_call | solution.py:659
  110.9 6.6 %all-to-all-done.3.x_ref = bf16[8,144,1024]{2,1,0:T(8,128)(2,1)S(1)} async-done(((bf16[8,144,1024]{2,1,0:T(8,128)(2,1)}), bf16[8,144,1024]{2,1,0:T(8,128)(2,1)S(1)}, u32[]{:S(2)}, u32[]{:S(2)}) %all-to-all-start.3) | async-done | bytes 2359328 | tf_op jit(solution)/shard_map/all_to_all | solution.py:25
  117.4 4.3 %all-to-all-start.2 = ((bf16[8,128,512]{2,1,0:T(8,128)(2,1)}), bf16[8,128,512]{2,1,0:T(8,128)(2,1)S(1)}, u32[]{:S(2)}, u32[]{:S(2)}) async-start(bf16[8,128,512]{2,1,0:T(8,128)(2,1)} %get-tuple-element.100), calls=%async_computation.2 | async-start | bytes 2097152 | tf_op jit(solution)/shard_map/all_to_all | solution.py:25
  121.8 19.8 %expert_kernel.3 = (bf16[8,144,512]{2,1,0:T(8,128)(2,1)}, bf16[8,272,512]{2,1,0:T(8,128)(2,1)}, bf16[8,144,2048]{2,1,0:T(8,128)(2,1)}, bf16[8,144,2048]{2,1,0:T(8,128)(2,1)}, bf16[8,144,512]{2,1,0:T(8,128)(2,1)}) custom-call(bf16[8,144,1024]{2,1,0:T(8,128)(2,1)} %copy-done, bf16[8,128,512]{2,1,0:T(8,128)(2,1)} %get-tuple-element.106.refs_0_, ...), custom_call_target="tpu_custom_call" | custom-call | flops 23100000256 | bytes 71400000 | tf_op jit(solution)/shard_map/expert_kernel/pallas_call | solution.py:633
  141.6 5.1 %all-to-all-start.4 = ((bf16[8,144,512]{2,1,0:T(8,128)(2,1)}), bf16[8,144,512]{2,1,0:T(8,128)(2,1)S(1)}, u32[]{:S(2)}, u32[]{:S(2)}) async-start(bf16[8,144,512]{2,1,0:T(8,128)(2,1)} %get-tuple-element.109), calls=%async_computation.4 | async-start | bytes 2359296 | tf_op jit(solution)/shard_map/all_to_all | solution.py:25
  146.7 11.7 %second_grad_kernel.1 = (bf16[2,1024,512]{2,1,0:T(8,128)(2,1)}, bf16[2,512,512]{2,1,0:T(8,128)(2,1)}, bf16[2,512,512]{2,1,0:T(8,128)(2,1)}) custom-call(bf16[1152,1024]{1,0:T(8,128)(2,1)} %bitcast.73, bf16[1152,2048]{1,0:T(8,128)(2,1)} %bitcast.96, bf16[1152,2048]{1,0:T(8,128)(2,1)} %bitcast.95, bf16[1152,512]{1,0:T(8,128)(2,1)} %bitcast.99, ...), custom_call_target="tpu_custom_call" | custom-call | flops 9900000256 | bytes 30600000 | tf_op jit(solution)/shard_map/second_grad_kernel/pallas_call | solution.py:659
  159.0 3.4 %all-to-all-done.4.back_b = bf16[8,144,512]{2,1,0:T(8,128)(2,1)S(1)} async-done(((bf16[8,144,512]{2,1,0:T(8,128)(2,1)}), bf16[8,144,512]{2,1,0:T(8,128)(2,1)S(1)}, u32[]{:S(2)}, u32[]{:S(2)}) %all-to-all-start.4) | async-done | bytes 1179680 | tf_op jit(solution)/shard_map/all_to_all | solution.py:25
  163.3 4.6 %all-to-all-start.6 = ((bf16[8,272,512]{2,1,0:T(8,128)(2,1)}), bf16[8,272,512]{2,1,0:T(8,128)(2,1)}, u32[]{:S(2)}, u32[]{:S(2)}) async-start(bf16[8,272,512]{2,1,0:T(8,128)(2,1)} %get-tuple-element.145), calls=%async_computation.6 | async-start | bytes 4456448 | tf_op jit(solution)/shard_map/all_to_all | solution.py:25
  167.9 2.4 add_convert_fusion
  170.4 1.7 collective-permute-start.11
  172.2 14.5 %combine_kernel.1 = (f32[1008,512]{1,0:T(8,128)}, bf16[1008,512]{1,0:T(8,128)(2,1)}, bf16[512,512]{1,0:T(8,128)(2,1)}, f32[128,512]{1,0:T(8,128)}, f32[8,512]{1,0:T(8,128)}) custom-call(bf16[8,128,512]{2,1,0:T(8,128)(2,1)} %copy-done.5, bf16[8,144,512]{2,1,0:T(8,128)(2,1)} %copy-done.2, s32[1008,128]{1,0:T(8,128)} %get-tuple-element.112.col_ref, ...), custom_call_target="tpu_custom_call" | custom-call | flops 18699999232 | bytes 57800000 | tf_op jit(solution)/shard_map/combine_kernel/pallas_call | solution.py:707
  186.7 14.0 %attention_back_kernel.1 = (bf16[1008,512]{1,0:T(8,128)(2,1)}, bf16[1008,512]{1,0:T(8,128)(2,1)}, bf16[1008,512]{1,0:T(8,128)(2,1)}, bf16[2,512,512]{2,1,0:T(8,1...) custom-call(s32[1]{0:T(128)} %bitcast.side_ref, ...), custom_call_target="tpu_custom_call" | custom-call | flops 1100000000 | bytes 3400000 | tf_op jit(solution)/shard_map/attention_back_kernel/pallas_call | solution.py:722
  203.8 1.3 fusion
  205.1 2.4 collective-permute-done.11
  207.5 3.6 %all-to-all-start.5 = ((bf16[8,128,512]{2,1,0:T(8,128)(2,1)}), bf16[8,128,512]{2,1,0:T(8,128)(2,1)S(1)}, u32[]{:S(2)}, u32[]{:S(2)}) async-start(bf16[8,128,512]{2,1,0:T(8,128)(2,1)} %bitcast.22), calls=%async_computation.5 | async-start | bytes 2097152 | tf_op jit(solution)/shard_map/all_to_all | solution.py:25
  212.3 3.7 %collective-permute-start.12 = (bf16[704,512]{1,0:T(8,128)(2,1)S(1)}, bf16[704,512]{1,0:T(8,128)(2,1)}, u32[]{:S(2)}, u32[]{:S(2)}) collective-permute-start(bf16[704,512]{1,0:T(8,128)(2,1)S(1)} %broadcast_select_fusion.2), channel_id=1, source_target_pairs={{0,16},{16,0},{1,17},{17,1},{2,18},{18,2},{3,19},{19,3},{4,20},{20... | collective-permute-start | bytes 2162696 | tf_op jit(solution)/shard_map/ppermute | solution.py:21
  216.1 3.2 %collective-permute-start.13 = (bf16[320,512]{1,0:T(8,128)(2,1)S(1)}, bf16[320,512]{1,0:T(8,128)(2,1)S(1)}, u32[]{:S(2)}, u32[]{:S(2)}) collective-permute-start(bf16[320,512]{1,0:T(8,128)(2,1)S(1)} %slice_bitcast_fusion.8), channel_id=1, source_target_pairs={{0,2},{2,0},{1,3},{3,1},{4,6},{6,4},{5,7},{7,5},{8,10},{10,8},{9,1... | collective-permute-start | bytes 983048 | tf_op jit(solution)/shard_map/ppermute | solution.py:21
  220.7 7.5 %image_kernel.1 = (f32[1008,512]{1,0:T(8,128)}, f32[8,512]{1,0:T(8,128)}) custom-call(bf16[1008,512]{1,0:T(8,128)(2,1)} %get-tuple-element.138.gq_ref, bf16[1008,512]{1,0:T(8,128)(2,1)} %get-tuple-element.139.gk_ref, bf16[1008,512]{1,0:T(8,128)(2,1)} %get-tuple-element.140.gv_ref, bf16[512,512]{1,0:T(8,128)(2,1)} %wq_ref.3, bf16[512,512]{1,0:T(8,128)(2,1)} %wk_ref.3, ...), custom_call_target="tpu_custom_call" | custom-call | flops 1100000000 | bytes 3400000 | tf_op jit(solution)/shard_map/image_kernel/pallas_call | solution.py:481
  229.4 4.0 %collective-permute-start.16 = (f32[12,512]{1,0:T(8,128)S(1)}, f32[12,512]{1,0:T(8,128)S(1)}, u32[]{:S(2)}, u32[]{:S(2)}) collective-permute-start(f32[12,512]{1,0:T(8,128)S(1)} %pad_maximum_fusion.3), channel_id=1, source_target_pairs={{0,24},{8,16},{16,8},{24,0},{1,25},{9,17},{17,9},{25,1},{2,26},{10... | collective-permute-start | bytes 73736 | tf_op jit(solution)/shard_map/ppermute | solution.py:21
  233.4 6.5 %output_kernel.1 = bf16[1008,512]{1,0:T(8,128)(2,1)} custom-call(s32[1008,128]{1,0:T(8,128)} %get-tuple-element.112.col_ref, f32[1008,512]{1,0:T(8,128)} %get-tuple-element.114.residual_ref, bf16[2176,512]{1,0:T(8,128)(2,1)} %bitcast.25.res_ref), custom_call_target="tpu_custom_call" | custom-call | flops 1100000000 | bytes 3400000 | tf_op jit(solution)/shard_map/output_kernel/pallas_call | solution.py:481
  241.1 9.0 %collective-permute-done.15 = f32[12,512]{1,0:T(8,128)S(1)} collective-permute-done((f32[12,512]{1,0:T(8,128)S(1)}, f32[12,512]{1,0:T(8,128)S(1)}, u32[]{:S(2)}, u32[]{:S(2)}) %collective-permute-start.15) | collective-permute-done | bytes 24608 | tf_op jit(solution)/shard_map/ppermute | solution.py:21
  250.3 4.4 %collective-permute-start.17 = (bf16[128,512]{1,0:T(8,128)(2,1)S(1)}, bf16[128,512]{1,0:T(8,128)(2,1)S(1)}, u32[]{:S(2)}, u32[]{:S(2)}) collective-permute-start(bf16[128,512]{1,0:T(8,128)(2,1)S(1)} %convert_element_type.63), channel_id=1, source_target_pairs={{0,16},{16,0},{1,17},{17,1},{2,18},{18,2},{3,19},{19,3},{4,20},{20... | collective-permute-start | bytes 393224 | tf_op jit(solution)/shard_map/ppermute | solution.py:21
  254.7 4.8 %collective-permute-done.17 = bf16[128,512]{1,0:T(8,128)(2,1)S(1)} collective-permute-done((bf16[128,512]{1,0:T(8,128)(2,1)S(1)}, bf16[128,512]{1,0:T(8,128)(2,1)S(1)}, u32[]{:S(2)}, u32[]{:S(2)}) %collective-permute-start.17) | collective-permute-done | bytes 131104 | tf_op jit(solution)/shard_map/ppermute | solution.py:21
  260.6 3.7 %all-to-all-start.7 = ((bf16[8,128,512]{2,1,0:T(8,128)(2,1)}), bf16[8,128,512]{2,1,0:T(8,128)(2,1)S(1)}, u32[]{:S(2)}, u32[]{:S(2)}) async-start(bf16[8,128,512]{2,1,0:T(8,128)(2,1)} %broadcast_in_dim.9), calls=%async_computation.7 | async-start | bytes 2097152 | tf_op jit(solution)/shard_map/all_to_all | solution.py:25
  264.3 2.4 collective-permute-start.22
  266.7 2.1 collective-permute-start.20
  268.7 1.5 collective-permute-start.21
  270.3 1.4 convert_add_fusion.1
  271.7 1.9 collective-permute-done.20
  274.3 8.1 %collective-permute-done.22 = bf16[320,512]{1,0:T(8,128)(2,1)S(1)} collective-permute-done((bf16[320,512]{1,0:T(8,128)(2,1)S(1)}, bf16[320,512]{1,0:T(8,128)(2,1)S(1)}, u32[]{:S(2)}, u32[]{:S(2)}) %collective-permute-start.22) | collective-permute-done | bytes 327712 | tf_op jit(solution)/shard_map/ppermute | solution.py:21
  283.6 3.0 %all-to-all-done.7 = bf16[8,128,512]{2,1,0:T(8,128)(2,1)S(1)} async-done(((bf16[8,128,512]{2,1,0:T(8,128)(2,1)}), bf16[8,128,512]{2,1,0:T(8,128)(2,1)S(1)}, u32[]{:S(2)}, u32[]{:S(2)}) %all-to-all-start.7) | async-done | bytes 1048608 | tf_op jit(solution)/shard_map/all_to_all | solution.py:25
  286.6 1.3 copy.36
  289.5 2.1 slice_bitcast_fusion
  (84 shorter events, 18.5 us)
Async XLA Ops:
  0.6 13.2 %copy-start.8 = (s32[7,144,2]{1,2,0:T(2,128)S(1)}, s32[7,144,2]{1,2,0:T(2,128)}, u32[]{:S(2)}) copy-start(s32[7,144,2]{1,2,0:T(2,128)} %param.19) | copy-start | bytes 24196
  4.0 44.5 %collective-permute-start = (bf16[1024,512]{1,0:T(8,128)(2,1)}, bf16[1024,512]{1,0:T(8,128)(2,1)}, u32[]{:S(2)}, u32[]{:S(2)}) collective-permute-start(bf16[1024,512]{1,0:T(8,128)(2,1)} %pad_maximum_fusion.1), channel_id=1, source_target_pairs={{0,16},{10,26},{18,2},{24,8},{1,17},{11,27},{19,3},{25,9},{4,20},{... | collective-permute-start | bytes 3145736 | tf_op jit(solution)/shard_map/ppermute | solution.py:504
  10.9 37.6 %collective-permute-start.1 = (bf16[1024,512]{1,0:T(8,128)(2,1)}, bf16[1024,512]{1,0:T(8,128)(2,1)S(1)}, u32[]{:S(2)}, u32[]{:S(2)}) collective-permute-start(bf16[1024,512]{1,0:T(8,128)(2,1)} %pad_maximum_fusion.1), channel_id=1, source_target_pairs={{2,0},{8,10},{16,18},{26,24},{3,1},{9,11},{17,19},{27,25},{6,4},{1... | collective-permute-start | bytes 3145736 | tf_op jit(solution)/shard_map/ppermute | solution.py:504
  12.2 36.3 %collective-permute-start.2 = (bf16[1024,512]{1,0:T(8,128)(2,1)}, bf16[1024,512]{1,0:T(8,128)(2,1)}, u32[]{:S(2)}, u32[]{:S(2)}) collective-permute-start(bf16[1024,512]{1,0:T(8,128)(2,1)} %pad_maximum_fusion.1), channel_id=1, source_target_pairs={{2,16},{8,26},{16,2},{26,8},{3,17},{9,27},{17,3},{27,9},{6,20},{12... | collective-permute-start | bytes 3145736 | tf_op jit(solution)/shard_map/ppermute | solution.py:504
  20.1 6.7 %copy-start.9 = (bf16[512,8]{0,1:T(8,128)(2,1)S(1)}, bf16[512,8]{0,1:T(8,128)(2,1)}, u32[]{:S(2)}) copy-start(bf16[512,8]{0,1:T(8,128)(2,1)} %param.29) | copy-start | bytes 24580
  20.1 42.3 %all-to-all-start = ((bf16[8,128,512]{2,1,0:T(8,128)(2,1)}), bf16[8,128,512]{2,1,0:T(8,128)(2,1)S(1)}, u32[]{:S(2)}, u32[]{:S(2)}) async-start(bf16[8,128,512]{2,1,0:T(8,128)(2,1)} %get-tuple-element.89), calls=%async_computation | async-start | bytes 2097152 | tf_op jit(solution)/shard_map/all_to_all | solution.py:25
  48.5 18.1 %copy-start.1 = (bf16[1,512,512]{2,1,0:T(8,128)(2,1)S(1)}, bf16[1,512,512]{2,1,0:T(8,128)(2,1)}, u32[]{:S(2)}) copy-start(bf16[1,512,512]{2,1,0:T(8,128)(2,1)} %param.31) | copy-start | bytes 1572868
  62.4 4.6 %copy-start.4 = (bf16[8,128,512]{2,1,0:T(8,128)(2,1)}, bf16[8,128,512]{2,1,0:T(8,128)(2,1)S(1)}, u32[]{:S(2)}) copy-start(bf16[8,128,512]{2,1,0:T(8,128)(2,1)S(1)} %all-to-all-done.refs_0_) | copy-start | bytes 3145732
  62.4 18.3 %all-to-all-start.1 = ((bf16[8,128,512]{2,1,0:T(8,128)(2,1)}), bf16[8,128,512]{2,1,0:T(8,128)(2,1)}, u32[]{:S(2)}, u32[]{:S(2)}) async-start(bf16[8,128,512]{2,1,0:T(8,128)(2,1)} %get-tuple-element.90), calls=%async_computation.1 | async-start | bytes 2097152 | tf_op jit(solution)/shard_map/all_to_all | solution.py:25
  66.9 1.0 copy-start.6
  66.9 2.7 collective-permute-start.3
  67.9 12.7 %copy-start.7 = (bf16[1024,512]{1,0:T(8,128)(2,1)}, bf16[1024,512]{1,0:T(8,128)(2,1)S(1)}, u32[]{:S(2)}) copy-start(bf16[1024,512]{1,0:T(8,128)(2,1)S(1)} %broadcast_select_fusion.refs_2_) | copy-start | bytes 3145732
  67.9 3.3 %collective-permute-start.4 = (bf16[1024,512]{1,0:T(8,128)(2,1)S(1)}, bf16[1024,512]{1,0:T(8,128)(2,1)S(1)}, u32[]{:S(2)}, u32[]{:S(2)}) collective-permute-start(bf16[1024,512]{1,0:T(8,128)(2,1)S(1)} %broadcast_select_fusion.refs_2_), channel_id=1, source_target_pairs={{0,1},{1,0},{2,3},{3,2},{4,5},{5,4},{6,7},{7,6},{8,9},{9,8},{10,11... | collective-permute-start | bytes 3145736 | tf_op jit(solution)/shard_map/ppermute | solution.py:21
  69.7 1.5 copy-start.10
  71.2 1.0 copy-start.11
  80.7 36.8 %all-to-all-start.3 = ((bf16[8,144,1024]{2,1,0:T(8,128)(2,1)}), bf16[8,144,1024]{2,1,0:T(8,128)(2,1)S(1)}, u32[]{:S(2)}, u32[]{:S(2)}) async-start(bf16[8,144,1024]{2,1,0:T(8,128)(2,1)} %get-tuple-element.101), calls=%async_computation.3 | async-start | bytes 4718592 | tf_op jit(solution)/shard_map/all_to_all | solution.py:25
  117.4 4.3 %copy-start = (bf16[8,144,1024]{2,1,0:T(8,128)(2,1)}, bf16[8,144,1024]{2,1,0:T(8,128)(2,1)S(1)}, u32[]{:S(2)}) copy-start(bf16[8,144,1024]{2,1,0:T(8,128)(2,1)S(1)} %all-to-all-done.3.x_ref) | copy-start | bytes 7077892
  117.4 24.2 %all-to-all-start.2 = ((bf16[8,128,512]{2,1,0:T(8,128)(2,1)}), bf16[8,128,512]{2,1,0:T(8,128)(2,1)S(1)}, u32[]{:S(2)}, u32[]{:S(2)}) async-start(bf16[8,128,512]{2,1,0:T(8,128)(2,1)} %get-tuple-element.100), calls=%async_computation.2 | async-start | bytes 2097152 | tf_op jit(solution)/shard_map/all_to_all | solution.py:25
  141.6 16.8 %copy-start.5 = (bf16[8,128,512]{2,1,0:T(8,128)(2,1)}, bf16[8,128,512]{2,1,0:T(8,128)(2,1)S(1)}, u32[]{:S(2)}) copy-start(bf16[8,128,512]{2,1,0:T(8,128)(2,1)S(1)} %all-to-all-done.2.back_a) | copy-start | bytes 3145732
  141.6 20.7 %all-to-all-start.4 = ((bf16[8,144,512]{2,1,0:T(8,128)(2,1)}), bf16[8,144,512]{2,1,0:T(8,128)(2,1)S(1)}, u32[]{:S(2)}, u32[]{:S(2)}) async-start(bf16[8,144,512]{2,1,0:T(8,128)(2,1)} %get-tuple-element.109), calls=%async_computation.4 | async-start | bytes 2359296 | tf_op jit(solution)/shard_map/all_to_all | solution.py:25
  158.4 9.5 %collective-permute-start.10 = (bf16[2,512,512]{2,1,0:T(8,128)(2,1)}, bf16[2,512,512]{2,1,0:T(8,128)(2,1)S(1)}, u32[]{:S(2)}, u32[]{:S(2)}) collective-permute-start(bf16[2,512,512]{2,1,0:T(8,128)(2,1)} %get-tuple-element.135), channel_id=1, source_target_pairs={{0,1},{1,0},{2,3},{3,2},{4,5},{5,4},{6,7},{7,6},{8,9},{9,8},{10,11... | collective-permute-start | bytes 3145736 | tf_op jit(solution)/shard_map/ppermute | solution.py:21
  158.5 9.5 %collective-permute-start.9 = (bf16[2,512,512]{2,1,0:T(8,128)(2,1)}, bf16[2,512,512]{2,1,0:T(8,128)(2,1)}, u32[]{:S(2)}, u32[]{:S(2)}) collective-permute-start(bf16[2,512,512]{2,1,0:T(8,128)(2,1)} %get-tuple-element.134), channel_id=1, source_target_pairs={{0,1},{1,0},{2,3},{3,2},{4,5},{5,4},{6,7},{7,6},{8,9},{9,8},{10,11... | collective-permute-start | bytes 3145736 | tf_op jit(solution)/shard_map/ppermute | solution.py:21
  162.3 1.0 copy-start.2
  163.3 44.2 %all-to-all-start.6 = ((bf16[8,272,512]{2,1,0:T(8,128)(2,1)}), bf16[8,272,512]{2,1,0:T(8,128)(2,1)}, u32[]{:S(2)}, u32[]{:S(2)}) async-start(bf16[8,272,512]{2,1,0:T(8,128)(2,1)} %get-tuple-element.145), calls=%async_computation.6 | async-start | bytes 4456448 | tf_op jit(solution)/shard_map/all_to_all | solution.py:25
  170.4 37.1 %collective-permute-start.11 = (bf16[704,512]{1,0:T(8,128)(2,1)S(1)}, bf16[704,512]{1,0:T(8,128)(2,1)}, u32[]{:S(2)}, u32[]{:S(2)}) collective-permute-start(bf16[704,512]{1,0:T(8,128)(2,1)S(1)} %slice_bitcast_fusion.6), channel_id=1, source_target_pairs={{0,2},{2,0},{1,3},{3,1},{4,6},{6,4},{5,7},{7,5},{8,10},{10,8},{9,1... | collective-permute-start | bytes 2162696 | tf_op jit(solution)/shard_map/ppermute | solution.py:21
  200.8 3.0 %copy-start.3 = (bf16[2,512,512]{2,1,0:T(8,128)(2,1)S(1)}, bf16[2,512,512]{2,1,0:T(8,128)(2,1)}, u32[]{:S(2)}) copy-start(bf16[2,512,512]{2,1,0:T(8,128)(2,1)} %get-tuple-element.124) | copy-start | bytes 3145732
  200.8 1.8 collective-permute-start.8
  200.9 2.1 collective-permute-start.7
  201.4 2.0 collective-permute-start.6
  201.4 2.3 collective-permute-start.5
  207.5 42.6 %all-to-all-start.5 = ((bf16[8,128,512]{2,1,0:T(8,128)(2,1)}), bf16[8,128,512]{2,1,0:T(8,128)(2,1)S(1)}, u32[]{:S(2)}, u32[]{:S(2)}) async-start(bf16[8,128,512]{2,1,0:T(8,128)(2,1)} %bitcast.22), calls=%async_computation.5 | async-start | bytes 2097152 | tf_op jit(solution)/shard_map/all_to_all | solution.py:25
  212.3 37.7 %collective-permute-start.12 = (bf16[704,512]{1,0:T(8,128)(2,1)S(1)}, bf16[704,512]{1,0:T(8,128)(2,1)}, u32[]{:S(2)}, u32[]{:S(2)}) collective-permute-start(bf16[704,512]{1,0:T(8,128)(2,1)S(1)} %broadcast_select_fusion.2), channel_id=1, source_target_pairs={{0,16},{16,0},{1,17},{17,1},{2,18},{18,2},{3,19},{19,3},{4,20},{20... | collective-permute-start | bytes 2162696 | tf_op jit(solution)/shard_map/ppermute | solution.py:21
  216.1 34.0 %collective-permute-start.13 = (bf16[320,512]{1,0:T(8,128)(2,1)S(1)}, bf16[320,512]{1,0:T(8,128)(2,1)S(1)}, u32[]{:S(2)}, u32[]{:S(2)}) collective-permute-start(bf16[320,512]{1,0:T(8,128)(2,1)S(1)} %slice_bitcast_fusion.8), channel_id=1, source_target_pairs={{0,2},{2,0},{1,3},{3,1},{4,6},{6,4},{5,7},{7,5},{8,10},{10,8},{9,1... | collective-permute-start | bytes 983048 | tf_op jit(solution)/shard_map/ppermute | solution.py:21
  228.9 12.2 %collective-permute-start.14 = (f32[12,512]{1,0:T(8,128)S(1)}, f32[12,512]{1,0:T(8,128)S(1)}, u32[]{:S(2)}, u32[]{:S(2)}) collective-permute-start(f32[12,512]{1,0:T(8,128)S(1)} %pad_maximum_fusion.3), channel_id=1, source_target_pairs={{0,8},{8,0},{16,24},{24,16},{1,9},{9,1},{17,25},{25,17},{2,10},{10... | collective-permute-start | bytes 73736 | tf_op jit(solution)/shard_map/ppermute | solution.py:21
  229.3 20.7 %collective-permute-start.15 = (f32[12,512]{1,0:T(8,128)S(1)}, f32[12,512]{1,0:T(8,128)S(1)}, u32[]{:S(2)}, u32[]{:S(2)}) collective-permute-start(f32[12,512]{1,0:T(8,128)S(1)} %pad_maximum_fusion.3), channel_id=1, source_target_pairs={{0,16},{8,24},{16,0},{24,8},{1,17},{9,25},{17,1},{25,9},{2,18},{10... | collective-permute-start | bytes 73736 | tf_op jit(solution)/shard_map/ppermute | solution.py:21
  229.4 20.7 %collective-permute-start.16 = (f32[12,512]{1,0:T(8,128)S(1)}, f32[12,512]{1,0:T(8,128)S(1)}, u32[]{:S(2)}, u32[]{:S(2)}) collective-permute-start(f32[12,512]{1,0:T(8,128)S(1)} %pad_maximum_fusion.3), channel_id=1, source_target_pairs={{0,24},{8,16},{16,8},{24,0},{1,25},{9,17},{17,9},{25,1},{2,26},{10... | collective-permute-start | bytes 73736 | tf_op jit(solution)/shard_map/ppermute | solution.py:21
  250.3 9.2 %collective-permute-start.17 = (bf16[128,512]{1,0:T(8,128)(2,1)S(1)}, bf16[128,512]{1,0:T(8,128)(2,1)S(1)}, u32[]{:S(2)}, u32[]{:S(2)}) collective-permute-start(bf16[128,512]{1,0:T(8,128)(2,1)S(1)} %convert_element_type.63), channel_id=1, source_target_pairs={{0,16},{16,0},{1,17},{17,1},{2,18},{18,2},{3,19},{19,3},{4,20},{20... | collective-permute-start | bytes 393224 | tf_op jit(solution)/shard_map/ppermute | solution.py:21
  260.6 26.0 %all-to-all-start.7 = ((bf16[8,128,512]{2,1,0:T(8,128)(2,1)}), bf16[8,128,512]{2,1,0:T(8,128)(2,1)S(1)}, u32[]{:S(2)}, u32[]{:S(2)}) async-start(bf16[8,128,512]{2,1,0:T(8,128)(2,1)} %broadcast_in_dim.9), calls=%async_computation.7 | async-start | bytes 2097152 | tf_op jit(solution)/shard_map/all_to_all | solution.py:25
  264.2 2.4 collective-permute-start.18
  264.3 18.0 %collective-permute-start.22 = (bf16[320,512]{1,0:T(8,128)(2,1)S(1)}, bf16[320,512]{1,0:T(8,128)(2,1)S(1)}, u32[]{:S(2)}, u32[]{:S(2)}) collective-permute-start(bf16[320,512]{1,0:T(8,128)(2,1)S(1)} %broadcast_select_fusion.3), channel_id=1, source_target_pairs={{0,16},{16,0},{1,17},{17,1},{2,18},{18,2},{3,19},{19,3},{4,20},{20... | collective-permute-start | bytes 983048 | tf_op jit(solution)/shard_map/ppermute | solution.py:21
  266.7 6.9 %collective-permute-start.20 = (f32[12,512]{1,0:T(8,128)S(1)}, f32[12,512]{1,0:T(8,128)S(1)}, u32[]{:S(2)}, u32[]{:S(2)}) collective-permute-start(f32[12,512]{1,0:T(8,128)S(1)} %add.45), channel_id=1, source_target_pairs={{0,4},{2,6},{4,0},{6,2},{1,5},{3,7},{5,1},{7,3},{8,12},{10,14},{12... | collective-permute-start | bytes 73736 | tf_op jit(solution)/shard_map/ppermute | solution.py:21
  268.7 5.5 %collective-permute-start.21 = (f32[12,512]{1,0:T(8,128)S(1)}, f32[12,512]{1,0:T(8,128)S(1)}, u32[]{:S(2)}, u32[]{:S(2)}) collective-permute-start(f32[12,512]{1,0:T(8,128)S(1)} %add.45), channel_id=1, source_target_pairs={{0,6},{2,4},{4,2},{6,0},{1,7},{3,5},{5,3},{7,1},{8,14},{10,12},{12... | collective-permute-start | bytes 73736 | tf_op jit(solution)/shard_map/ppermute | solution.py:21
  270.2 4.0 %collective-permute-start.19 = (f32[12,512]{1,0:T(8,128)S(1)}, f32[12,512]{1,0:T(8,128)S(1)}, u32[]{:S(2)}, u32[]{:S(2)}) collective-permute-start(f32[12,512]{1,0:T(8,128)S(1)} %add.45), channel_id=1, source_target_pairs={{0,2},{2,0},{4,6},{6,4},{1,3},{3,1},{5,7},{7,5},{8,10},{10,8},{12,... | collective-permute-start | bytes 73736 | tf_op jit(solution)/shard_map/ppermute | solution.py:21
  286.6 2.7 collective-permute-start.23

commit v6 on v5

--- a/solution.py
+++ b/solution.py
@@ -87,6 +87,12 @@
     slot = iota((count, rows), 0) + start
     hit = (targets[0:1, :] == slot) | (targets[1:2, :] == slot)
     return dot(jnp.where(hit, 1.0, 0.0).astype(BF), data)
+
+
+def pack_kernel(in_ref, out_ref, both_ref):
+    units = out_ref.shape[0]
+    both_ref[0:units, :] = jnp.transpose(in_ref[...])
+    both_ref[units:, :] = out_ref[...]
 
 
 def to_columns(row):
@@ -456,6 +462,7 @@
 
 
 LENGTH = {
+    "pack": 1,
     "route": 7,
     "forward": 19,
     "expert": 21,
@@ -575,7 +582,7 @@
         token_low = ((rows, width), BF)
         token_wide = ((rows, width), F32)
 
-        own = jnp.concatenate([w_expert_in[0].T, w_expert_out[0]])
+        (own,) = call(pack_kernel, [((2 * units, width), BF)], [w_expert_in[0], w_expert_out[0]])
         moved = [step(own, True, 1, 0), step(own, False, 0, 1), step(own, False, 1, 1)]
 
         cot = out_grad.reshape(rows, width)

time: 293 us -> 292 us (level)
    pallas_call x4 -> x5, Pallas kernels: 40.3 us -> 42.6 us  [call(): pl.pallas_call(functools.partial(kernel, **names) if names else kernel, o...]
  transfers between devices with their start and end apart: 32 -> 32, of which waited for: 19 -> 19; matrix products, arithmetic and copies ran while one was open for 5% -> 5% of each run, Pallas kernels for 43% -> 44%
where the time goes in v6:
time: 292 us; the launch traced here: 291 us
  Pallas kernels  129 us (44%)
  starting transfers between devices  71 us (24%)
  waiting for transfers between devices  69.8 us (24%)
  local copies, waits for them, and re-layouts  11.2 us (4%)
  other arithmetic  8.42 us (3%)
    pallas_call x5, Pallas kernels, call(): pl.pallas_call(functools.partial(kernel, **names) if names else kernel, o...  42.6 us
    pallas_call x2, Pallas kernels, serve(): pl.pallas_call(functools.partial(expert_kernel, begin=begin), grid=(exper...  37.1 us
    all_to_all x8, waiting for transfers between devices, to_all(): return lax.all_to_all(blocks, axes, split_axis=0, concat_axis=0, tiled=True)  36.5 us
    all_to_all x8, starting transfers between devices, to_all(): return lax.all_to_all(blocks, axes, split_axis=0, concat_axis=0, tiled=True)  35.9 us
    ppermute x21, waiting for transfers between devices, swap(): return lax.ppermute(value, axis, [(i, i ^ flip) for i in range(size)])  33.3 us
    ppermute x21, starting transfers between devices, swap(): return lax.ppermute(value, axis, [(i, i ^ flip) for i in range(size)])  25.2 us
    pallas_call x2, Pallas kernels, weight_grads(): pl.pallas_call(kernel, grid=(hidden,), out_shape=[jax.ShapeDtypeStruct((n...  20.8 us
    pallas_call x1, Pallas kernels, on_device(): pl.pallas_call(functools.partial(combine_kernel, experts=experts, stride=...  14.5 us
  transfers between devices with their start and end apart: 32, of which 19 were waited for; matrix products, arithmetic and copies ran while one was open for 5% of the time, Pallas kernels for 44%

profile of v6, /device:TPU:0, one launch (start us, length us, event | category | flops | bytes accessed | tf_op | source)
XLA Modules:
  0.0 290.6 jit_solution(10372068723856852505)
XLA Ops:
  0.7 2.4 pack_kernel.1
  3.0 6.9 %collective-permute-start = (bf16[1024,512]{1,0:T(8,128)(2,1)}, bf16[1024,512]{1,0:T(8,128)(2,1)}, u32[]{:S(2)}, u32[]{:S(2)}) collective-permute-start(bf16[1024,512]{1,0:T(8,128)(2,1)} %pack_kernel.1), channel_id=1, source_target_pairs={{0,16},{10,26},{18,2},{24,8},{1,17},{11,27},{19,3},{25,9},{4,20},{... | collective-permute-start | bytes 3145736 | tf_op jit(solution)/shard_map/ppermute | solution.py:511
  10.0 1.3 collective-permute-start.1
  11.2 1.7 collective-permute-start.2
  13.6 5.5 %route_kernel.1 = (s32[1008,128]{1,0:T(8,128)}, s32[8,1008]{1,0:T(8,128)}, bf16[8,128,512]{2,1,0:T(8,128)(2,1)}) custom-call(s32[7]{0:T(128)} %len_ref.3, s32[1,1008]{1,0:T(1,128)} %pri_ref.1, s32[2,1008]{1,0:T(2,128)} %bitcast.74, bf16[1008,512]{1,0:T(8,128)(2,1)} %bitcast.82), custom_call_target="tpu_custom_call" | custom-call | flops 7699999744 | bytes 23800000 | tf_op jit(solution)/shard_map/route_kernel/pallas_call | solution.py:488
  19.1 6.7 %all-to-all-start = ((bf16[8,128,512]{2,1,0:T(8,128)(2,1)}), bf16[8,128,512]{2,1,0:T(8,128)(2,1)S(1)}, u32[]{:S(2)}, u32[]{:S(2)}) async-start(bf16[8,128,512]{2,1,0:T(8,128)(2,1)} %get-tuple-element.89), calls=%async_computation | async-start | bytes 2097152 | tf_op jit(solution)/shard_map/all_to_all | solution.py:25
  26.6 20.9 %forward_kernel.1 = (bf16[1008,512]{1,0:T(8,128)(2,1)}, bf16[1008,512]{1,0:T(8,128)(2,1)}, bf16[1008,512]{1,0:T(8,128)(2,1)}, bf16[1008,512]{1,0:T(8,128)(2,1)},...) custom-call(s32[7]{0:T(128)} %len_ref.3, ...), custom_call_target="tpu_custom_call" | custom-call | flops 20899999744 | bytes 64600000 | tf_op jit(solution)/shard_map/forward_kernel/pallas_call | solution.py:488
  47.5 13.8 %all-to-all-done.refs_0_ = bf16[8,128,512]{2,1,0:T(8,128)(2,1)S(1)} async-done(((bf16[8,128,512]{2,1,0:T(8,128)(2,1)}), bf16[8,128,512]{2,1,0:T(8,128)(2,1)S(1)}, u32[]{:S(2)}, u32[]{:S(2)}) %all-to-all-start) | async-done | bytes 1048608 | tf_op jit(solution)/shard_map/all_to_all | solution.py:25
  61.4 4.2 %all-to-all-start.1 = ((bf16[8,128,512]{2,1,0:T(8,128)(2,1)}), bf16[8,128,512]{2,1,0:T(8,128)(2,1)}, u32[]{:S(2)}, u32[]{:S(2)}) async-start(bf16[8,128,512]{2,1,0:T(8,128)(2,1)} %get-tuple-element.90), calls=%async_computation.1 | async-start | bytes 2097152 | tf_op jit(solution)/shard_map/all_to_all | solution.py:25
  66.8 1.8 collective-permute-done.3.refs_3_
  68.5 1.5 collective-permute-done.4.refs_4_
  70.0 9.7 %all-to-all-done.1.x_ref = bf16[8,128,512]{2,1,0:T(8,128)(2,1)} async-done(((bf16[8,128,512]{2,1,0:T(8,128)(2,1)}), bf16[8,128,512]{2,1,0:T(8,128)(2,1)}, u32[]{:S(2)}, u32[]{:S(2)}) %all-to-all-start.1) | async-done | bytes 1048608 | tf_op jit(solution)/shard_map/all_to_all | solution.py:25
  79.7 3.8 %all-to-all-start.3 = ((bf16[8,144,1024]{2,1,0:T(8,128)(2,1)}), bf16[8,144,1024]{2,1,0:T(8,128)(2,1)S(1)}, u32[]{:S(2)}, u32[]{:S(2)}) async-start(bf16[8,144,1024]{2,1,0:T(8,128)(2,1)} %get-tuple-element.101), calls=%async_computation.3 | async-start | bytes 4718592 | tf_op jit(solution)/shard_map/all_to_all | solution.py:25
  83.5 17.3 %expert_kernel.2 = (bf16[8,128,512]{2,1,0:T(8,128)(2,1)}, bf16[8,128,512]{2,1,0:T(8,128)(2,1)}, bf16[8,128,2048]{2,1,0:T(8,128)(2,1)}, bf16[8,128,2048]{2,1,0:T(8,128)(2,1)}, bf16[8,128,512]{2,1,0:T(8,128)(2,1)}) custom-call(bf16[8,128,512]{2,1,0:T(8,128)(2,1)} %all-to-all-done.1.x_ref, bf16[8,128,512]{2,1,0:T(8,128)(2,1)} %copy-done.3, ...), custom_call_target="tpu_custom_call" | custom-call | flops 23100000256 | bytes 71400000 | tf_op jit(solution)/shard_map/expert_kernel/pallas_call | solution.py:640
  100.8 9.1 %first_grad_kernel.1.first_ref = bf16[4,1024,512]{2,1,0:T(8,128)(2,1)} custom-call(bf16[1024,512]{1,0:T(8,128)(2,1)} %bitcast.10.x_ref, bf16[1024,2048]{1,0:T(8,128)(2,1)} %bitcast.94, bf16[1024,2048]{1,0:T(8,128)(2,1)} %bitcast.93, bf16[1024,512]{1,0:T(8,128)(2,1)} %bitcast.96), custom_call_target="tpu_custom_call" | custom-call | flops 9900000256 | bytes 30600000 | tf_op jit(solution)/shard_map/first_grad_kernel/pallas_call | solution.py:666
  109.9 6.6 %all-to-all-done.3.x_ref = bf16[8,144,1024]{2,1,0:T(8,128)(2,1)S(1)} async-done(((bf16[8,144,1024]{2,1,0:T(8,128)(2,1)}), bf16[8,144,1024]{2,1,0:T(8,128)(2,1)S(1)}, u32[]{:S(2)}, u32[]{:S(2)}) %all-to-all-start.3) | async-done | bytes 2359328 | tf_op jit(solution)/shard_map/all_to_all | solution.py:25
  116.5 4.3 %all-to-all-start.2 = ((bf16[8,128,512]{2,1,0:T(8,128)(2,1)}), bf16[8,128,512]{2,1,0:T(8,128)(2,1)S(1)}, u32[]{:S(2)}, u32[]{:S(2)}) async-start(bf16[8,128,512]{2,1,0:T(8,128)(2,1)} %get-tuple-element.100), calls=%async_computation.2 | async-start | bytes 2097152 | tf_op jit(solution)/shard_map/all_to_all | solution.py:25
  120.8 19.8 %expert_kernel.3 = (bf16[8,144,512]{2,1,0:T(8,128)(2,1)}, bf16[8,272,512]{2,1,0:T(8,128)(2,1)}, bf16[8,144,2048]{2,1,0:T(8,128)(2,1)}, bf16[8,144,2048]{2,1,0:T(8,128)(2,1)}, bf16[8,144,512]{2,1,0:T(8,128)(2,1)}) custom-call(bf16[8,144,1024]{2,1,0:T(8,128)(2,1)} %copy-done, bf16[8,128,512]{2,1,0:T(8,128)(2,1)} %get-tuple-element.106.refs_0_, ...), custom_call_target="tpu_custom_call" | custom-call | flops 23100000256 | bytes 71400000 | tf_op jit(solution)/shard_map/expert_kernel/pallas_call | solution.py:640
  140.7 5.1 %all-to-all-start.4 = ((bf16[8,144,512]{2,1,0:T(8,128)(2,1)}), bf16[8,144,512]{2,1,0:T(8,128)(2,1)S(1)}, u32[]{:S(2)}, u32[]{:S(2)}) async-start(bf16[8,144,512]{2,1,0:T(8,128)(2,1)} %get-tuple-element.109), calls=%async_computation.4 | async-start | bytes 2359296 | tf_op jit(solution)/shard_map/all_to_all | solution.py:25
  145.7 11.7 %second_grad_kernel.1 = (bf16[2,1024,512]{2,1,0:T(8,128)(2,1)}, bf16[2,512,512]{2,1,0:T(8,128)(2,1)}, bf16[2,512,512]{2,1,0:T(8,128)(2,1)}) custom-call(bf16[1152,1024]{1,0:T(8,128)(2,1)} %bitcast.69, bf16[1152,2048]{1,0:T(8,128)(2,1)} %bitcast.92, bf16[1152,2048]{1,0:T(8,128)(2,1)} %bitcast.91, bf16[1152,512]{1,0:T(8,128)(2,1)} %bitcast.95, ...), custom_call_target="tpu_custom_call" | custom-call | flops 9900000256 | bytes 30600000 | tf_op jit(solution)/shard_map/second_grad_kernel/pallas_call | solution.py:666
  158.0 3.4 %all-to-all-done.4.back_b = bf16[8,144,512]{2,1,0:T(8,128)(2,1)S(1)} async-done(((bf16[8,144,512]{2,1,0:T(8,128)(2,1)}), bf16[8,144,512]{2,1,0:T(8,128)(2,1)S(1)}, u32[]{:S(2)}, u32[]{:S(2)}) %all-to-all-start.4) | async-done | bytes 1179680 | tf_op jit(solution)/shard_map/all_to_all | solution.py:25
  162.4 4.6 %all-to-all-start.6 = ((bf16[8,272,512]{2,1,0:T(8,128)(2,1)}), bf16[8,272,512]{2,1,0:T(8,128)(2,1)}, u32[]{:S(2)}, u32[]{:S(2)}) async-start(bf16[8,272,512]{2,1,0:T(8,128)(2,1)} %get-tuple-element.145), calls=%async_computation.6 | async-start | bytes 4456448 | tf_op jit(solution)/shard_map/all_to_all | solution.py:25
  167.0 2.4 add_convert_fusion
  169.5 1.7 collective-permute-start.11
  171.3 14.5 %combine_kernel.1 = (f32[1008,512]{1,0:T(8,128)}, bf16[1008,512]{1,0:T(8,128)(2,1)}, bf16[512,512]{1,0:T(8,128)(2,1)}, f32[128,512]{1,0:T(8,128)}, f32[8,512]{1,0:T(8,128)}) custom-call(bf16[8,128,512]{2,1,0:T(8,128)(2,1)} %copy-done.4, bf16[8,144,512]{2,1,0:T(8,128)(2,1)} %copy-done.1, s32[1008,128]{1,0:T(8,128)} %get-tuple-element.112.col_ref, ...), custom_call_target="tpu_custom_call" | custom-call | flops 18699999232 | bytes 57800000 | tf_op jit(solution)/shard_map/combine_kernel/pallas_call | solution.py:714
  185.8 14.0 %attention_back_kernel.1 = (bf16[1008,512]{1,0:T(8,128)(2,1)}, bf16[1008,512]{1,0:T(8,128)(2,1)}, bf16[1008,512]{1,0:T(8,128)(2,1)}, bf16[2,512,512]{2,1,0:T(8,1...) custom-call(s32[1]{0:T(128)} %bitcast.side_ref, ...), custom_call_target="tpu_custom_call" | custom-call | flops 1100000000 | bytes 3400000 | tf_op jit(solution)/shard_map/attention_back_kernel/pallas_call | solution.py:729
  202.9 1.3 fusion
  204.2 2.4 collective-permute-done.11
  206.6 3.6 %all-to-all-start.5 = ((bf16[8,128,512]{2,1,0:T(8,128)(2,1)}), bf16[8,128,512]{2,1,0:T(8,128)(2,1)S(1)}, u32[]{:S(2)}, u32[]{:S(2)}) async-start(bf16[8,128,512]{2,1,0:T(8,128)(2,1)} %bitcast.21), calls=%async_computation.5 | async-start | bytes 2097152 | tf_op jit(solution)/shard_map/all_to_all | solution.py:25
  211.4 3.7 %collective-permute-start.12 = (bf16[704,512]{1,0:T(8,128)(2,1)S(1)}, bf16[704,512]{1,0:T(8,128)(2,1)}, u32[]{:S(2)}, u32[]{:S(2)}) collective-permute-start(bf16[704,512]{1,0:T(8,128)(2,1)S(1)} %broadcast_select_fusion.2), channel_id=1, source_target_pairs={{0,16},{16,0},{1,17},{17,1},{2,18},{18,2},{3,19},{19,3},{4,20},{20... | collective-permute-start | bytes 2162696 | tf_op jit(solution)/shard_map/ppermute | solution.py:21
  215.1 3.2 %collective-permute-start.13 = (bf16[320,512]{1,0:T(8,128)(2,1)S(1)}, bf16[320,512]{1,0:T(8,128)(2,1)S(1)}, u32[]{:S(2)}, u32[]{:S(2)}) collective-permute-start(bf16[320,512]{1,0:T(8,128)(2,1)S(1)} %slice_bitcast_fusion.8), channel_id=1, source_target_pairs={{0,2},{2,0},{1,3},{3,1},{4,6},{6,4},{5,7},{7,5},{8,10},{10,8},{9,1... | collective-permute-start | bytes 983048 | tf_op jit(solution)/shard_map/ppermute | solution.py:21
  219.7 7.4 %image_kernel.1 = (f32[1008,512]{1,0:T(8,128)}, f32[8,512]{1,0:T(8,128)}) custom-call(bf16[1008,512]{1,0:T(8,128)(2,1)} %get-tuple-element.138.gq_ref, bf16[1008,512]{1,0:T(8,128)(2,1)} %get-tuple-element.139.gk_ref, bf16[1008,512]{1,0:T(8,128)(2,1)} %get-tuple-element.140.gv_ref, bf16[512,512]{1,0:T(8,128)(2,1)} %wq_ref.3, bf16[512,512]{1,0:T(8,128)(2,1)} %wk_ref.3, ...), custom_call_target="tpu_custom_call" | custom-call | flops 1100000000 | bytes 3400000 | tf_op jit(solution)/shard_map/image_kernel/pallas_call | solution.py:488
  228.3 4.0 %collective-permute-start.16 = (f32[12,512]{1,0:T(8,128)S(1)}, f32[12,512]{1,0:T(8,128)S(1)}, u32[]{:S(2)}, u32[]{:S(2)}) collective-permute-start(f32[12,512]{1,0:T(8,128)S(1)} %pad_maximum_fusion.2), channel_id=1, source_target_pairs={{0,24},{8,16},{16,8},{24,0},{1,25},{9,17},{17,9},{25,1},{2,26},{10... | collective-permute-start | bytes 73736 | tf_op jit(solution)/shard_map/ppermute | solution.py:21
  232.3 6.5 %output_kernel.1 = bf16[1008,512]{1,0:T(8,128)(2,1)} custom-call(s32[1008,128]{1,0:T(8,128)} %get-tuple-element.112.col_ref, f32[1008,512]{1,0:T(8,128)} %get-tuple-element.114.residual_ref, bf16[2176,512]{1,0:T(8,128)(2,1)} %bitcast.24.res_ref), custom_call_target="tpu_custom_call" | custom-call | flops 1100000000 | bytes 3400000 | tf_op jit(solution)/shard_map/output_kernel/pallas_call | solution.py:488
  238.8 1.4 collective-permute-done.14
  240.2 8.9 %collective-permute-done.15 = f32[12,512]{1,0:T(8,128)S(1)} collective-permute-done((f32[12,512]{1,0:T(8,128)S(1)}, f32[12,512]{1,0:T(8,128)S(1)}, u32[]{:S(2)}, u32[]{:S(2)}) %collective-permute-start.15) | collective-permute-done | bytes 24608 | tf_op jit(solution)/shard_map/ppermute | solution.py:21
  249.3 4.4 %collective-permute-start.17 = (bf16[128,512]{1,0:T(8,128)(2,1)S(1)}, bf16[128,512]{1,0:T(8,128)(2,1)S(1)}, u32[]{:S(2)}, u32[]{:S(2)}) collective-permute-start(bf16[128,512]{1,0:T(8,128)(2,1)S(1)} %convert_element_type.63), channel_id=1, source_target_pairs={{0,16},{16,0},{1,17},{17,1},{2,18},{18,2},{3,19},{19,3},{4,20},{20... | collective-permute-start | bytes 393224 | tf_op jit(solution)/shard_map/ppermute | solution.py:21
  253.7 4.8 %collective-permute-done.17 = bf16[128,512]{1,0:T(8,128)(2,1)S(1)} collective-permute-done((bf16[128,512]{1,0:T(8,128)(2,1)S(1)}, bf16[128,512]{1,0:T(8,128)(2,1)S(1)}, u32[]{:S(2)}, u32[]{:S(2)}) %collective-permute-start.17) | collective-permute-done | bytes 131104 | tf_op jit(solution)/shard_map/ppermute | solution.py:21
  259.6 3.7 %all-to-all-start.7 = ((bf16[8,128,512]{2,1,0:T(8,128)(2,1)}), bf16[8,128,512]{2,1,0:T(8,128)(2,1)S(1)}, u32[]{:S(2)}, u32[]{:S(2)}) async-start(bf16[8,128,512]{2,1,0:T(8,128)(2,1)} %broadcast_in_dim.9), calls=%async_computation.7 | async-start | bytes 2097152 | tf_op jit(solution)/shard_map/all_to_all | solution.py:25
  263.3 2.4 collective-permute-start.22
  265.7 2.1 collective-permute-start.20
  267.8 1.5 collective-permute-start.21
  269.3 1.4 convert_add_fusion.1
  270.7 1.9 collective-permute-done.20
  273.3 8.0 %collective-permute-done.22 = bf16[320,512]{1,0:T(8,128)(2,1)S(1)} collective-permute-done((bf16[320,512]{1,0:T(8,128)(2,1)S(1)}, bf16[320,512]{1,0:T(8,128)(2,1)S(1)}, u32[]{:S(2)}, u32[]{:S(2)}) %collective-permute-start.22) | collective-permute-done | bytes 327712 | tf_op jit(solution)/shard_map/ppermute | solution.py:21
  282.6 3.0 %all-to-all-done.7 = bf16[8,128,512]{2,1,0:T(8,128)(2,1)S(1)} async-done(((bf16[8,128,512]{2,1,0:T(8,128)(2,1)}), bf16[8,128,512]{2,1,0:T(8,128)(2,1)S(1)}, u32[]{:S(2)}, u32[]{:S(2)}) %all-to-all-start.7) | async-done | bytes 1048608 | tf_op jit(solution)/shard_map/all_to_all | solution.py:25
  285.6 1.3 copy.34
  288.5 2.1 slice_bitcast_fusion
  (83 shorter events, 16.1 us)
Async XLA Ops:
  0.6 12.3 %copy-start.8 = (s32[7,144,2]{1,2,0:T(2,128)S(1)}, s32[7,144,2]{1,2,0:T(2,128)}, u32[]{:S(2)}) copy-start(s32[7,144,2]{1,2,0:T(2,128)} %param.19) | copy-start | bytes 24196
  3.0 44.5 %collective-permute-start = (bf16[1024,512]{1,0:T(8,128)(2,1)}, bf16[1024,512]{1,0:T(8,128)(2,1)}, u32[]{:S(2)}, u32[]{:S(2)}) collective-permute-start(bf16[1024,512]{1,0:T(8,128)(2,1)} %pack_kernel.1), channel_id=1, source_target_pairs={{0,16},{10,26},{18,2},{24,8},{1,17},{11,27},{19,3},{25,9},{4,20},{... | collective-permute-start | bytes 3145736 | tf_op jit(solution)/shard_map/ppermute | solution.py:511
  10.0 37.6 %collective-permute-start.1 = (bf16[1024,512]{1,0:T(8,128)(2,1)}, bf16[1024,512]{1,0:T(8,128)(2,1)S(1)}, u32[]{:S(2)}, u32[]{:S(2)}) collective-permute-start(bf16[1024,512]{1,0:T(8,128)(2,1)} %pack_kernel.1), channel_id=1, source_target_pairs={{2,0},{8,10},{16,18},{26,24},{3,1},{9,11},{17,19},{27,25},{6,4},{1... | collective-permute-start | bytes 3145736 | tf_op jit(solution)/shard_map/ppermute | solution.py:511
  11.2 36.3 %collective-permute-start.2 = (bf16[1024,512]{1,0:T(8,128)(2,1)}, bf16[1024,512]{1,0:T(8,128)(2,1)}, u32[]{:S(2)}, u32[]{:S(2)}) collective-permute-start(bf16[1024,512]{1,0:T(8,128)(2,1)} %pack_kernel.1), channel_id=1, source_target_pairs={{2,16},{8,26},{16,2},{26,8},{3,17},{9,27},{17,3},{27,9},{6,20},{12... | collective-permute-start | bytes 3145736 | tf_op jit(solution)/shard_map/ppermute | solution.py:511
  19.1 6.7 %copy-start.9 = (bf16[512,8]{0,1:T(8,128)(2,1)S(1)}, bf16[512,8]{0,1:T(8,128)(2,1)}, u32[]{:S(2)}) copy-start(bf16[512,8]{0,1:T(8,128)(2,1)} %param.29) | copy-start | bytes 24580
  19.1 42.3 %all-to-all-start = ((bf16[8,128,512]{2,1,0:T(8,128)(2,1)}), bf16[8,128,512]{2,1,0:T(8,128)(2,1)S(1)}, u32[]{:S(2)}, u32[]{:S(2)}) async-start(bf16[8,128,512]{2,1,0:T(8,128)(2,1)} %get-tuple-element.89), calls=%async_computation | async-start | bytes 2097152 | tf_op jit(solution)/shard_map/all_to_all | solution.py:25
  47.5 18.1 %copy-start.5 = (bf16[1024,512]{1,0:T(8,128)(2,1)S(1)}, bf16[1024,512]{1,0:T(8,128)(2,1)}, u32[]{:S(2)}) copy-start(bf16[1024,512]{1,0:T(8,128)(2,1)} %pack_kernel.1) | copy-start | bytes 3145732
  61.4 4.4 %copy-start.3 = (bf16[8,128,512]{2,1,0:T(8,128)(2,1)}, bf16[8,128,512]{2,1,0:T(8,128)(2,1)S(1)}, u32[]{:S(2)}) copy-start(bf16[8,128,512]{2,1,0:T(8,128)(2,1)S(1)} %all-to-all-done.refs_0_) | copy-start | bytes 3145732
  61.4 18.3 %all-to-all-start.1 = ((bf16[8,128,512]{2,1,0:T(8,128)(2,1)}), bf16[8,128,512]{2,1,0:T(8,128)(2,1)}, u32[]{:S(2)}, u32[]{:S(2)}) async-start(bf16[8,128,512]{2,1,0:T(8,128)(2,1)} %get-tuple-element.90), calls=%async_computation.1 | async-start | bytes 2097152 | tf_op jit(solution)/shard_map/all_to_all | solution.py:25
  65.8 1.0 copy-start.6
  65.8 2.7 collective-permute-start.3
  66.8 1.8 copy-start.7
  66.8 3.3 %collective-permute-start.4 = (bf16[1024,512]{1,0:T(8,128)(2,1)S(1)}, bf16[1024,512]{1,0:T(8,128)(2,1)S(1)}, u32[]{:S(2)}, u32[]{:S(2)}) collective-permute-start(bf16[1024,512]{1,0:T(8,128)(2,1)S(1)} %broadcast_select_fusion.refs_2_), channel_id=1, source_target_pairs={{0,1},{1,0},{2,3},{3,2},{4,5},{5,4},{6,7},{7,6},{8,9},{9,8},{10,11... | collective-permute-start | bytes 3145736 | tf_op jit(solution)/shard_map/ppermute | solution.py:21
  68.5 11.2 %copy-start.10 = (bf16[1024,512]{1,0:T(8,128)(2,1)}, bf16[1024,512]{1,0:T(8,128)(2,1)S(1)}, u32[]{:S(2)}) copy-start(bf16[1024,512]{1,0:T(8,128)(2,1)S(1)} %collective-permute-done.3.refs_3_) | copy-start | bytes 3145732
  70.0 9.7 %copy-start.11 = (bf16[1024,512]{1,0:T(8,128)(2,1)}, bf16[1024,512]{1,0:T(8,128)(2,1)S(1)}, u32[]{:S(2)}) copy-start(bf16[1024,512]{1,0:T(8,128)(2,1)S(1)} %collective-permute-done.4.refs_4_) | copy-start | bytes 3145732
  79.7 36.8 %all-to-all-start.3 = ((bf16[8,144,1024]{2,1,0:T(8,128)(2,1)}), bf16[8,144,1024]{2,1,0:T(8,128)(2,1)S(1)}, u32[]{:S(2)}, u32[]{:S(2)}) async-start(bf16[8,144,1024]{2,1,0:T(8,128)(2,1)} %get-tuple-element.101), calls=%async_computation.3 | async-start | bytes 4718592 | tf_op jit(solution)/shard_map/all_to_all | solution.py:25
  116.5 4.3 %copy-start = (bf16[8,144,1024]{2,1,0:T(8,128)(2,1)}, bf16[8,144,1024]{2,1,0:T(8,128)(2,1)S(1)}, u32[]{:S(2)}) copy-start(bf16[8,144,1024]{2,1,0:T(8,128)(2,1)S(1)} %all-to-all-done.3.x_ref) | copy-start | bytes 7077892
  116.5 24.1 %all-to-all-start.2 = ((bf16[8,128,512]{2,1,0:T(8,128)(2,1)}), bf16[8,128,512]{2,1,0:T(8,128)(2,1)S(1)}, u32[]{:S(2)}, u32[]{:S(2)}) async-start(bf16[8,128,512]{2,1,0:T(8,128)(2,1)} %get-tuple-element.100), calls=%async_computation.2 | async-start | bytes 2097152 | tf_op jit(solution)/shard_map/all_to_all | solution.py:25
  140.7 16.8 %copy-start.4 = (bf16[8,128,512]{2,1,0:T(8,128)(2,1)}, bf16[8,128,512]{2,1,0:T(8,128)(2,1)S(1)}, u32[]{:S(2)}) copy-start(bf16[8,128,512]{2,1,0:T(8,128)(2,1)S(1)} %all-to-all-done.2.back_a) | copy-start | bytes 3145732
  140.7 20.7 %all-to-all-start.4 = ((bf16[8,144,512]{2,1,0:T(8,128)(2,1)}), bf16[8,144,512]{2,1,0:T(8,128)(2,1)S(1)}, u32[]{:S(2)}, u32[]{:S(2)}) async-start(bf16[8,144,512]{2,1,0:T(8,128)(2,1)} %get-tuple-element.109), calls=%async_computation.4 | async-start | bytes 2359296 | tf_op jit(solution)/shard_map/all_to_all | solution.py:25
  157.5 9.5 %collective-permute-start.10 = (bf16[2,512,512]{2,1,0:T(8,128)(2,1)}, bf16[2,512,512]{2,1,0:T(8,128)(2,1)S(1)}, u32[]{:S(2)}, u32[]{:S(2)}) collective-permute-start(bf16[2,512,512]{2,1,0:T(8,128)(2,1)} %get-tuple-element.135), channel_id=1, source_target_pairs={{0,1},{1,0},{2,3},{3,2},{4,5},{5,4},{6,7},{7,6},{8,9},{9,8},{10,11... | collective-permute-start | bytes 3145736 | tf_op jit(solution)/shard_map/ppermute | solution.py:21
  157.5 9.5 %collective-permute-start.9 = (bf16[2,512,512]{2,1,0:T(8,128)(2,1)}, bf16[2,512,512]{2,1,0:T(8,128)(2,1)}, u32[]{:S(2)}, u32[]{:S(2)}) collective-permute-start(bf16[2,512,512]{2,1,0:T(8,128)(2,1)} %get-tuple-element.134), channel_id=1, source_target_pairs={{0,1},{1,0},{2,3},{3,2},{4,5},{5,4},{6,7},{7,6},{8,9},{9,8},{10,11... | collective-permute-start | bytes 3145736 | tf_op jit(solution)/shard_map/ppermute | solution.py:21
  161.4 1.0 copy-start.1
  162.4 44.2 %all-to-all-start.6 = ((bf16[8,272,512]{2,1,0:T(8,128)(2,1)}), bf16[8,272,512]{2,1,0:T(8,128)(2,1)}, u32[]{:S(2)}, u32[]{:S(2)}) async-start(bf16[8,272,512]{2,1,0:T(8,128)(2,1)} %get-tuple-element.145), calls=%async_computation.6 | async-start | bytes 4456448 | tf_op jit(solution)/shard_map/all_to_all | solution.py:25
  169.5 37.0 %collective-permute-start.11 = (bf16[704,512]{1,0:T(8,128)(2,1)S(1)}, bf16[704,512]{1,0:T(8,128)(2,1)}, u32[]{:S(2)}, u32[]{:S(2)}) collective-permute-start(bf16[704,512]{1,0:T(8,128)(2,1)S(1)} %slice_bitcast_fusion.6), channel_id=1, source_target_pairs={{0,2},{2,0},{1,3},{3,1},{4,6},{6,4},{5,7},{7,5},{8,10},{10,8},{9,1... | collective-permute-start | bytes 2162696 | tf_op jit(solution)/shard_map/ppermute | solution.py:21
  199.9 3.0 %copy-start.2 = (bf16[2,512,512]{2,1,0:T(8,128)(2,1)S(1)}, bf16[2,512,512]{2,1,0:T(8,128)(2,1)}, u32[]{:S(2)}) copy-start(bf16[2,512,512]{2,1,0:T(8,128)(2,1)} %get-tuple-element.124) | copy-start | bytes 3145732
  199.9 1.8 collective-permute-start.8
  199.9 2.1 collective-permute-start.7
  200.4 2.0 collective-permute-start.6
  200.5 2.3 collective-permute-start.5
  206.6 42.5 %all-to-all-start.5 = ((bf16[8,128,512]{2,1,0:T(8,128)(2,1)}), bf16[8,128,512]{2,1,0:T(8,128)(2,1)S(1)}, u32[]{:S(2)}, u32[]{:S(2)}) async-start(bf16[8,128,512]{2,1,0:T(8,128)(2,1)} %bitcast.21), calls=%async_computation.5 | async-start | bytes 2097152 | tf_op jit(solution)/shard_map/all_to_all | solution.py:25
  211.4 37.7 %collective-permute-start.12 = (bf16[704,512]{1,0:T(8,128)(2,1)S(1)}, bf16[704,512]{1,0:T(8,128)(2,1)}, u32[]{:S(2)}, u32[]{:S(2)}) collective-permute-start(bf16[704,512]{1,0:T(8,128)(2,1)S(1)} %broadcast_select_fusion.2), channel_id=1, source_target_pairs={{0,16},{16,0},{1,17},{17,1},{2,18},{18,2},{3,19},{19,3},{4,20},{20... | collective-permute-start | bytes 2162696 | tf_op jit(solution)/shard_map/ppermute | solution.py:21
  215.1 34.0 %collective-permute-start.13 = (bf16[320,512]{1,0:T(8,128)(2,1)S(1)}, bf16[320,512]{1,0:T(8,128)(2,1)S(1)}, u32[]{:S(2)}, u32[]{:S(2)}) collective-permute-start(bf16[320,512]{1,0:T(8,128)(2,1)S(1)} %slice_bitcast_fusion.8), channel_id=1, source_target_pairs={{0,2},{2,0},{1,3},{3,1},{4,6},{6,4},{5,7},{7,5},{8,10},{10,8},{9,1... | collective-permute-start | bytes 983048 | tf_op jit(solution)/shard_map/ppermute | solution.py:21
  227.9 12.3 %collective-permute-start.14 = (f32[12,512]{1,0:T(8,128)S(1)}, f32[12,512]{1,0:T(8,128)S(1)}, u32[]{:S(2)}, u32[]{:S(2)}) collective-permute-start(f32[12,512]{1,0:T(8,128)S(1)} %pad_maximum_fusion.2), channel_id=1, source_target_pairs={{0,8},{8,0},{16,24},{24,16},{1,9},{9,1},{17,25},{25,17},{2,10},{10... | collective-permute-start | bytes 73736 | tf_op jit(solution)/shard_map/ppermute | solution.py:21
  228.3 20.8 %collective-permute-start.15 = (f32[12,512]{1,0:T(8,128)S(1)}, f32[12,512]{1,0:T(8,128)S(1)}, u32[]{:S(2)}, u32[]{:S(2)}) collective-permute-start(f32[12,512]{1,0:T(8,128)S(1)} %pad_maximum_fusion.2), channel_id=1, source_target_pairs={{0,16},{8,24},{16,0},{24,8},{1,17},{9,25},{17,1},{25,9},{2,18},{10... | collective-permute-start | bytes 73736 | tf_op jit(solution)/shard_map/ppermute | solution.py:21
  228.3 20.8 %collective-permute-start.16 = (f32[12,512]{1,0:T(8,128)S(1)}, f32[12,512]{1,0:T(8,128)S(1)}, u32[]{:S(2)}, u32[]{:S(2)}) collective-permute-start(f32[12,512]{1,0:T(8,128)S(1)} %pad_maximum_fusion.2), channel_id=1, source_target_pairs={{0,24},{8,16},{16,8},{24,0},{1,25},{9,17},{17,9},{25,1},{2,26},{10... | collective-permute-start | bytes 73736 | tf_op jit(solution)/shard_map/ppermute | solution.py:21
  249.3 9.2 %collective-permute-start.17 = (bf16[128,512]{1,0:T(8,128)(2,1)S(1)}, bf16[128,512]{1,0:T(8,128)(2,1)S(1)}, u32[]{:S(2)}, u32[]{:S(2)}) collective-permute-start(bf16[128,512]{1,0:T(8,128)(2,1)S(1)} %convert_element_type.63), channel_id=1, source_target_pairs={{0,16},{16,0},{1,17},{17,1},{2,18},{18,2},{3,19},{19,3},{4,20},{20... | collective-permute-start | bytes 393224 | tf_op jit(solution)/shard_map/ppermute | solution.py:21
  259.6 26.0 %all-to-all-start.7 = ((bf16[8,128,512]{2,1,0:T(8,128)(2,1)}), bf16[8,128,512]{2,1,0:T(8,128)(2,1)S(1)}, u32[]{:S(2)}, u32[]{:S(2)}) async-start(bf16[8,128,512]{2,1,0:T(8,128)(2,1)} %broadcast_in_dim.9), calls=%async_computation.7 | async-start | bytes 2097152 | tf_op jit(solution)/shard_map/all_to_all | solution.py:25
  263.2 2.4 collective-permute-start.18
  263.3 18.0 %collective-permute-start.22 = (bf16[320,512]{1,0:T(8,128)(2,1)S(1)}, bf16[320,512]{1,0:T(8,128)(2,1)S(1)}, u32[]{:S(2)}, u32[]{:S(2)}) collective-permute-start(bf16[320,512]{1,0:T(8,128)(2,1)S(1)} %broadcast_select_fusion.3), channel_id=1, source_target_pairs={{0,16},{16,0},{1,17},{17,1},{2,18},{18,2},{3,19},{19,3},{4,20},{20... | collective-permute-start | bytes 983048 | tf_op jit(solution)/shard_map/ppermute | solution.py:21
  265.7 6.9 %collective-permute-start.20 = (f32[12,512]{1,0:T(8,128)S(1)}, f32[12,512]{1,0:T(8,128)S(1)}, u32[]{:S(2)}, u32[]{:S(2)}) collective-permute-start(f32[12,512]{1,0:T(8,128)S(1)} %add.45), channel_id=1, source_target_pairs={{0,4},{2,6},{4,0},{6,2},{1,5},{3,7},{5,1},{7,3},{8,12},{10,14},{12... | collective-permute-start | bytes 73736 | tf_op jit(solution)/shard_map/ppermute | solution.py:21
  267.8 5.5 %collective-permute-start.21 = (f32[12,512]{1,0:T(8,128)S(1)}, f32[12,512]{1,0:T(8,128)S(1)}, u32[]{:S(2)}, u32[]{:S(2)}) collective-permute-start(f32[12,512]{1,0:T(8,128)S(1)} %add.45), channel_id=1, source_target_pairs={{0,6},{2,4},{4,2},{6,0},{1,7},{3,5},{5,3},{7,1},{8,14},{10,12},{12... | collective-permute-start | bytes 73736 | tf_op jit(solution)/shard_map/ppermute | solution.py:21
  269.2 4.1 %collective-permute-start.19 = (f32[12,512]{1,0:T(8,128)S(1)}, f32[12,512]{1,0:T(8,128)S(1)}, u32[]{:S(2)}, u32[]{:S(2)}) collective-permute-start(f32[12,512]{1,0:T(8,128)S(1)} %add.45), channel_id=1, source_target_pairs={{0,2},{2,0},{4,6},{6,4},{1,3},{3,1},{5,7},{7,5},{8,10},{10,8},{12,... | collective-permute-start | bytes 73736 | tf_op jit(solution)/shard_map/ppermute | solution.py:21
  285.6 2.7 collective-permute-start.23
